TPU v7x, 32 devices: a whole 2x2x4 slice. The times are simulated.
32 devices in a mesh: rows: 8 (over z, core), heads: 4 (over y, x).
Axes of the slice: x: 2, y: 2, z: 4, core: 2. Of those that a mesh axis runs over, the one named last changes fastest.
Arguments:
- tokens: bfloat16 [16384, 1024], P(('rows', 'heads')), may hold values from -6 to 6
- memory: bfloat16 [16384, 1024], P(('rows', 'heads')), may hold values from -6 to 6
- cotangent: bfloat16 [16384, 1024], P(('rows', 'heads')), may hold values from -6 to 6
- dec_seg: int32 [16384], P('rows'), may hold values from 0 to 3, as said below
- mem_seg: int32 [16384], P('rows'), may hold values from 0 to 3, as said below
- w_self: bfloat16 [3, 1024, 1024], P(None, None, 'heads'), may hold values from -0.1875 to 0.1875
- w_self_out: bfloat16 [1024, 1024], P('heads'), may hold values from -1.5 to 1.5
- w_cross_q: bfloat16 [1024, 1024], P(None, 'heads'), may hold values from -0.1875 to 0.1875
- w_cross_kv: bfloat16 [2, 1024, 1024], P(None, None, 'heads'), may hold values from -0.1875 to 0.1875
- w_cross_out: bfloat16 [1024, 1024], P('heads'), may hold values from -1.5 to 1.5
- fc_in: bfloat16 [1024, 4096], P(None, 'heads'), may hold values from -0.1875 to 0.1875
- fc_out: bfloat16 [4096, 1024], P('heads'), may hold values from -0.09375 to 0.09375
- ad_down: bfloat16 [1024, 512], P(None, 'heads'), may hold values from -0.1875 to 0.1875
- ad_up: bfloat16 [512, 1024], P('heads'), may hold values from -0.0625 to 0.0625
- prefix: bfloat16 [2, 30, 1024], P(None, None, 'heads'), may hold values from -6 to 6
- ln_gain: float32 [3, 1024], replicated, may hold values from 0.5 to 1.5
- ln_bias: float32 [3, 1024], replicated, may hold values from -1.2 to 1.2
Outputs:
- output: bfloat16 [16384, 1024], P(('rows', 'heads'))
- grad_input: float32 [16384, 1024], P(('rows', 'heads'))
- grad_memory: float32 [16384, 1024], P(('rows', 'heads'))
- grad_prefix: float32 [2, 30, 1024], P(None, None, 'heads')
- grad_down: float32 [1024, 512], P(None, 'heads')
- grad_up: float32 [512, 1024], P('heads')
Inputs may be any that keep to these rules, and one draw needn't show every extreme that they name: `dec_seg`: within each decoder sequence of 1024 tokens the document numbers start at 0, never fall, take every value 0 to 3, and no document is empty. `mem_seg`: within each memory of 1024 rows the document numbers start at 0, never fall, take every value 0 to 3, and no document is empty; so every decoder token has memory rows of its own document.
All inputs are finite; a program needn't handle non-finite values.
Results may differ from a plain program's by a relative error of at most 0.024.
The roundings to bfloat16 on the way count: a program that leaves them out, or rounds other values in their place, can miss the bound.
Values may be sent and summed in bfloat16 or wider, within the bound.
A program may use at most 128 MiB of HBM per device.

v0:
```python
import jax
import jax.numpy as jnp
from jax import lax
from jax.sharding import PartitionSpec as P

HD = 64
SEQ = 1024
MLEN = 1024


epsilon = 1e-05
adapter_scale = 4.0
masked_score = -1e30


def dot_right(left, right):
    return lax.dot_general(
        left, right, (((1,), (1,)), ((), ())), preferred_element_type=jnp.float32
    )


def dot_left(left, right):
    return lax.dot_general(
        left, right, (((0,), (0,)), ((), ())), preferred_element_type=jnp.float32
    )


def norm_parts(resid):
    average = jnp.mean(resid, axis=-1, keepdims=True)
    centered = resid - average
    inv_scale = lax.rsqrt(jnp.mean(centered * centered, axis=-1, keepdims=True) + epsilon)
    return (centered * inv_scale, inv_scale)


def norm_forward(resid, gain, shift):
    normed, inv_scale = norm_parts(resid)
    return normed * gain + shift


def norm_backward(resid, gain, grad_out):
    normed, inv_scale = norm_parts(resid)
    scaled = grad_out * gain
    return inv_scale * (
        scaled
        - jnp.mean(scaled, axis=-1, keepdims=True)
        - normed * jnp.mean(scaled * normed, axis=-1, keepdims=True)
    )


def gelu_slope(pre_gelu):
    return (
        0.5 * (1.0 + lax.erf(pre_gelu * 0.7071067811865476))
        + pre_gelu * jnp.exp(-0.5 * pre_gelu * pre_gelu) * 0.3989422804014327
    )


def silu_slope(pre_relu):
    sigma = jax.nn.sigmoid(pre_relu)
    return sigma * (1.0 + pre_relu * (1.0 - sigma))


def to_heads(arrays, heads_here):
    return arrays.reshape(arrays.shape[0], arrays.shape[1], heads_here, HD).transpose(0, 2, 1, 3)


def from_heads(arrays):
    return arrays.transpose(0, 2, 1, 3).reshape(
        arrays.shape[0] * arrays.shape[2], arrays.shape[1] * arrays.shape[3]
    )


def join_blocks(stacked):
    moved = jnp.moveaxis(stacked, 0, 1)
    return moved.reshape((moved.shape[0], moved.shape[1] * moved.shape[2]) + moved.shape[3:])


def block_mask(row_segs, key_segs, offset, causal):
    allowed = row_segs[:, None] == key_segs[None, :]
    if causal:
        row_places = offset + lax.iota(jnp.int32, row_segs.shape[0])
        key_places = lax.iota(jnp.int32, key_segs.shape[0])
        allowed = allowed & (key_places[None, :] <= row_places[:, None])
    return allowed


def block_scores(queries, key_rows, allowed, prefix_keys):
    qk_scale = HD ** (-0.5)
    token_scores = (
        jnp.einsum("hqe,hke->hqk", queries, key_rows, preferred_element_type=jnp.float32) * qk_scale
    )
    token_scores = jnp.where(allowed[None], token_scores, masked_score)
    if prefix_keys is None:
        return (token_scores, None)
    prefix_scores = (
        jnp.einsum("hqe,hpe->hqp", queries, prefix_keys, preferred_element_type=jnp.float32)
        * qk_scale
    )
    return (token_scores, prefix_scores)


def attend_block(queries, key_rows, value_rows, allowed, prefix_keys, prefix_values):
    token_scores, prefix_scores = block_scores(queries, key_rows, allowed, prefix_keys)
    row_max = jnp.max(token_scores, axis=-1, keepdims=True)
    if prefix_scores is not None:
        row_max = jnp.maximum(row_max, jnp.max(prefix_scores, axis=-1, keepdims=True))
    token_weights = jnp.exp(token_scores - row_max)
    row_total = jnp.sum(token_weights, axis=-1, keepdims=True)
    if prefix_scores is not None:
        prefix_weights = jnp.exp(prefix_scores - row_max)
        row_total = row_total + jnp.sum(prefix_weights, axis=-1, keepdims=True)
    context = jnp.einsum(
        "hqk,hke->hqe",
        (token_weights / row_total).astype(jnp.bfloat16),
        value_rows,
        preferred_element_type=jnp.float32,
    )
    if prefix_scores is not None:
        context = context + jnp.einsum(
            "hqp,hpe->hqe",
            (prefix_weights / row_total).astype(jnp.bfloat16),
            prefix_values,
            preferred_element_type=jnp.float32,
        )
    return (context.astype(jnp.bfloat16), row_max + jnp.log(row_total))


def attend_back(
    queries, key_rows, value_rows, allowed, prefix_keys, prefix_values, log_total, context_grad
):
    qk_scale = HD ** (-0.5)
    token_scores, prefix_scores = block_scores(queries, key_rows, allowed, prefix_keys)
    token_probs = jnp.exp(token_scores - log_total)
    token_dprob = jnp.einsum(
        "hqe,hke->hqk", context_grad, value_rows, preferred_element_type=jnp.float32
    )
    inner = jnp.sum(token_probs * token_dprob, axis=-1, keepdims=True)
    if prefix_scores is not None:
        prefix_probs = jnp.exp(prefix_scores - log_total)
        prefix_dprob = jnp.einsum(
            "hqe,hpe->hqp", context_grad, prefix_values, preferred_element_type=jnp.float32
        )
        inner = inner + jnp.sum(prefix_probs * prefix_dprob, axis=-1, keepdims=True)
    token_dscore = (token_probs * (token_dprob - inner)).astype(jnp.bfloat16)
    query_grad = jnp.einsum(
        "hqk,hke->hqe", token_dscore, key_rows, preferred_element_type=jnp.float32
    )
    key_grad = (
        jnp.einsum("hqk,hqe->hke", token_dscore, queries, preferred_element_type=jnp.float32)
        * qk_scale
    )
    value_grad = jnp.einsum(
        "hqk,hqe->hke",
        token_probs.astype(jnp.bfloat16),
        context_grad,
        preferred_element_type=jnp.float32,
    )
    if prefix_scores is None:
        return (query_grad * qk_scale, (key_grad, value_grad))
    prefix_dscore = (prefix_probs * (prefix_dprob - inner)).astype(jnp.bfloat16)
    query_grad = query_grad + jnp.einsum(
        "hqp,hpe->hqe", prefix_dscore, prefix_keys, preferred_element_type=jnp.float32
    )
    prefix_key_grad = (
        jnp.einsum("hqp,hqe->hpe", prefix_dscore, queries, preferred_element_type=jnp.float32)
        * qk_scale
    )
    prefix_value_grad = jnp.einsum(
        "hqp,hqe->hpe",
        prefix_probs.astype(jnp.bfloat16),
        context_grad,
        preferred_element_type=jnp.float32,
    )
    return (query_grad * qk_scale, (key_grad, value_grad, prefix_key_grad, prefix_value_grad))


def sequence_forward(
    queries, key_rows, value_rows, row_segs, key_segs, prefix_keys, prefix_values, causal
):
    seq_width = queries.shape[1]
    block_rows = min(512, seq_width)

    def one_block(block_index):
        offset = block_index * block_rows
        allowed = block_mask(
            lax.dynamic_slice_in_dim(row_segs, offset, block_rows, 0), key_segs, offset, causal
        )
        query_part = lax.dynamic_slice_in_dim(queries, offset, block_rows, 1)
        return attend_block(query_part, key_rows, value_rows, allowed, prefix_keys, prefix_values)

    context, log_total = lax.map(one_block, jnp.arange(seq_width // block_rows, dtype=jnp.int32))
    return (join_blocks(context), join_blocks(log_total))


def sequence_backward(
    queries,
    key_rows,
    value_rows,
    row_segs,
    key_segs,
    prefix_keys,
    prefix_values,
    causal,
    log_total,
    context_grad,
):
    seq_width = queries.shape[1]
    block_rows = min(512, seq_width)
    key_zero = jnp.zeros(key_rows.shape, jnp.float32)
    initial = (key_zero, key_zero)
    if prefix_keys is not None:
        prefix_zero = jnp.zeros(prefix_keys.shape, jnp.float32)
        initial = initial + (prefix_zero, prefix_zero)

    def one_block(running, block_index):
        offset = block_index * block_rows
        allowed = block_mask(
            lax.dynamic_slice_in_dim(row_segs, offset, block_rows, 0), key_segs, offset, causal
        )
        query_part = lax.dynamic_slice_in_dim(queries, offset, block_rows, 1)
        total_part = lax.dynamic_slice_in_dim(log_total, offset, block_rows, 1)
        grad_part = lax.dynamic_slice_in_dim(context_grad, offset, block_rows, 1)
        query_grad, block_grads = attend_back(
            query_part,
            key_rows,
            value_rows,
            allowed,
            prefix_keys,
            prefix_values,
            total_part,
            grad_part,
        )
        return (tuple((summed + added for summed, added in zip(running, block_grads))), query_grad)

    running, query_grad = lax.scan(
        one_block, initial, jnp.arange(seq_width // block_rows, dtype=jnp.int32)
    )
    outputs = (
        join_blocks(query_grad).astype(jnp.bfloat16),
        running[0].astype(jnp.bfloat16),
        running[1].astype(jnp.bfloat16),
    )
    return outputs + running[2:]


def gather_rows(row_share):
    return lax.all_gather(row_share, "heads", axis=0, tiled=True)


def gather_grads(row_share):
    return lax.all_gather(row_share, "heads", axis=0, tiled=True)


def sum_rows(partial_value):
    return lax.psum_scatter(partial_value, "heads", scatter_dimension=0, tiled=True)


def sum_grads(partial_value):
    return lax.psum_scatter(partial_value, "heads", scatter_dimension=0, tiled=True)


def body(
    tokens,
    memory,
    cotangent,
    dec_seg,
    mem_seg,
    w_self,
    w_self_out,
    w_cross_q,
    w_cross_kv,
    w_cross_out,
    fc_in,
    fc_out,
    ad_down,
    ad_up,
    prefix,
    ln_gain,
    ln_bias,
):
    local_width = w_self.shape[2]
    heads_here = local_width // HD
    seg_dec = dec_seg.reshape(-1, SEQ)
    seg_mem = mem_seg.reshape(-1, MLEN)
    seq_count = seg_dec.shape[0]
    prefix_heads = to_heads(prefix, heads_here)
    prefix_keys = prefix_heads[0]
    prefix_values = prefix_heads[1]
    gathered_x = gather_rows(tokens)
    self_proj = jnp.einsum(
        "td,cdn->ctn", gathered_x, w_self, preferred_element_type=jnp.float32
    ).astype(jnp.bfloat16)
    self_proj = self_proj.reshape(3, seq_count, SEQ, local_width)
    self_queries = to_heads(self_proj[0], heads_here)
    self_keys = to_heads(self_proj[1], heads_here)
    self_values = to_heads(self_proj[2], heads_here)

    def self_forward(packed):
        return sequence_forward(
            packed[0], packed[1], packed[2], packed[3], packed[3], prefix_keys, prefix_values, True
        )

    self_context, self_total = lax.map(
        self_forward, (self_queries, self_keys, self_values, seg_dec)
    )
    attn_partial = jnp.dot(from_heads(self_context), w_self_out, preferred_element_type=jnp.float32)
    resid_one = tokens.astype(jnp.float32) + sum_rows(attn_partial)
    hidden_one = norm_forward(resid_one, ln_gain[0], ln_bias[0])
    gathered_one = gather_rows(hidden_one.astype(jnp.bfloat16))
    gathered_mem = lax.all_gather(memory, "heads", axis=0, tiled=True)
    cross_rows = jnp.dot(gathered_one, w_cross_q, preferred_element_type=jnp.float32).astype(
        jnp.bfloat16
    )
    cross_proj = jnp.einsum(
        "td,cdn->ctn", gathered_mem, w_cross_kv, preferred_element_type=jnp.float32
    ).astype(jnp.bfloat16)
    cross_queries = to_heads(cross_rows.reshape(seq_count, SEQ, local_width), heads_here)
    cross_proj = cross_proj.reshape(2, seq_count, MLEN, local_width)
    cross_keys = to_heads(cross_proj[0], heads_here)
    cross_values = to_heads(cross_proj[1], heads_here)

    def cross_forward(packed):
        return sequence_forward(
            packed[0], packed[1], packed[2], packed[3], packed[4], None, None, False
        )

    cross_context, cross_total = lax.map(
        cross_forward, (cross_queries, cross_keys, cross_values, seg_dec, seg_mem)
    )
    cross_partial = jnp.dot(
        from_heads(cross_context), w_cross_out, preferred_element_type=jnp.float32
    )
    resid_two = hidden_one + sum_rows(cross_partial)
    hidden_two = norm_forward(resid_two, ln_gain[1], ln_bias[1])
    hidden_low = hidden_two.astype(jnp.bfloat16)
    full_in, full_out, full_down, full_up = (fc_in, fc_out, ad_down, ad_up)
    ffn_rows = gather_rows(hidden_low)
    pre_gelu = jnp.dot(ffn_rows, full_in, preferred_element_type=jnp.float32)
    activated = jax.nn.gelu(pre_gelu, approximate=False).astype(jnp.bfloat16)
    pre_relu = jnp.dot(ffn_rows, full_down, preferred_element_type=jnp.float32)
    adapted = (pre_relu * jax.nn.sigmoid(pre_relu)).astype(jnp.bfloat16)
    branch = jnp.dot(
        activated, full_out, preferred_element_type=jnp.float32
    ) + adapter_scale * jnp.dot(adapted, full_up, preferred_element_type=jnp.float32)
    resid_three = hidden_two + sum_rows(branch)
    output = norm_forward(resid_three, ln_gain[2], ln_bias[2]).astype(jnp.bfloat16)
    grad_three = norm_backward(resid_three, ln_gain[2], cotangent.astype(jnp.float32))
    grad_branch = grad_three.astype(jnp.bfloat16)
    branch_rows = gather_grads(grad_branch)
    grad_gelu = (dot_right(branch_rows, full_out) * gelu_slope(pre_gelu)).astype(jnp.bfloat16)
    grad_relu = (adapter_scale * dot_right(branch_rows, full_up) * silu_slope(pre_relu)).astype(
        jnp.bfloat16
    )
    up_grad = adapter_scale * dot_left(adapted, branch_rows)
    down_grad = dot_left(ffn_rows, grad_relu)
    hidden_partial = dot_right(grad_gelu, full_in) + dot_right(grad_relu, full_down)
    grad_two_in = grad_three + sum_grads(hidden_partial)
    down_grad, up_grad = (
        lax.psum(down_grad.astype(jnp.bfloat16), "rows").astype(jnp.float32),
        lax.psum(up_grad.astype(jnp.bfloat16), "rows").astype(jnp.float32),
    )
    grad_two = norm_backward(resid_two, ln_gain[1], grad_two_in)
    cross_out_rows = gather_grads(grad_two.astype(jnp.bfloat16))
    cross_dctx = dot_right(cross_out_rows, w_cross_out).astype(jnp.bfloat16)
    cross_dctx = to_heads(cross_dctx.reshape(seq_count, SEQ, local_width), heads_here)

    def cross_back(packed):
        return sequence_backward(
            packed[0],
            packed[1],
            packed[2],
            packed[3],
            packed[4],
            None,
            None,
            False,
            packed[5],
            packed[6],
        )

    cross_qgrad, cross_kgrad, cross_vgrad = lax.map(
        cross_back,
        (cross_queries, cross_keys, cross_values, seg_dec, seg_mem, cross_total, cross_dctx),
    )
    memory_kv = jnp.stack([from_heads(cross_kgrad), from_heads(cross_vgrad)])
    one_partial = dot_right(from_heads(cross_qgrad), w_cross_q)
    grad_one_in = grad_two + sum_grads(one_partial)
    memory_partial = jnp.einsum(
        "ctn,cdn->td", memory_kv, w_cross_kv, preferred_element_type=jnp.float32
    )
    grad_memory = lax.psum_scatter(
        memory_partial.astype(jnp.bfloat16), "heads", scatter_dimension=0, tiled=True
    ).astype(jnp.float32)
    grad_one = norm_backward(resid_one, ln_gain[0], grad_one_in)
    attn_rows = gather_grads(grad_one.astype(jnp.bfloat16))
    self_dctx = dot_right(attn_rows, w_self_out).astype(jnp.bfloat16)
    self_dctx = to_heads(self_dctx.reshape(seq_count, SEQ, local_width), heads_here)

    def self_back(running, packed):
        query_grad, key_grad, value_grad, pkey_grad, pvalue_grad = sequence_backward(
            packed[0],
            packed[1],
            packed[2],
            packed[3],
            packed[3],
            prefix_keys,
            prefix_values,
            True,
            packed[4],
            packed[5],
        )
        return (
            (running[0] + pkey_grad, running[1] + pvalue_grad),
            (query_grad, key_grad, value_grad),
        )

    zero_grad = jnp.zeros(prefix_keys.shape, jnp.float32)
    prefix_sums, self_grads = lax.scan(
        self_back,
        (zero_grad, zero_grad),
        (self_queries, self_keys, self_values, seg_dec, self_total, self_dctx),
    )
    self_stack = jnp.stack(
        [from_heads(self_grads[0]), from_heads(self_grads[1]), from_heads(self_grads[2])]
    )
    input_partial = jnp.einsum(
        "ctn,cdn->td", self_stack, w_self, preferred_element_type=jnp.float32
    )
    grad_input = grad_one + sum_grads(input_partial)
    prefix_grad = (
        jnp.stack([prefix_sums[0], prefix_sums[1]])
        .transpose(0, 2, 1, 3)
        .reshape(2, prefix.shape[1], local_width)
    )
    prefix_grad = lax.psum(prefix_grad, "rows")
    return (output, grad_input, grad_memory, prefix_grad, down_grad, up_grad)


def solution(mesh):
    in_specs = (
        P(("rows", "heads"), None),
        P(("rows", "heads"), None),
        P(("rows", "heads"), None),
        P("rows"),
        P("rows"),
        P(None, None, "heads"),
        P("heads", None),
        P(None, "heads"),
        P(None, None, "heads"),
        P("heads", None),
        P(None, "heads"),
        P("heads", None),
        P(None, "heads"),
        P("heads", None),
        P(None, None, "heads"),
        P(),
        P(),
    )
    out_specs = (
        P(("rows", "heads"), None),
        P(("rows", "heads"), None),
        P(("rows", "heads"), None),
        P(None, None, "heads"),
        P(None, "heads"),
        P("heads", None),
    )
    return jax.shard_map(body, mesh=mesh, in_specs=in_specs, out_specs=out_specs, check_vma=False)
```

profile of v0, /device:TPU:1, one launch (start us, length us, event | category | flops | bytes accessed | tf_op | source)
XLA Modules:
  0.0 1450.2 jit_solution(60743607893666727)
XLA Ops:
  10.2 54.5 %all-gather.8.cloned.1.call-done = bf16[2048,1024]{1,0:T(8,128)(2,1)} async-done(((bf16[512,1024]{1,0:T(8,128)(2,1)}), bf16[2048,1024]{1,0:T(8,128)(2,1)}) %all-gather.8.cloned.1.call-update) | async-done | bytes 4194320 | tf_op jit(solution)/shard_map/all_gather | solution.py:246
  85.6 56.0 %while.117 = (s32[]{:T(128)}, bf16[2,4,1024,64]{3,2,1,0:T(8,128)(2,1)}, f32[2,4,1024,1]{2,3,1,0:T(1,128)}, s32[2,1024]{1,0:T(2,128)S(1)}, bf16[2,4,1024,64]{2,3,...) while((s32[]{:T(128)}, ...), condition=%wide.region_7.8_spmd, body=%wide.region_0.7_spmd.sunk | while | flops 580028928 | bytes 43276864 | solution.py:302
  88.8 21.6 %while.124 = (s32[]{:T(128)}, bf16[2,4,512,64]{2,3,1,0:T(8,128)(2,1)}, f32[2,4,512,1]{2,1,3,0:T(4,128)S(1)}, s32[2]{0:T(128)S(1)}, s32[1024]{0:T(1024)S(1)}, /*i...) while((s32[]{:T(128)}, ...), condition=%wide.region_6.6_spmd, body=%wide.region_1.5_spmd.sunk | while | flops 580028928 | bytes 37401896 | solution.py:190
  116.8 21.6 %while.124 = (s32[]{:T(128)}, bf16[2,4,512,64]{2,3,1,0:T(8,128)(2,1)}, f32[2,4,512,1]{2,1,3,0:T(4,128)S(1)}, s32[2]{0:T(128)S(1)}, s32[1024]{0:T(1024)S(1)}, /*i...) while((s32[]{:T(128)}, ...), condition=%wide.region_6.6_spmd, body=%wide.region_1.5_spmd.sunk | while | flops 580028928 | bytes 37401896 | solution.py:190
  152.5 84.5 %reduce-scatter.8.cloned.1.call-done = f32[512,1024]{1,0:T(8,128)} async-done(((f32[2048,1024]{1,0:T(8,128)}), f32[512,1024]{1,0:T(8,128)}) %reduce-scatter.8.cloned.1.call-update) | async-done | bytes 2097168 | tf_op jit(solution)/shard_map/reduce_scatter | solution.py:254
  241.7 50.1 %all-gather.12.cloned.1.call-done = bf16[2048,1024]{1,0:T(8,128)(2,1)} async-done(((bf16[512,1024]{1,0:T(8,128)(2,1)}), bf16[2048,1024]{1,0:T(8,128)(2,1)}) %all-gather.12.cloned.1.call-update) | async-done | bytes 4194320 | tf_op jit(solution)/shard_map/all_gather | solution.py:309
  306.0 41.0 %all-gather.10.cloned.1.call-done = bf16[2048,1024]{1,0:T(8,128)(2,1)} async-done(((bf16[512,1024]{1,0:T(8,128)(2,1)}), bf16[2048,1024]{1,0:T(8,128)(2,1)}) %all-gather.10.cloned.1.call-update) | async-done | bytes 4194320 | tf_op jit(solution)/shard_map/all_gather | solution.py:246
  358.7 49.3 %while.119 = (s32[]{:T(128)}, bf16[2,4,1024,64]{3,2,1,0:T(8,128)(2,1)}, f32[2,4,1024,1]{2,3,1,0:T(1,128)S(1)}, s32[2,1024]{1,0:T(2,128)S(1)}, s32[2,1024]{1,0:T(...) while((s32[]{:T(128)}, ...), condition=%wide.region_16.17_spmd, body=%wide.region_11.16_spmd.sunk | while | flops 562690048 | bytes 36892140 | solution.py:326
  417.0 86.4 %reduce-scatter.10.cloned.1.call-done = f32[512,1024]{1,0:T(8,128)} async-done(((f32[2048,1024]{1,0:T(8,128)}), f32[512,1024]{1,0:T(8,128)}) %reduce-scatter.10.cloned.1.call-update) | async-done | bytes 2097168 | tf_op jit(solution)/shard_map/reduce_scatter | solution.py:254
  509.2 52.9 %all-gather.14.cloned.1.call-done = bf16[2048,1024]{1,0:T(8,128)(2,1)} async-done(((bf16[512,1024]{1,0:T(8,128)(2,1)}), bf16[2048,1024]{1,0:T(8,128)(2,1)}) %all-gather.14.cloned.1.call-update) | async-done | bytes 4194320 | tf_op jit(solution)/shard_map/all_gather | solution.py:246
  601.0 86.1 %reduce-scatter.12.cloned.1.call-done = f32[512,1024]{1,0:T(8,128)} async-done(((f32[2048,1024]{1,0:T(8,128)}), f32[512,1024]{1,0:T(8,128)}) %reduce-scatter.12.cloned.1.call-update) | async-done | bytes 2097168 | tf_op jit(solution)/shard_map/reduce_scatter | solution.py:254
  692.9 52.8 %all-gather.16.cloned.1.call-done = bf16[2048,1024]{1,0:T(8,128)(2,1)} async-done(((bf16[512,1024]{1,0:T(8,128)(2,1)}), bf16[2048,1024]{1,0:T(8,128)(2,1)}) %all-gather.16.cloned.1.call-update) | async-done | bytes 4194320 | tf_op jit(solution)/shard_map/all_gather | solution.py:250
  773.2 86.5 %reduce-scatter.14.cloned.1.call-done = f32[512,1024]{1,0:T(8,128)} async-done(((f32[2048,1024]{1,0:T(8,128)}), f32[512,1024]{1,0:T(8,128)}) %reduce-scatter.14.cloned.1.call-update) | async-done | bytes 2097168 | tf_op jit(solution)/shard_map/reduce_scatter | solution.py:258
  866.0 52.8 %all-gather.18.cloned.1.call-done = bf16[2048,1024]{1,0:T(8,128)(2,1)} async-done(((bf16[512,1024]{1,0:T(8,128)(2,1)}), bf16[2048,1024]{1,0:T(8,128)(2,1)}) %all-gather.18.cloned.1.call-update) | async-done | bytes 4194320 | tf_op jit(solution)/shard_map/all_gather | solution.py:250
  928.9 109.8 %while.121 = (s32[]{:T(128)}, bf16[2,4,1024,64]{3,2,1,0:T(8,128)(2,1)}, bf16[2,4,1024,64]{2,3,1,0:T(8,128)(2,1)}, bf16[2,4,1024,64]{2,3,1,0:T(8,128)(2,1)}, s32[...) while((s32[]{:T(128)}, ...), condition=%wide.region_32.33_spmd, body=%wide.region_28.32_spmd.sunk | while | flops 1376122880 | bytes 153768112 | solution.py:380
  934.9 44.0 %while.126 = (s32[]{:T(128)}, f32[4,1024,64]{1,2,0:T(8,128)S(1)}, f32[4,1024,64]{1,2,0:T(8,128)}, bf16[2,4,512,64]{2,3,1,0:T(8,128)(2,1)}, s32[2]{0:T(128)S(1)},...) while((s32[]{:T(128)}, f32[4,1024,64]{1,2,0:T(8,128)S(1)}, ...), condition=%wide.region_31.31_spmd.clone, body=%wide.region_29.30_spmd.clone.sunk | while | flops 1375598592 | bytes 143723376 | solution.py:234
  989.8 44.0 %while.126 = (s32[]{:T(128)}, f32[4,1024,64]{1,2,0:T(8,128)S(1)}, f32[4,1024,64]{1,2,0:T(8,128)}, bf16[2,4,512,64]{2,3,1,0:T(8,128)(2,1)}, s32[2]{0:T(128)S(1)},...) while((s32[]{:T(128)}, f32[4,1024,64]{1,2,0:T(8,128)S(1)}, ...), condition=%wide.region_31.31_spmd.clone, body=%wide.region_29.30_spmd.clone.sunk | while | flops 1375598592 | bytes 143723376 | solution.py:234
  1046.9 86.5 %reduce-scatter.16.cloned.1.call-done = f32[512,1024]{1,0:T(8,128)} async-done(((f32[2048,1024]{1,0:T(8,128)}), f32[512,1024]{1,0:T(8,128)}) %reduce-scatter.16.cloned.1.call-update) | async-done | bytes 2097168 | tf_op jit(solution)/shard_map/reduce_scatter | solution.py:258
  1158.5 32.9 %all-gather.20.cloned.1.call-done = bf16[2048,1024]{1,0:T(8,128)(2,1)} async-done(((bf16[512,1024]{1,0:T(8,128)(2,1)}), bf16[2048,1024]{1,0:T(8,128)(2,1)}) %all-gather.20.cloned.1.call-update) | async-done | bytes 4194320 | tf_op jit(solution)/shard_map/all_gather | solution.py:250
  1202.0 127.9 %while.123 = (s32[]{:T(128)}, f32[4,30,64]{2,1,0:T(8,128)}, f32[4,30,64]{2,1,0:T(8,128)}, bf16[2,4,1024,64]{3,2,1,0:T(8,128)(2,1)}, bf16[2,4,1024,64]{2,3,1,0:T(...) while((s32[]{:T(128)}, f32[4,30,64]{2,1,0:T(8,128)}, ...), condition=%wide.region_41.42_spmd.clone, body=%wide.region_36.41_spmd.clone.sunk | while | flops 1417185280 | bytes 157952208 | solution.py:417
  1209.2 51.1 %while.127 = (s32[]{:T(128)}, f32[4,1024,64]{1,2,0:T(8,128)S(1)}, f32[4,1024,64]{1,2,0:T(8,128)}, f32[4,30,64]{2,1,0:T(8,128)}, f32[4,30,64]{2,1,0:T(8,128)}, /*...) while((s32[]{:T(128)}, f32[4,1024,64]{1,2,0:T(8,128)S(1)}, ...), condition=%wide.region_40.40_spmd.clone, body=%wide.region_37.39_spmd.clone.sunk | while | flops 1416630272 | bytes 138081360 | solution.py:234
  1273.1 51.0 %while.127 = (s32[]{:T(128)}, f32[4,1024,64]{1,2,0:T(8,128)S(1)}, f32[4,1024,64]{1,2,0:T(8,128)}, f32[4,30,64]{2,1,0:T(8,128)}, f32[4,30,64]{2,1,0:T(8,128)}, /*...) while((s32[]{:T(128)}, f32[4,1024,64]{1,2,0:T(8,128)S(1)}, ...), condition=%wide.region_40.40_spmd.clone, body=%wide.region_37.39_spmd.clone.sunk | while | flops 1416630272 | bytes 138081360 | solution.py:234
  1359.6 26.4 %psum.21 = f32[2,30,256]{2,0,1:T(2,128)} all-reduce(f32[2,30,256]{2,0,1:T(2,128)S(1)} %reshape.386), channel_id=1, replica_groups=mesh['rows'=8,'heads'=4] {'rows'}, use_global_device_ids=true, to_apply=%region_44.45 | all-reduce | flops 15360 | bytes 122880 | tf_op jit(solution)/shard_map/psum | solution.py:434
  1386.0 53.4 %reduce-scatter.18.cloned.1.call-done = f32[512,1024]{1,0:T(8,128)} async-done(((f32[2048,1024]{1,0:T(8,128)}), f32[512,1024]{1,0:T(8,128)}) %reduce-scatter.18.cloned.1.call-update) | async-done | bytes 2097168 | tf_op jit(solution)/shard_map/reduce_scatter | solution.py:258
  (715 shorter events, 613.9 us)
Async XLA Ops:
  7.2 565.2 %copy-start = (bf16[1024,1024]{1,0:T(8,128)(2,1)S(1)}, bf16[1024,1024]{1,0:T(8,128)(2,1)}, u32[]{:S(2)}) copy-start(bf16[1024,1024]{1,0:T(8,128)(2,1)} %param.44) | copy-start | bytes 6291460
  7.2 57.5 %all-gather.8.cloned.1.call-start = ((), (), s32[]{:S(2)}) async-start(), calls=%async_computation.7 | async-start | bytes 5242880 | tf_op jit(solution)/shard_map/all_gather | solution.py:246
  7.9 229.1 %reduce-scatter.8.cloned.1.call-start = ((), (), s32[]{:S(2)}) async-start(), calls=%async_computation.8 | async-start | bytes 10485760 | tf_op jit(solution)/shard_map/reduce_scatter | solution.py:254
  150.5 141.3 %all-gather.12.cloned.1.call-start = ((), (), s32[]{:S(2)}) async-start(), calls=%async_computation.10 | async-start | bytes 5242880 | tf_op jit(solution)/shard_map/all_gather | solution.py:309
  151.2 195.7 %all-gather.10.cloned.1.call-start = ((), (), s32[]{:S(2)}) async-start(), calls=%async_computation.9 | async-start | bytes 5242880 | tf_op jit(solution)/shard_map/all_gather | solution.py:246
  151.9 89.7 %copy-start.59 = (f32[1,1024]{1,0:T(1,128)}, f32[1,1024]{1,0:T(1,128)S(1)}, u32[]{:S(2)}) copy-start(f32[1,1024]{1,0:T(1,128)S(1)} %get-tuple-element.941) | copy-start | bytes 12292
  152.5 89.1 %copy-start.68 = (f32[1,1024]{1,0:T(1,128)}, f32[1,1024]{1,0:T(1,128)S(1)}, u32[]{:S(2)}) copy-start(f32[1,1024]{1,0:T(1,128)S(1)} %get-tuple-element.944) | copy-start | bytes 12292
  241.7 261.8 %reduce-scatter.10.cloned.1.call-start = ((), (), s32[]{:S(2)}) async-start(), calls=%async_computation.11 | async-start | bytes 10485760 | tf_op jit(solution)/shard_map/reduce_scatter | solution.py:254
  417.0 90.7 %copy-start.63 = (f32[1,1024]{1,0:T(1,128)S(1)}, f32[1,1024]{1,0:T(1,128)}, u32[]{:S(2)}) copy-start(f32[1,1024]{1,0:T(1,128)} %get-tuple-element.942) | copy-start | bytes 12292
  417.0 90.7 %copy-start.67 = (f32[1,1024]{1,0:T(1,128)S(1)}, f32[1,1024]{1,0:T(1,128)}, u32[]{:S(2)}) copy-start(f32[1,1024]{1,0:T(1,128)} %get-tuple-element.945) | copy-start | bytes 12292
  417.0 145.0 %all-gather.14.cloned.1.call-start = ((), (), s32[]{:S(2)}) async-start(), calls=%async_computation.12 | async-start | bytes 5242880 | tf_op jit(solution)/shard_map/all_gather | solution.py:246
  509.1 178.0 %reduce-scatter.12.cloned.1.call-start = ((), (), s32[]{:S(2)}) async-start(), calls=%async_computation.13 | async-start | bytes 10485760 | tf_op jit(solution)/shard_map/reduce_scatter | solution.py:254
  600.5 89.8 %copy-start.29 = (bf16[512,1024]{1,0:T(8,128)(2,1)S(1)}, bf16[512,1024]{1,0:T(8,128)(2,1)}, u32[]{:S(2)}) copy-start(bf16[512,1024]{1,0:T(8,128)(2,1)} %param.35) | copy-start | bytes 3145732
  600.5 89.8 %copy-start.62 = (f32[1,1024]{1,0:T(1,128)S(1)}, f32[1,1024]{1,0:T(1,128)}, u32[]{:S(2)}) copy-start(f32[1,1024]{1,0:T(1,128)} %get-tuple-element.940) | copy-start | bytes 12292
  600.5 145.2 %all-gather.16.cloned.1.call-start = ((), (), s32[]{:S(2)}) async-start(), calls=%async_computation.14 | async-start | bytes 5242880 | tf_op jit(solution)/shard_map/all_gather | solution.py:250
  692.9 166.8 %reduce-scatter.14.cloned.1.call-start = ((), (), s32[]{:S(2)}) async-start(), calls=%async_computation.15 | async-start | bytes 10485760 | tf_op jit(solution)/shard_map/reduce_scatter | solution.py:258
  773.1 145.6 %all-gather.18.cloned.1.call-start = ((), (), s32[]{:S(2)}) async-start(), calls=%async_computation.16 | async-start | bytes 5242880 | tf_op jit(solution)/shard_map/all_gather | solution.py:250
  865.9 267.5 %reduce-scatter.16.cloned.1.call-start = ((), (), s32[]{:S(2)}) async-start(), calls=%async_computation.17 | async-start | bytes 10485760 | tf_op jit(solution)/shard_map/reduce_scatter | solution.py:258
  1046.9 86.6 %copy-start.66 = (f32[512]{0:T(512)S(1)}, f32[512]{0:T(512)}, u32[]{:S(2)}) copy-start(f32[512]{0:T(512)} %copy-done.64) | copy-start | bytes 6148
  1046.9 144.6 %all-gather.20.cloned.1.call-start = ((), (), s32[]{:S(2)}) async-start(), calls=%async_computation.18 | async-start | bytes 5242880 | tf_op jit(solution)/shard_map/all_gather | solution.py:250
  1138.6 214.2 %all-reduce.3.cloned.1.call-start = ((), (), s32[]{:S(2)}) async-start(), calls=%async_computation.21 | async-start | bytes 1048576 | tf_op jit(solution)/shard_map/psum | solution.py:358
  1144.6 211.9 %reduce-scatter.20.cloned.1.call-start = ((), (), s32[]{:S(2)}) async-start(), calls=%async_computation.20 | async-start | bytes 5242880 | tf_op jit(solution)/shard_map/reduce_scatter | solution.py:390
  1158.5 280.9 %reduce-scatter.18.cloned.1.call-start = ((), (), s32[]{:S(2)}) async-start(), calls=%async_computation.19 | async-start | bytes 10485760 | tf_op jit(solution)/shard_map/reduce_scatter | solution.py:258
  1356.5 87.0 %copy-start.1 = (bf16[1024,1024]{1,0:T(8,128)(2,1)S(1)}, bf16[1024,1024]{1,0:T(8,128)(2,1)}, u32[]{:S(2)}) copy-start(bf16[1024,1024]{1,0:T(8,128)(2,1)} %param.44) | copy-start | bytes 6291460
  (130 other events, 1499.2 us)
Sparse Core Ops, SparseCore 0:
  9.9 54.7 all-gather.7
  150.6 86.3 reduce-scatter.7
  239.0 52.7 all-gather.11
  294.2 52.6 all-gather.9
  417.1 86.3 reduce-scatter.9
  509.2 52.7 all-gather.13
  600.6 86.3 reduce-scatter.11
  693.0 52.7 all-gather.15
  773.3 86.3 reduce-scatter.13
  866.0 52.6 all-gather.17
  1047.0 86.3 reduce-scatter.15
  1138.7 52.7 all-gather.19
  1194.0 54.5 all-reduce.2
  1251.4 53.5 reduce-scatter.19
  1352.9 86.4 reduce-scatter.17
where the time goes:
time: 1460 us; the launch traced here: 1450 us
  waiting for transfers between devices  822 us (56%)
  matrix products  299 us (20%)
  local copies, waits for them, and re-layouts  178 us (12%)
  other arithmetic  97.1 us (7%)
  blocking collectives  26.4 us (2%)
  between operations  14.9 us (1%)
    reduce_scatter x3, waiting for transfers between devices, sum_rows(): lax.psum_scatter(partial_value, 'heads', scatter_dimension=0, tiled=True)  257 us
    reduce_scatter x3, waiting for transfers between devices, sum_grads(): lax.psum_scatter(partial_value, 'heads', scatter_dimension=0, tiled=True)  226 us
    all_gather x3, waiting for transfers between devices, gather_rows(): return lax.all_gather(row_share, 'heads', axis=0, tiled=True)  148 us
    all_gather x3, waiting for transfers between devices, gather_grads(): return lax.all_gather(row_share, 'heads', axis=0, tiled=True)  139 us
    all_gather x1, waiting for transfers between devices, body(): gathered_mem = lax.all_gather(memory, 'heads', axis=0, tiled=True)  50.1 us
    dot_general x6, matrix products, dot_right(): lax.dot_general(left, right, (((1,), (1,)), ((), ())), preferred_element_...  38.9 us
    dot_general x8, matrix products, attend_back(): jnp.einsum('hqk,hqe->hke', token_probs.astype(jnp.bfloat16), context_grad...  35.8 us
    squeeze x24, local copies, waits for them, and re-layouts, body(): lax.map(self_forward, (self_queries, self_keys, self_values, seg_dec))  33.2 us
  transfers between devices with their start and end apart: 15, of which 13 were waited for; matrix products, arithmetic and copies ran while one was open for 13% of the time, Pallas kernels for 0%

commit v1 on v0

--- a/solution.py
+++ b/solution.py
@@ -1,6 +1,11 @@
+import functools
+import math
+
 import jax
 import jax.numpy as jnp
 from jax import lax
+from jax.experimental import pallas as pl
+from jax.experimental.pallas import tpu as pltpu
 from jax.sharding import PartitionSpec as P
 
 HD = 64
@@ -435,6 +440,489 @@
     return (output, grad_input, grad_memory, prefix_grad, down_grad, up_grad)
 
 
+QB = 256
+KB = 256
+LOG2E = math.log2(math.e)
+NEG = -1e30
+WIDTHS = (256, 384, 512, 768, 1024)
+
+
+def nt(a, b):
+    return lax.dot_general(a, b, (((1,), (1,)), ((), ())), preferred_element_type=jnp.float32)
+
+
+def nn(a, b):
+    return lax.dot_general(a, b, (((1,), (0,)), ((), ())), preferred_element_type=jnp.float32)
+
+
+def half_lanes(v, h):
+    lane = lax.broadcasted_iota(jnp.int32, v.shape, 1)
+    keep = (lane < 64) if h == 0 else (lane >= 64)
+    return jnp.where(keep, v, jnp.zeros_like(v))
+
+
+def prefix_rows(scores):
+    row = lax.broadcasted_iota(jnp.int32, scores.shape, 0)
+    return jnp.where(lax.rem(row, 64) < 30, scores, NEG)
+
+
+def fwd_kernel(has_prefix, win, q_ref, k_ref, v_ref, lo_ref, hi_ref, *rest):
+    if has_prefix:
+        kp_ref, vp_ref, ctx_ref, lse_ref, vt_ref = rest
+    else:
+        ctx_ref, lse_ref, vt_ref = rest
+    scale = 0.125 * LOG2E
+    vt_ref[...] = v_ref[...].astype(jnp.float32).T.astype(jnp.bfloat16)
+    if has_prefix:
+        vpt = vp_ref[0].astype(jnp.float32).T.astype(jnp.bfloat16)
+
+    def one(qi, _):
+        q0 = pl.multiple_of(qi * QB, QB)
+        q = q_ref[pl.ds(q0, QB), :]
+        lo = lo_ref[:, pl.ds(q0, QB)]
+        hi = hi_ref[:, pl.ds(q0, QB)]
+        st = pl.multiple_of(win[qi, 0], 128)
+
+        def run(width):
+            k = k_ref[pl.ds(st, width), :]
+            pos = st + lax.broadcasted_iota(jnp.int32, (width, QB), 0)
+            mask = (pos >= lo) & (pos <= hi)
+            if has_prefix:
+                sp = prefix_rows(nt(kp_ref[0], q) * scale)
+            outs, tops, sums = [], [], []
+            for h in range(2):
+                s = nt(k, half_lanes(q, h)) * scale
+                s = jnp.where(mask, s, NEG)
+                m = jnp.max(s, axis=0, keepdims=True)
+                if has_prefix:
+                    m = jnp.maximum(m, jnp.max(sp[h * 64 : h * 64 + 32], axis=0, keepdims=True))
+                e = jnp.exp2(s - m)
+                l = jnp.sum(e, axis=0, keepdims=True)
+                vt = vt_ref[h * 64 : h * 64 + 64, pl.ds(st, width)]
+                outs.append(nn(vt, e.astype(jnp.bfloat16)))
+                tops.append(m)
+                sums.append(l)
+            if has_prefix:
+                mm = jnp.concatenate([jnp.broadcast_to(t, (64, QB)) for t in tops], axis=0)
+                ep = jnp.exp2(sp - mm)
+                sums = [
+                    sums[h] + jnp.sum(ep[h * 64 : h * 64 + 32], axis=0, keepdims=True)
+                    for h in range(2)
+                ]
+                extra = nn(vpt, ep.astype(jnp.bfloat16))
+                outs = [outs[h] + extra[h * 64 : h * 64 + 64] for h in range(2)]
+            both = jnp.concatenate([outs[h] * (1.0 / sums[h]) for h in range(2)], axis=0)
+            ctx_ref[pl.ds(q0, QB), :] = both.T.astype(jnp.bfloat16)
+            for h in range(2):
+                lse_ref[0, h : h + 1, pl.ds(q0, QB)] = tops[h] + jnp.log2(sums[h])
+
+        for index, width in enumerate(WIDTHS):
+            pl.when(win[qi, 1] == index)(functools.partial(run, width))
+        return 0
+
+    lax.fori_loop(0, SEQ // QB, one, 0)
+
+
+def bwd_kernel(has_prefix, win, q_ref, k_ref, v_ref, lo_ref, hi_ref, ctx_ref, dctx_ref, lse_ref, *rest):
+    if has_prefix:
+        kp_ref, vp_ref, dq_ref, dk_ref, dv_ref, dpre_ref, kt_ref, dk_acc, dv_acc, dq_acc, dpre_acc = rest
+    else:
+        dq_ref, dk_ref, dv_ref, kt_ref, dk_acc, dv_acc, dq_acc = rest
+    scale = 0.125 * LOG2E
+    kt_ref[...] = k_ref[...].astype(jnp.float32).T.astype(jnp.bfloat16)
+    dk_acc[...] = jnp.zeros_like(dk_acc)
+    dv_acc[...] = jnp.zeros_like(dv_acc)
+    if has_prefix:
+        dpre_acc[...] = jnp.zeros_like(dpre_acc)
+        kpt = kp_ref[0].astype(jnp.float32).T.astype(jnp.bfloat16)
+
+    def one(qi, _):
+        q0 = pl.multiple_of(qi * QB, QB)
+        q = q_ref[pl.ds(q0, QB), :]
+        dctx = dctx_ref[pl.ds(q0, QB), :]
+        lo = lo_ref[:, pl.ds(q0, QB)]
+        hi = hi_ref[:, pl.ds(q0, QB)]
+        prod = (dctx.astype(jnp.float32) * ctx_ref[pl.ds(q0, QB), :].astype(jnp.float32)).T
+        inner = [jnp.sum(prod[h * 64 : h * 64 + 64], axis=0, keepdims=True) for h in range(2)]
+        lse = [lse_ref[0, h : h + 1, pl.ds(q0, QB)] for h in range(2)]
+        qh = [half_lanes(q, h) for h in range(2)]
+        dh = [half_lanes(dctx, h) for h in range(2)]
+        if has_prefix:
+            sp = prefix_rows(nt(kp_ref[0], q) * scale)
+            rows = lambda pair: jnp.concatenate([jnp.broadcast_to(t, (64, QB)) for t in pair], axis=0)
+            pp = jnp.exp2(sp - rows(lse))
+            dpp = nt(vp_ref[0], dctx)
+            dsp = (pp * (dpp - rows(inner))).astype(jnp.bfloat16)
+            dpre_acc[0] += nn(dsp, q)
+            dpre_acc[1] += nn(pp.astype(jnp.bfloat16), dctx)
+            dq_acc[...] = nn(kpt, dsp)
+        else:
+            dq_acc[...] = jnp.zeros_like(dq_acc)
+
+        def chunk(ki, _):
+            k0 = pl.multiple_of(ki * KB, KB)
+            k = k_ref[pl.ds(k0, KB), :]
+            v = v_ref[pl.ds(k0, KB), :]
+            pos = k0 + lax.broadcasted_iota(jnp.int32, (KB, QB), 0)
+            mask = (pos >= lo) & (pos <= hi)
+            ps, dss = [], []
+            for h in range(2):
+                s = nt(k, qh[h]) * scale
+                p = jnp.exp2(jnp.where(mask, s, NEG) - lse[h])
+                dp = nt(v, dh[h])
+                ds = (p * (dp - inner[h])).astype(jnp.bfloat16)
+                ps.append(p.astype(jnp.bfloat16))
+                dss.append(ds)
+                dq_acc[h * 64 : h * 64 + 64, :] += nn(kt_ref[h * 64 : h * 64 + 64, pl.ds(k0, KB)], ds)
+            dv_acc[pl.ds(k0, KB), :] += nn(ps[0], dh[0]) + nn(ps[1], dh[1])
+            dk_acc[pl.ds(k0, KB), :] += nn(dss[0], qh[0]) + nn(dss[1], qh[1])
+            return 0
+
+        lax.fori_loop(win[qi, 2], win[qi, 3], chunk, 0)
+        dq_ref[pl.ds(q0, QB), :] = (dq_acc[...].T * 0.125).astype(jnp.bfloat16)
+        return 0
+
+    lax.fori_loop(0, SEQ // QB, one, 0)
+    dk_ref[...] = (dk_acc[...] * 0.125).astype(jnp.bfloat16)
+    dv_ref[...] = dv_acc[...].astype(jnp.bfloat16)
+    if has_prefix:
+        lane = lax.broadcasted_iota(jnp.int32, (32, 128), 1)
+        for i, factor in ((0, 0.125), (1, 1.0)):
+            dpre_ref[0, i] = jnp.where(lane < 64, dpre_acc[i, 0:32], dpre_acc[i, 64:96]) * factor
+
+
+def row_spec():
+    return pl.BlockSpec((1, SEQ), lambda j, *_: (0, 0))
+
+
+def col_spec(offset):
+    return pl.BlockSpec((SEQ, 128), lambda j, *_: (0, offset + j))
+
+
+def pre_spec():
+    return pl.BlockSpec((1, 128, 128), lambda j, *_: (j, 0, 0))
+
+
+def lse_spec():
+    return pl.BlockSpec((1, 8, SEQ), lambda j, *_: (j, 0, 0))
+
+
+def attend_fwd(q, k, v, offs, lo, hi, win, prefix_kv=None):
+    pairs = 4
+    in_specs = [col_spec(offs[0]), col_spec(offs[1]), col_spec(offs[2]), row_spec(), row_spec()]
+    args = [q, k, v, lo, hi]
+    if prefix_kv is not None:
+        in_specs += [pre_spec(), pre_spec()]
+        args += list(prefix_kv)
+    return pl.pallas_call(
+        functools.partial(fwd_kernel, prefix_kv is not None),
+        grid_spec=pltpu.PrefetchScalarGridSpec(
+            num_scalar_prefetch=1,
+            grid=(pairs,),
+            in_specs=in_specs,
+            out_specs=[col_spec(0), lse_spec()],
+            scratch_shapes=[pltpu.VMEM((128, SEQ), jnp.bfloat16)],
+        ),
+        out_shape=[
+            jax.ShapeDtypeStruct((SEQ, 128 * pairs), jnp.bfloat16),
+            jax.ShapeDtypeStruct((pairs, 8, SEQ), jnp.float32),
+        ],
+        compiler_params=pltpu.CompilerParams(vmem_limit_bytes=40 * 2**20),
+        cost_estimate=pl.CostEstimate(flops=2 * 2 * 8 * SEQ * SEQ * 64, bytes_accessed=6 * 2**20, transcendentals=8 * SEQ * SEQ),
+        name="attend_forward",
+    )(win, *args)
+
+
+def attend_bwd(q, k, v, offs, lo, hi, win, ctx, dctx, lse, prefix_kv=None):
+    pairs = 4
+    in_specs = [col_spec(offs[0]), col_spec(offs[1]), col_spec(offs[2]), row_spec(), row_spec(), col_spec(0), col_spec(0), lse_spec()]
+    args = [q, k, v, lo, hi, ctx, dctx, lse]
+    wide = jax.ShapeDtypeStruct((SEQ, 128 * pairs), jnp.bfloat16)
+    out_specs = [col_spec(0)] * 3
+    out_shape = [wide] * 3
+    if prefix_kv is not None:
+        in_specs += [pre_spec(), pre_spec()]
+        args += list(prefix_kv)
+        out_specs = out_specs + [pl.BlockSpec((1, 2, 32, 128), lambda j, *_: (j, 0, 0, 0))]
+        out_shape = out_shape + [jax.ShapeDtypeStruct((pairs, 2, 32, 128), jnp.float32)]
+    return pl.pallas_call(
+        functools.partial(bwd_kernel, prefix_kv is not None),
+        grid_spec=pltpu.PrefetchScalarGridSpec(
+            num_scalar_prefetch=1,
+            grid=(pairs,),
+            in_specs=in_specs,
+            out_specs=out_specs,
+            scratch_shapes=[
+                pltpu.VMEM((128, SEQ), jnp.bfloat16),
+                pltpu.VMEM((SEQ, 128), jnp.float32),
+                pltpu.VMEM((SEQ, 128), jnp.float32),
+                pltpu.VMEM((128, QB), jnp.float32),
+            ]
+            + ([pltpu.VMEM((2, 128, 128), jnp.float32)] if prefix_kv is not None else []),
+        ),
+        out_shape=out_shape,
+        compiler_params=pltpu.CompilerParams(vmem_limit_bytes=40 * 2**20),
+        cost_estimate=pl.CostEstimate(flops=5 * 2 * 8 * SEQ * SEQ * 64, bytes_accessed=10 * 2**20, transcendentals=8 * SEQ * SEQ),
+        name="attend_backward",
+    )(win, *args)
+
+
+def windows(lo, hi):
+    first = lo.reshape(-1, QB)[:, 0]
+    last = hi.reshape(-1, QB)[:, -1]
+    start = first // 128 * 128
+    need = last + 1 - start
+    variant = sum((need > width).astype(jnp.int32) for width in WIDTHS[:-1])
+    width = jnp.full_like(variant, WIDTHS[0])
+    for index in range(1, len(WIDTHS)):
+        width = jnp.where(variant == index, WIDTHS[index], width)
+    start = jnp.minimum(start, SEQ - width)
+    return jnp.stack([start, variant, first // KB, last // KB + 1], axis=1).astype(jnp.int32)
+
+
+AXES = ("rows", "heads")
+
+
+def fast_fits(mesh):
+    rows, heads = mesh.shape["rows"], mesh.shape["heads"]
+    return heads == 4 and rows % 2 == 0 and (rows & (rows - 1)) == 0
+
+
+def pairs_of(rows, move):
+    def number(z, c, y, x):
+        return (z * 2 + c) * 4 + y * 2 + x
+
+    found = []
+    for z in range(rows // 2):
+        for c in range(2):
+            for y in range(2):
+                for x in range(2):
+                    found.append((number(z, c, y, x), number(*move(z, c, y, x))))
+    return found
+
+
+class Moves:
+    def __init__(self, rows):
+        def perm(move):
+            table = pairs_of(rows, move)
+            return lambda value: lax.ppermute(value, AXES, table)
+
+        self.core = perm(lambda z, c, y, x: (z, 1 - c, y, x))
+        self.x = perm(lambda z, c, y, x: (z, c, y, 1 - x))
+        self.y = perm(lambda z, c, y, x: (z, c, 1 - y, x))
+        self.swap = perm(lambda z, c, y, x: (z, x, y, c))
+        self.z = []
+        step = 1
+        while step < rows // 2:
+            self.z.append(perm(lambda z, c, y, x, step=step: (z ^ step, c, y, x)))
+            step *= 2
+
+
+def fast_body(
+    rows,
+    tokens,
+    memory,
+    cotangent,
+    dec_seg,
+    mem_seg,
+    w_self,
+    w_self_out,
+    w_cross_q,
+    w_cross_kv,
+    w_cross_out,
+    fc_in,
+    fc_out,
+    ad_down,
+    ad_up,
+    prefix,
+    ln_gain,
+    ln_bias,
+):
+    bf16 = jnp.bfloat16
+    f32 = jnp.float32
+    move = Moves(rows)
+    core = lax.axis_index("rows") % 2
+    x_place = lax.axis_index("heads") % 2
+    y_place = lax.axis_index("heads") // 2
+
+    def half(value, axis):
+        size = value.shape[axis] // 2
+        return lax.dynamic_slice_in_dim(value, core * size, size, axis)
+
+    def own_rows(value):
+        size = value.shape[0] // 2
+        return lax.dynamic_slice_in_dim(value, core * size, size, 0)
+
+    def other_rows(value):
+        size = value.shape[0] // 2
+        return lax.dynamic_slice_in_dim(value, (1 - core) * size, size, 0)
+
+    def whole(mine, others):
+        return jnp.where(
+            core == 0,
+            jnp.concatenate([mine, others], axis=0),
+            jnp.concatenate([others, mine], axis=0),
+        )
+
+    def four(value, axis, through_x):
+        from_x = move.x(value)
+        from_y = move.y(value)
+        from_d = move.x(from_y) if through_x else move.y(from_x)
+        return jnp.concatenate([value, from_x, from_y, from_d], axis=axis)
+
+    tok = move.swap(tokens)
+    tok_all = whole(tok, move.core(tok))
+    self_w = four(half(w_self, 2), 2, False)
+    prefix_all = four(half(prefix, 2), 2, False)
+    mem_rows = move.swap(memory)
+    mem_all = whole(mem_rows, move.core(mem_rows))
+    self_out_m = four(half(w_self_out, 0), 0, True)
+    self_out_o = move.core(self_out_m)
+    cross_q_m = four(half(w_cross_q, 1), 1, True)
+    cross_q_o = move.core(cross_q_m)
+    cross_kv = four(half(w_cross_kv, 2), 2, False)
+    cross_out_m = four(half(w_cross_out, 0), 0, True)
+    cross_out_o = move.core(cross_out_m)
+    cot = move.swap(cotangent).astype(f32)
+    fc_in_m = four(half(fc_in, 1), 1, False)
+    fc_in_o = move.core(fc_in_m)
+    down_m = four(half(ad_down.T, 0), 0, False)
+    down_o = move.core(down_m)
+    fc_out_m = four(half(fc_out, 0), 0, True)
+    fc_out_o = move.core(fc_out_m)
+    up_m = four(half(ad_up, 0), 0, False)
+    up_o = move.core(up_m)
+
+    def chip_seg(seg):
+        both = jnp.where(core == x_place, seg, move.core(seg))
+        return lax.dynamic_slice_in_dim(both, y_place * SEQ, SEQ, 0)
+
+    seg = chip_seg(dec_seg)
+    mseg = chip_seg(mem_seg)
+    self_lo = jnp.sum(seg[None, :] < seg[:, None], axis=1, dtype=jnp.int32)
+    self_hi = lax.iota(jnp.int32, SEQ)
+    cross_lo = jnp.sum(mseg[None, :] < seg[:, None], axis=1, dtype=jnp.int32)
+    cross_hi = jnp.sum(mseg[None, :] <= seg[:, None], axis=1, dtype=jnp.int32) - 1
+    self_win = windows(self_lo, self_hi)
+    cross_win = windows(cross_lo, cross_hi)
+    self_lo, self_hi = self_lo[None], self_hi[None]
+    cross_lo, cross_hi = cross_lo[None], cross_hi[None]
+
+    count = prefix.shape[1]
+    blocks = prefix_all.reshape(2, count, 4, 2, HD)
+    placed = jnp.zeros((2, 4, 2, HD, 2, HD), bf16)
+    for head in range(2):
+        placed = placed.at[:, :, head, :count, head, :].set(blocks[:, :, :, head].transpose(0, 2, 1, 3))
+    placed = placed.reshape(2, 4, 128, 128)
+    prefix_kv = (placed[0], placed[1])
+
+    def dot(left, right):
+        return jnp.dot(left, right, preferred_element_type=f32)
+
+    width = self_w.shape[2]
+    qkv = jnp.concatenate([dot(tok_all, self_w[i]).astype(bf16) for i in range(3)], axis=1)
+    groups = width // 128
+    self_offs = (0, groups, 2 * groups)
+    self_ctx, self_lse = attend_fwd(qkv, qkv, qkv, self_offs, self_lo, self_hi, self_win, prefix_kv)
+    got = move.core(other_rows(self_ctx))
+    resid_one = tok.astype(f32) + dot(own_rows(self_ctx), self_out_m) + dot(got, self_out_o)
+    hidden_one = norm_forward(resid_one, ln_gain[0], ln_bias[0])
+    low_one = hidden_one.astype(bf16)
+
+    kv = jnp.concatenate([dot(mem_all, cross_kv[i]).astype(bf16) for i in range(2)], axis=1)
+    q_send = dot(low_one, cross_q_o).astype(bf16)
+    cross_q = whole(dot(low_one, cross_q_m).astype(bf16), move.core(q_send))
+    cross_offs = (0, 0, groups)
+    cross_ctx, cross_lse = attend_fwd(cross_q, kv, kv, cross_offs, cross_lo, cross_hi, cross_win)
+    got = move.core(other_rows(cross_ctx))
+    resid_two = hidden_one + dot(own_rows(cross_ctx), cross_out_m) + dot(got, cross_out_o)
+    hidden_two = norm_forward(resid_two, ln_gain[1], ln_bias[1])
+    low_two = hidden_two.astype(bf16)
+
+    pre_m = dot(low_two, fc_in_m)
+    pre_o = dot(low_two, fc_in_o)
+    act_m = jax.nn.gelu(pre_m, approximate=False).astype(bf16)
+    act_o = jax.nn.gelu(pre_o, approximate=False).astype(bf16)
+    relu_m = dot_right(low_two, down_m)
+    relu_o = dot_right(low_two, down_o)
+    ada_m = (relu_m * jax.nn.sigmoid(relu_m)).astype(bf16)
+    ada_o = (relu_o * jax.nn.sigmoid(relu_o)).astype(bf16)
+    branch = dot(act_m, fc_out_m) + dot(act_o, fc_out_o)
+    branch = branch + adapter_scale * (dot(ada_m, up_m) + dot(ada_o, up_o))
+    resid_three = hidden_two + branch
+    output = move.swap(norm_forward(resid_three, ln_gain[2], ln_bias[2]).astype(bf16))
+    grad_three = norm_backward(resid_three, ln_gain[2], cot)
+    grad_branch = grad_three.astype(bf16)
+    gelu_m = (dot_right(grad_branch, fc_out_m) * gelu_slope(pre_m)).astype(bf16)
+    gelu_o = (dot_right(grad_branch, fc_out_o) * gelu_slope(pre_o)).astype(bf16)
+    grelu_m = (adapter_scale * dot_right(grad_branch, up_m) * silu_slope(relu_m)).astype(bf16)
+    grelu_o = (adapter_scale * dot_right(grad_branch, up_o) * silu_slope(relu_o)).astype(bf16)
+    grad_two_in = grad_three + dot_right(gelu_m, fc_in_m) + dot_right(gelu_o, fc_in_o)
+    grad_two_in = grad_two_in + dot(grelu_m, down_m) + dot(grelu_o, down_o)
+    grad_two = norm_backward(resid_two, ln_gain[1], grad_two_in)
+
+    def unit_grads(grelu, ada):
+        return jnp.concatenate(
+            [dot_left(grelu, low_two), adapter_scale * dot_left(ada, grad_branch)], axis=1
+        )
+
+    unit_mine = unit_grads(grelu_m, ada_m) + move.core(unit_grads(grelu_o, ada_o).astype(bf16)).astype(f32)
+    units = unit_mine.shape[0] // 4
+    pieces = [unit_mine[i * units : (i + 1) * units] for i in range(4)]
+    low_pieces = [piece.astype(bf16) for piece in pieces]
+    unit_sum = (
+        pieces[0]
+        + move.x(low_pieces[1]).astype(f32)
+        + move.y(low_pieces[2]).astype(f32)
+        + move.x(move.y(low_pieces[3])).astype(f32)
+    )
+    for step in move.z:
+        unit_sum = unit_sum + step(unit_sum.astype(bf16)).astype(f32)
+    unit_all = whole(unit_sum, move.core(unit_sum.astype(bf16)).astype(f32))
+    features = low_two.shape[1]
+    down_grad = unit_all[:, :features].T
+    up_grad = unit_all[:, features:]
+
+    low_grad_two = grad_two.astype(bf16)
+    d_send = dot_right(low_grad_two, cross_out_o).astype(bf16)
+    cross_dctx = whole(dot_right(low_grad_two, cross_out_m).astype(bf16), move.core(d_send))
+    cross_dq, cross_dk, cross_dv = attend_bwd(
+        cross_q, kv, kv, cross_offs, cross_lo, cross_hi, cross_win, cross_ctx, cross_dctx, cross_lse
+    )
+    got = move.core(other_rows(cross_dq))
+    grad_one_in = grad_two + dot_right(own_rows(cross_dq), cross_q_m) + dot_right(got, cross_q_o)
+    memory_part = dot_right(cross_dk, cross_kv[0]) + dot_right(cross_dv, cross_kv[1])
+    memory_sum = own_rows(memory_part) + move.core(other_rows(memory_part).astype(bf16)).astype(f32)
+    grad_memory = move.swap(memory_sum.astype(bf16)).astype(f32)
+    grad_one = norm_backward(resid_one, ln_gain[0], grad_one_in)
+
+    low_grad_one = grad_one.astype(bf16)
+    d_send = dot_right(low_grad_one, self_out_o).astype(bf16)
+    self_dctx = whole(dot_right(low_grad_one, self_out_m).astype(bf16), move.core(d_send))
+    self_dq, self_dk, self_dv, prefix_blocks = attend_bwd(
+        qkv, qkv, qkv, self_offs, self_lo, self_hi, self_win, self_ctx, self_dctx, self_lse, prefix_kv
+    )
+    input_part = dot_right(self_dq, self_w[0]) + dot_right(self_dk, self_w[1]) + dot_right(self_dv, self_w[2])
+    input_sum = own_rows(input_part) + move.core(other_rows(input_part).astype(bf16)).astype(f32) + grad_one
+    grad_input = move.swap(input_sum.astype(bf16)).astype(f32)
+
+    prefix_sum = (
+        prefix_blocks[0]
+        + move.x(prefix_blocks[1])
+        + move.y(prefix_blocks[2])
+        + move.x(move.y(prefix_blocks[3]))
+    )
+    for step in move.z:
+        prefix_sum = prefix_sum + step(prefix_sum)
+    prefix_other = move.core(prefix_sum)
+    prefix_grad = jnp.where(
+        core == 0,
+        jnp.concatenate([prefix_sum, prefix_other], axis=2),
+        jnp.concatenate([prefix_other, prefix_sum], axis=2),
+    )[:, :count]
+    return (output, grad_input, grad_memory, prefix_grad, down_grad, up_grad)
+
+
 def solution(mesh):
     in_specs = (
         P(("rows", "heads"), None),
@@ -463,4 +951,5 @@
         P(None, "heads"),
         P("heads", None),
     )
-    return jax.shard_map(body, mesh=mesh, in_specs=in_specs, out_specs=out_specs, check_vma=False)
+    chosen = functools.partial(fast_body, mesh.shape["rows"]) if fast_fits(mesh) else body
+    return jax.shard_map(chosen, mesh=mesh, in_specs=in_specs, out_specs=out_specs, check_vma=False)

time: 1460 us -> 490 us (0.34)
  waiting for transfers between devices: 822 us -> 81.3 us
  matrix products: 299 us -> 101 us
  local copies, waits for them, and re-layouts: 178 us -> 31.4 us
  starting transfers between devices: 1.02 us -> 137 us
  Pallas kernels: 0 us -> 97.9 us
  other arithmetic: 97.1 us -> 35 us
  blocking collectives: 26.4 us -> 0 us
    reduce_scatter x7 -> x0, waiting for transfers between devices: 483 us -> none  [the longest x3 257 us: sum_rows(): lax.psum_scatter(partial_value, 'heads', scatter_dimension=0, tiled=True)]
    all_gather x7 -> x0, waiting for transfers between devices: 337 us -> none  [the longest x3 148 us: gather_rows(): return lax.all_gather(row_share, 'heads', axis=0, tiled=True)]
    dot_general x95 -> x19, matrix products: 254 us -> 59 us  [dot(): return jnp.dot(left, right, preferred_element_type=f32)]
    ppermute x0 -> x70, starting transfers between devices: none -> 137 us  [perm(): return lambda value: lax.ppermute(value, AXES, table)]
    pallas_call x0 -> x4, Pallas kernels: none -> 97.9 us  [the longest x2 63.6 us: attend_bwd(): pl.pallas_call(functools.partial(bwd_kernel, prefix_kv is not None), grid...]
    ppermute x0 -> x70, waiting for transfers between devices: none -> 81.3 us  [perm(): return lambda value: lax.ppermute(value, AXES, table)]
    another operation x29 -> x0, local copies, waits for them, and re-layouts: 48.8 us -> none  [the longest x9 15.5 us: to_heads(): arrays.reshape(arrays.shape[0], arrays.shape[1], heads_here, HD)]
    squeeze x25 -> x3, local copies, waits for them, and re-layouts: 33.2 us -> 0.3 us  [the longest x2 0.3 us: fast_body(): prefix_kv = (placed[0], placed[1])]
  transfers between devices with their start and end apart: 15 -> 70, of which waited for: 13 -> 18; matrix products, arithmetic and copies ran while one was open for 13% -> 30% of each run, Pallas kernels for 0% -> 20%
where the time goes in v1:
time: 490 us; the launch traced here: 487 us
  starting transfers between devices  137 us (28%)
  matrix products  101 us (21%)
  Pallas kernels  97.9 us (20%)
  waiting for transfers between devices  81.3 us (17%)
  other arithmetic  35 us (7%)
  local copies, waits for them, and re-layouts  31.4 us (6%)
    ppermute x70, starting transfers between devices, perm(): return lambda value: lax.ppermute(value, AXES, table)  137 us
    ppermute x70, waiting for transfers between devices, perm(): return lambda value: lax.ppermute(value, AXES, table)  81.3 us
    pallas_call x2, Pallas kernels, attend_bwd(): pl.pallas_call(functools.partial(bwd_kernel, prefix_kv is not None), grid...  63.6 us
    dot_general x19, matrix products, dot(): return jnp.dot(left, right, preferred_element_type=f32)  59 us
    dot_general x17, matrix products, dot_right(): lax.dot_general(left, right, (((1,), (1,)), ((), ())), preferred_element_...  39.4 us
    pallas_call x2, Pallas kernels, attend_fwd(): pl.pallas_call(functools.partial(fwd_kernel, prefix_kv is not None), grid...  34.3 us
    concatenate x10, other arithmetic, four(): return jnp.concatenate([value, from_x, from_y, from_d], axis=axis)  13.9 us
    dynamic_slice x10, local copies, waits for them, and re-layouts, half(): return lax.dynamic_slice_in_dim(value, core * size, size, axis)  13.5 us
  transfers between devices with their start and end apart: 70, of which 18 were waited for; matrix products, arithmetic and copies ran while one was open for 30% of the time, Pallas kernels for 20%

profile of v1, /device:TPU:1, one launch (start us, length us, event | category | flops | bytes accessed | tf_op | source)
XLA Modules:
  0.0 487.3 jit_solution(1909859201539783215)
XLA Ops:
  37.0 6.3 %collective-permute-start.25 = (bf16[128,1024]{1,0:T(8,128)(2,1)S(1)}, bf16[128,1024]{1,0:T(8,128)(2,1)S(1)}, u32[]{:S(2)}, u32[]{:S(2)}) collective-permute-start(bf16[128,1024]{1,0:T(8,128)(2,1)S(1)} %constant_dynamic-slice_fusion.5), channel_id=1, source_target_pairs={{0,1},{1,0},{2,3},{3,2},{4,5},{5,4},{6,7},{7,6},{8,9},{9,8},{10,11... | collective-permute-start | bytes 786440 | tf_op jit(solution)/shard_map/ppermute | solution.py:708
  44.6 15.6 %collective-permute-done.38 = bf16[64,1024]{0,1:T(8,128)(2,1)S(1)} collective-permute-done((bf16[64,1024]{0,1:T(8,128)(2,1)}, bf16[64,1024]{0,1:T(8,128)(2,1)S(1)}, u32[]{:S(2)}, u32[]{:S(2)}) %collective-permute-start.38) | collective-permute-done | bytes 131104 | tf_op jit(solution)/shard_map/ppermute | solution.py:708
  73.9 18.2 %collective-permute-done.9 = bf16[128,1024]{1,0:T(8,128)(2,1)S(1)} collective-permute-done((bf16[128,1024]{1,0:T(8,128)(2,1)S(1)}, bf16[128,1024]{1,0:T(8,128)(2,1)S(1)}, u32[]{:S(2)}, u32[]{:S(2)}) %collective-permute-start.9) | collective-permute-done | bytes 262176 | tf_op jit(solution)/shard_map/ppermute | solution.py:708
  92.4 5.2 %collective-permute-start.20 = (bf16[512,1024]{1,0:T(8,128)(2,1)}, bf16[512,1024]{1,0:T(8,128)(2,1)}, u32[]{:S(2)}, u32[]{:S(2)}) collective-permute-start(bf16[512,1024]{1,0:T(8,128)(2,1)} %param.22), channel_id=1, source_target_pairs={{0,0},{1,4},{2,2},{3,6},{4,1},{5,5},{6,3},{7,7},{8,8},{9,12},{10,1... | collective-permute-start | bytes 3145736 | tf_op jit(solution)/shard_map/ppermute | solution.py:708
  97.7 6.9 %collective-permute-start.11 = (bf16[128,1024]{1,0:T(8,128)(2,1)}, bf16[128,1024]{1,0:T(8,128)(2,1)}, u32[]{:S(2)}, u32[]{:S(2)}) collective-permute-start(bf16[128,1024]{1,0:T(8,128)(2,1)} %collective-permute-done.10), channel_id=1, source_target_pairs={{0,1},{1,0},{2,3},{3,2},{4,5},{5,4},{6,7},{7,6},{8,9},{9,8},{10,11... | collective-permute-start | bytes 786440 | tf_op jit(solution)/shard_map/ppermute | solution.py:708
  146.9 15.8 %attend_forward.2 = (bf16[1024,512]{1,0:T(8,128)(2,1)S(1)}, f32[4,8,1024]{2,1,0:T(8,128)S(1)}) custom-call(s32[4,4]{1,0:T(4,128)S(1)} %pad_add_fusion.win, bf16[1024,1536]{1,0:T(8,128)(2,1)S(1)} %pad_maximum_fusion.3.q_ref.k_ref.v_ref, bf16[1024,1536]{1,0:T(8,128)(2,1)S(1)} %pad_maximum_fusion.3.q_ref.k_ref.v_ref, ...), custom_call_target="tpu_custom_call" | custom-call | flops 2147483648 | bytes 6291456 | tf_op jit(solution)/shard_map/attend_forward/pallas_call | solution.py:617
  162.7 7.9 %collective-permute-done.24 = bf16[2,1024,128]{2,1,0:T(8,128)(2,1)S(1)} collective-permute-done((bf16[2,1024,128]{2,1,0:T(8,128)(2,1)S(1)}, bf16[2,1024,128]{2,1,0:T(8,128)(2,1)S(1)}, u32[]{:S(2)}, u32[]{:S(2)}) %collective-permute-start.24) | collective-permute-done | bytes 524320 | tf_op jit(solution)/shard_map/ppermute | solution.py:708
  192.4 18.5 %attend_forward.3 = (bf16[1024,512]{1,0:T(8,128)(2,1)S(1)}, f32[4,8,1024]{2,1,0:T(8,128)S(1)}) custom-call(s32[4,4]{1,0:T(4,128)S(1)} %pad_add_fusion.1.win, bf16[1024,512]{1,0:T(8,128)(2,1)S(1)} %maximum_select_fusion.2.q_ref, bf16[1024,1024]{1,0:T(8,128)(2,1)S(1)} %pad_maximum_fusion.5.k_ref.v_ref, bf16[1024,1024]{1,0:T(8,128)(2,1)S(1)} %pad_maximum_fusion.5.k_ref.v_ref, ...), custom_call_target="tpu_custom_call" | custom-call | flops 2147483648 | bytes 6291456 | tf_op jit(solution)/shard_map/attend_forward/pallas_call | solution.py:617
  211.1 5.1 %collective-permute-start.47 = (bf16[512,1024]{1,0:T(8,128)(2,1)}, bf16[512,1024]{1,0:T(8,128)(2,1)S(1)}, u32[]{:S(2)}, u32[]{:S(2)}) collective-permute-start(bf16[512,1024]{1,0:T(8,128)(2,1)} %param.23), channel_id=1, source_target_pairs={{0,0},{1,4},{2,2},{3,6},{4,1},{5,5},{6,3},{7,7},{8,8},{9,12},{10,1... | collective-permute-start | bytes 3145736 | tf_op jit(solution)/shard_map/ppermute | solution.py:708
  216.1 5.4 %collective-permute-done.32 = bf16[1024,512]{1,0:T(8,128)(2,1)S(1)} collective-permute-done((bf16[1024,512]{1,0:T(8,128)(2,1)}, bf16[1024,512]{1,0:T(8,128)(2,1)S(1)}, u32[]{:S(2)}, u32[]{:S(2)}) %collective-permute-start.32) | collective-permute-done | bytes 1048608 | tf_op jit(solution)/shard_map/ppermute | solution.py:708
  237.6 12.9 %fusion.35 = f32[512,1024]{1,0:T(8,128)S(1)} fusion(f32[512,2048]{1,0:T(8,128)S(1)} %fusion.176, bf16[512,1024]{1,0:T(8,128)(2,1)} %collective-permute-done.35, bf16[512,1024]{1,0:T(8,128)(2,1)S(1)} %copy-done.74, bf16[512,1024]{1,0:T(8,128)(2,1)S(1)} %copy-done.76, bf16[512,1024]{1,0:T(8,128)(2,1)S(1)} %copy-done.38), kind=kOutput, calls=%fused_computation.90 | convolution fusion | flops 2232418304 | bytes 10485760 | tf_op jit(solution)/shard_map/dot_general | solution.py:820
  253.0 10.7 %fusion.33 = f32[512,1024]{1,0:T(8,128)S(1)} fusion(bf16[2048,1024]{1,0:T(8,128)(2,1)S(1)} %collective-permute-done.37, f32[512,2048]{1,0:T(8,128)S(1)} %fusion.177), kind=kOutput, calls=%fused_computation.89 | convolution fusion | flops 2215641088 | bytes 10485760 | tf_op jit(solution)/shard_map/dot_general | solution.py:820
  277.8 10.9 %fusion.47 = f32[512,1024]{1,0:T(8,128)} fusion(bf16[1024,2048]{1,0:T(8,128)(2,1)} %copy-done.117, f32[512,2048]{1,0:T(8,128)} %copy-done.121, bf16[512,1024]{1,0:T(8,128)(2,1)} %copy-done.54, bf16[2048,1024]{1,0:T(8,128)(2,1)} %copy-done.116), kind=kOutput, calls=%fused_computation.133 | convolution fusion | flops 4305453056 | bytes 15728640 | tf_op jit(solution)/shard_map/dot_general | solution.py:22
  288.7 11.0 %fusion.48 = f32[512,1024]{1,0:T(8,128)} fusion(bf16[1024,2048]{1,0:T(8,128)(2,1)} %copy-done.36, f32[512,2048]{1,0:T(8,128)} %copy-done.120, bf16[512,1024]{1,0:T(8,128)(2,1)} %copy-done.54, bf16[512,1024]{1,0:T(8,128)(2,1)} %collective-permute-done.35, bf16[512,1024]{1,0:T(8,128)(2,1)} %copy-done.73, bf16[512,1024]{1,0:T(8,128)(2,1)} %copy-done.75, ...), kind=kOutput, calls=%fused_computation.134 | convolution fusion | flops 4322230272 | bytes 15728640 | tf_op jit(solution)/shard_map/dot_general | solution.py:22
  308.2 5.5 %collective-permute-start.48 = (bf16[512,512]{1,0:T(8,128)(2,1)S(1)}, bf16[512,512]{1,0:T(8,128)(2,1)S(1)}, u32[]{:S(2)}, u32[]{:S(2)}) collective-permute-start(bf16[512,512]{1,0:T(8,128)(2,1)S(1)} %convolution_convert_fusion.8), channel_id=1, source_target_pairs={{0,4},{1,5},{2,6},{3,7},{4,0},{5,1},{6,2},{7,3},{8,12},{9,13},{10,... | collective-permute-start | bytes 1572872 | tf_op jit(solution)/shard_map/ppermute | solution.py:708
  316.9 31.3 %attend_backward.2 = (bf16[1024,512]{1,0:T(8,128)(2,1)S(1)}, bf16[1024,512]{1,0:T(8,128)(2,1)S(1)}, bf16[1024,512]{1,0:T(8,128)(2,1)S(1)}) custom-call(s32[4,4]{1,0:T(4,128)S(1)} %pad_add_fusion.1.win, bf16[1024,512]{1,0:T(8,128)(2,1)S(1)} %copy-done.7, bf16[1024,1024]{1,0:T(8,128)(2,1)S(1)} %copy-done.5, bf16[1024,1024]{1,0:T(8,128)(2,1)S(1)} %copy-done.5, ...), custom_call_target="tpu_custom_call" | custom-call | flops 5368709120 | bytes 10485760 | tf_op jit(solution)/shard_map/attend_backward/pallas_call | solution.py:648
  359.0 5.1 %collective-permute-start.63 = (bf16[64,2048]{1,0:T(8,128)(2,1)S(1)}, bf16[64,2048]{1,0:T(8,128)(2,1)S(1)}, u32[]{:S(2)}, u32[]{:S(2)}) collective-permute-start(bf16[64,2048]{1,0:T(8,128)(2,1)S(1)} %get-tuple-element.95), channel_id=1, source_target_pairs={{0,1},{1,0},{2,3},{3,2},{4,5},{5,4},{6,7},{7,6},{8,9},{9,8},{10,11... | collective-permute-start | bytes 786440 | tf_op jit(solution)/shard_map/ppermute | solution.py:708
  364.1 10.9 %collective-permute-start.65 = (bf16[64,2048]{1,0:T(8,128)(2,1)S(1)}, bf16[64,2048]{1,0:T(8,128)(2,1)}, u32[]{:S(2)}, u32[]{:S(2)}) collective-permute-start(bf16[64,2048]{1,0:T(8,128)(2,1)S(1)} %get-tuple-element.96), channel_id=1, source_target_pairs={{0,2},{1,3},{2,0},{3,1},{4,6},{5,7},{6,4},{7,5},{8,10},{9,11},{10,... | collective-permute-start | bytes 786440 | tf_op jit(solution)/shard_map/ppermute | solution.py:708
  376.9 4.9 collective-permute-done.65
  384.5 32.3 %attend_backward.3 = (bf16[1024,512]{1,0:T(8,128)(2,1)S(1)}, bf16[1024,512]{1,0:T(8,128)(2,1)S(1)}, bf16[1024,512]{1,0:T(8,128)(2,1)S(1)}, f32[4,2,32,128]{3,2,1,0:T(8,128)S(1)}) custom-call(s32[4,4]{1,0:T(4,128)S(1)} %copy-done.17, bf16[1024,1536]{1,0:T(8,128)(2,1)S(1)} %copy-done.3, bf16[1024,1536]{1,0:T(8,128)(2,1)S(1)} %copy-done.3, ...), custom_call_target="tpu_custom_call" | custom-call | flops 5368709120 | bytes 10485760 | tf_op jit(solution)/shard_map/attend_backward/pallas_call | solution.py:648
  423.5 4.9 collective-permute-start.54
  434.1 10.0 %collective-permute-start.68 = (bf16[64,2048]{1,0:T(8,128)(2,1)S(1)}, bf16[64,2048]{1,0:T(8,128)(2,1)S(1)}, u32[]{:S(2)}, u32[]{:S(2)}) collective-permute-start(bf16[64,2048]{1,0:T(8,128)(2,1)S(1)} %fusion.58), channel_id=1, source_target_pairs={{0,16},{1,17},{2,18},{3,19},{4,20},{5,21},{6,22},{7,23},{8,24},{9,... | collective-permute-start | bytes 786440 | tf_op jit(solution)/shard_map/ppermute | solution.py:708
  447.4 9.1 %collective-permute-done.68 = bf16[64,2048]{1,0:T(8,128)(2,1)S(1)} collective-permute-done((bf16[64,2048]{1,0:T(8,128)(2,1)S(1)}, bf16[64,2048]{1,0:T(8,128)(2,1)S(1)}, u32[]{:S(2)}, u32[]{:S(2)}) %collective-permute-start.68) | collective-permute-done | bytes 262176 | tf_op jit(solution)/shard_map/ppermute | solution.py:708
  460.4 6.2 %collective-permute-start.69 = (bf16[64,2048]{1,0:T(8,128)(2,1)S(1)}, bf16[64,2048]{1,0:T(8,128)(2,1)S(1)}, u32[]{:S(2)}, u32[]{:S(2)}) collective-permute-start(bf16[64,2048]{1,0:T(8,128)(2,1)S(1)} %get-tuple-element.79), channel_id=1, source_target_pairs={{0,4},{1,5},{2,6},{3,7},{4,0},{5,1},{6,2},{7,3},{8,12},{9,13},{10,... | collective-permute-start | bytes 786440 | tf_op jit(solution)/shard_map/ppermute | solution.py:708
  (502 shorter events, 213.6 us)
Async XLA Ops:
  6.3 30.6 %collective-permute-start.42 = (bf16[64,1024]{1,0:T(8,128)(2,1)S(1)}, bf16[64,1024]{1,0:T(8,128)(2,1)}, u32[]{:S(2)}, u32[]{:S(2)}) collective-permute-start(bf16[64,1024]{1,0:T(8,128)(2,1)S(1)} %constant_dynamic-slice_fusion.1), channel_id=1, source_target_pairs={{0,2},{1,3},{2,0},{3,1},{4,6},{5,7},{6,4},{7,5},{8,10},{9,11},{10,... | collective-permute-start | bytes 393224 | tf_op jit(solution)/shard_map/ppermute | solution.py:708
  6.6 36.6 %collective-permute-start.41 = (bf16[64,1024]{1,0:T(8,128)(2,1)S(1)}, bf16[64,1024]{1,0:T(8,128)(2,1)}, u32[]{:S(2)}, u32[]{:S(2)}) collective-permute-start(bf16[64,1024]{1,0:T(8,128)(2,1)S(1)} %constant_dynamic-slice_fusion.1), channel_id=1, source_target_pairs={{0,1},{1,0},{2,3},{3,2},{4,5},{5,4},{6,7},{7,6},{8,9},{9,8},{10,11... | collective-permute-start | bytes 393224 | tf_op jit(solution)/shard_map/ppermute | solution.py:708
  23.9 39.4 %collective-permute-start.26 = (bf16[128,1024]{1,0:T(8,128)(2,1)S(1)}, bf16[128,1024]{1,0:T(8,128)(2,1)}, u32[]{:S(2)}, u32[]{:S(2)}) collective-permute-start(bf16[128,1024]{1,0:T(8,128)(2,1)S(1)} %constant_dynamic-slice_fusion.5), channel_id=1, source_target_pairs={{0,2},{1,3},{2,0},{3,1},{4,6},{5,7},{6,4},{7,5},{8,10},{9,11},{10,... | collective-permute-start | bytes 786440 | tf_op jit(solution)/shard_map/ppermute | solution.py:708
  32.5 73.4 %collective-permute-start = (bf16[512,1024]{1,0:T(8,128)(2,1)}, bf16[512,1024]{1,0:T(8,128)(2,1)}, u32[]{:S(2)}, u32[]{:S(2)}) collective-permute-start(bf16[512,1024]{1,0:T(8,128)(2,1)} %param.21), channel_id=1, source_target_pairs={{0,0},{1,4},{2,2},{3,6},{4,1},{5,5},{6,3},{7,7},{8,8},{9,12},{10,1... | collective-permute-start | bytes 3145736 | tf_op jit(solution)/shard_map/ppermute | solution.py:708
  63.3 41.3 %collective-permute-start.3 = (bf16[3,1024,128]{2,1,0:T(8,128)(2,1)}, bf16[3,1024,128]{2,1,0:T(8,128)(2,1)}, u32[]{:S(2)}, u32[]{:S(2)}) collective-permute-start(bf16[3,1024,128]{2,1,0:T(8,128)(2,1)} %constant_dynamic-slice_fusion.11), channel_id=1, source_target_pairs={{0,1},{1,0},{2,3},{3,2},{4,5},{5,4},{6,7},{7,6},{8,9},{9,8},{10,11... | collective-permute-start | bytes 2359304 | tf_op jit(solution)/shard_map/ppermute | solution.py:708
  92.1 33.0 %collective-permute-start.4 = (bf16[3,1024,128]{2,1,0:T(8,128)(2,1)S(1)}, bf16[3,1024,128]{2,1,0:T(8,128)(2,1)}, u32[]{:S(2)}, u32[]{:S(2)}) collective-permute-start(bf16[3,1024,128]{2,1,0:T(8,128)(2,1)S(1)} %copy-done.40), channel_id=1, source_target_pairs={{0,2},{1,3},{2,0},{3,1},{4,6},{5,7},{6,4},{7,5},{8,10},{9,11},{10,... | collective-permute-start | bytes 2359304 | tf_op jit(solution)/shard_map/ppermute | solution.py:708
  92.4 39.5 %collective-permute-start.20 = (bf16[512,1024]{1,0:T(8,128)(2,1)}, bf16[512,1024]{1,0:T(8,128)(2,1)}, u32[]{:S(2)}, u32[]{:S(2)}) collective-permute-start(bf16[512,1024]{1,0:T(8,128)(2,1)} %param.22), channel_id=1, source_target_pairs={{0,0},{1,4},{2,2},{3,6},{4,1},{5,5},{6,3},{7,7},{8,8},{9,12},{10,1... | collective-permute-start | bytes 3145736 | tf_op jit(solution)/shard_map/ppermute | solution.py:708
  127.3 50.8 %collective-permute-start.30 = (bf16[1024,512]{1,0:T(8,128)(2,1)S(1)}, bf16[1024,512]{1,0:T(8,128)(2,1)}, u32[]{:S(2)}, u32[]{:S(2)}) collective-permute-start(bf16[1024,512]{1,0:T(8,128)(2,1)S(1)} %copy-done.39), channel_id=1, source_target_pairs={{0,1},{1,0},{2,3},{3,2},{4,5},{5,4},{6,7},{7,6},{8,9},{9,8},{10,11... | collective-permute-start | bytes 3145736 | tf_op jit(solution)/shard_map/ppermute | solution.py:708
  131.9 48.5 %collective-permute-start.34 = (bf16[512,1024]{1,0:T(8,128)(2,1)S(1)}, bf16[512,1024]{1,0:T(8,128)(2,1)S(1)}, u32[]{:S(2)}, u32[]{:S(2)}) collective-permute-start(bf16[512,1024]{1,0:T(8,128)(2,1)S(1)} %constant_dynamic-slice_fusion.2), channel_id=1, source_target_pairs={{0,2},{1,3},{2,0},{3,1},{4,6},{5,7},{6,4},{7,5},{8,10},{9,11},{10,... | collective-permute-start | bytes 3145736 | tf_op jit(solution)/shard_map/ppermute | solution.py:708
  132.2 42.0 %collective-permute-start.21 = (bf16[512,1024]{1,0:T(8,128)(2,1)}, bf16[512,1024]{1,0:T(8,128)(2,1)S(1)}, u32[]{:S(2)}, u32[]{:S(2)}) collective-permute-start(bf16[512,1024]{1,0:T(8,128)(2,1)} %collective-permute-done.20), channel_id=1, source_target_pairs={{0,4},{1,5},{2,6},{3,7},{4,0},{5,1},{6,2},{7,3},{8,12},{9,13},{10,... | collective-permute-start | bytes 3145736 | tf_op jit(solution)/shard_map/ppermute | solution.py:708
  145.1 35.4 %collective-permute-start.13 = (bf16[512,1024]{1,0:T(8,128)(2,1)S(1)}, bf16[512,1024]{1,0:T(8,128)(2,1)S(1)}, u32[]{:S(2)}, u32[]{:S(2)}) collective-permute-start(bf16[512,1024]{1,0:T(8,128)(2,1)S(1)} %pad_maximum_fusion.6), channel_id=1, source_target_pairs={{0,4},{1,5},{2,6},{3,7},{4,0},{5,1},{6,2},{7,3},{8,12},{9,13},{10,... | collective-permute-start | bytes 3145736 | tf_op jit(solution)/shard_map/ppermute | solution.py:708
  174.1 36.9 %collective-permute-start.31 = (bf16[1024,512]{1,0:T(8,128)(2,1)S(1)}, bf16[1024,512]{1,0:T(8,128)(2,1)}, u32[]{:S(2)}, u32[]{:S(2)}) collective-permute-start(bf16[1024,512]{1,0:T(8,128)(2,1)S(1)} %copy-done.39), channel_id=1, source_target_pairs={{0,2},{1,3},{2,0},{3,1},{4,6},{5,7},{6,4},{7,5},{8,10},{9,11},{10,... | collective-permute-start | bytes 3145736 | tf_op jit(solution)/shard_map/ppermute | solution.py:708
  178.1 47.3 %collective-permute-start.33 = (bf16[512,1024]{1,0:T(8,128)(2,1)S(1)}, bf16[512,1024]{1,0:T(8,128)(2,1)S(1)}, u32[]{:S(2)}, u32[]{:S(2)}) collective-permute-start(bf16[512,1024]{1,0:T(8,128)(2,1)S(1)} %constant_dynamic-slice_fusion.2), channel_id=1, source_target_pairs={{0,1},{1,0},{2,3},{3,2},{4,5},{5,4},{6,7},{7,6},{8,9},{9,8},{10,11... | collective-permute-start | bytes 3145736 | tf_op jit(solution)/shard_map/ppermute | solution.py:708
  180.6 41.0 %collective-permute-start.32 = (bf16[1024,512]{1,0:T(8,128)(2,1)}, bf16[1024,512]{1,0:T(8,128)(2,1)S(1)}, u32[]{:S(2)}, u32[]{:S(2)}) collective-permute-start(bf16[1024,512]{1,0:T(8,128)(2,1)} %collective-permute-done.30), channel_id=1, source_target_pairs={{0,2},{1,3},{2,0},{3,1},{4,6},{5,7},{6,4},{7,5},{8,10},{9,11},{10,... | collective-permute-start | bytes 3145736 | tf_op jit(solution)/shard_map/ppermute | solution.py:708
  181.4 45.1 %collective-permute-start.35 = (bf16[512,1024]{1,0:T(8,128)(2,1)S(1)}, bf16[512,1024]{1,0:T(8,128)(2,1)}, u32[]{:S(2)}, u32[]{:S(2)}) collective-permute-start(bf16[512,1024]{1,0:T(8,128)(2,1)S(1)} %collective-permute-done.34), channel_id=1, source_target_pairs={{0,1},{1,0},{2,3},{3,2},{4,5},{5,4},{6,7},{7,6},{8,9},{9,8},{10,11... | collective-permute-start | bytes 3145736 | tf_op jit(solution)/shard_map/ppermute | solution.py:708
  191.6 37.5 %collective-permute-start.29 = (bf16[512,1024]{1,0:T(8,128)(2,1)S(1)}, bf16[512,1024]{1,0:T(8,128)(2,1)S(1)}, u32[]{:S(2)}, u32[]{:S(2)}) collective-permute-start(bf16[512,1024]{1,0:T(8,128)(2,1)S(1)} %pad_maximum_fusion.8), channel_id=1, source_target_pairs={{0,4},{1,5},{2,6},{3,7},{4,0},{5,1},{6,2},{7,3},{8,12},{9,13},{10,... | collective-permute-start | bytes 3145736 | tf_op jit(solution)/shard_map/ppermute | solution.py:708
  211.1 55.2 %collective-permute-start.47 = (bf16[512,1024]{1,0:T(8,128)(2,1)}, bf16[512,1024]{1,0:T(8,128)(2,1)S(1)}, u32[]{:S(2)}, u32[]{:S(2)}) collective-permute-start(bf16[512,1024]{1,0:T(8,128)(2,1)} %param.23), channel_id=1, source_target_pairs={{0,0},{1,4},{2,2},{3,6},{4,1},{5,5},{6,3},{7,7},{8,8},{9,12},{10,1... | collective-permute-start | bytes 3145736 | tf_op jit(solution)/shard_map/ppermute | solution.py:708
  273.1 78.7 %collective-permute-start.62 = (bf16[256,2048]{1,0:T(8,128)(2,1)}, bf16[256,2048]{1,0:T(8,128)(2,1)}, u32[]{:S(2)}, u32[]{:S(2)}) collective-permute-start(bf16[256,2048]{1,0:T(8,128)(2,1)} %pad_maximum_fusion.9), channel_id=1, source_target_pairs={{0,4},{1,5},{2,6},{3,7},{4,0},{5,1},{6,2},{7,3},{8,12},{9,13},{10,... | collective-permute-start | bytes 3145736 | tf_op jit(solution)/shard_map/ppermute | solution.py:708
  273.1 202.5 %collective-permute-start.46 = (bf16[512,1024]{1,0:T(8,128)(2,1)}, bf16[512,1024]{1,0:T(8,128)(2,1)}, u32[]{:S(2)}, u32[]{:S(2)}) collective-permute-start(bf16[512,1024]{1,0:T(8,128)(2,1)} %get-tuple-element.92), channel_id=1, source_target_pairs={{0,0},{1,4},{2,2},{3,6},{4,1},{5,5},{6,3},{7,7},{8,8},{9,12},{10,1... | collective-permute-start | bytes 3145736 | tf_op jit(solution)/shard_map/ppermute | solution.py:708
  351.6 71.5 %collective-permute-start.53 = (bf16[512,1024]{1,0:T(8,128)(2,1)S(1)}, bf16[512,1024]{1,0:T(8,128)(2,1)S(1)}, u32[]{:S(2)}, u32[]{:S(2)}) collective-permute-start(bf16[512,1024]{1,0:T(8,128)(2,1)S(1)} %dynamic-slice_convert_fusion), channel_id=1, source_target_pairs={{0,4},{1,5},{2,6},{3,7},{4,0},{5,1},{6,2},{7,3},{8,12},{9,13},{10,... | collective-permute-start | bytes 3145736 | tf_op jit(solution)/shard_map/ppermute | solution.py:708
  359.0 61.9 %collective-permute-start.63 = (bf16[64,2048]{1,0:T(8,128)(2,1)S(1)}, bf16[64,2048]{1,0:T(8,128)(2,1)S(1)}, u32[]{:S(2)}, u32[]{:S(2)}) collective-permute-start(bf16[64,2048]{1,0:T(8,128)(2,1)S(1)} %get-tuple-element.95), channel_id=1, source_target_pairs={{0,1},{1,0},{2,3},{3,2},{4,5},{5,4},{6,7},{7,6},{8,9},{9,8},{10,11... | collective-permute-start | bytes 786440 | tf_op jit(solution)/shard_map/ppermute | solution.py:708
  381.7 41.2 %collective-permute-start.64 = (bf16[64,2048]{1,0:T(8,128)(2,1)S(1)}, bf16[64,2048]{1,0:T(8,128)(2,1)S(1)}, u32[]{:S(2)}, u32[]{:S(2)}) collective-permute-start(bf16[64,2048]{1,0:T(8,128)(2,1)S(1)} %get-tuple-element.97), channel_id=1, source_target_pairs={{0,2},{1,3},{2,0},{3,1},{4,6},{5,7},{6,4},{7,5},{8,10},{9,11},{10,... | collective-permute-start | bytes 786440 | tf_op jit(solution)/shard_map/ppermute | solution.py:708
  382.9 40.0 %collective-permute-start.66 = (bf16[64,2048]{1,0:T(8,128)(2,1)}, bf16[64,2048]{1,0:T(8,128)(2,1)S(1)}, u32[]{:S(2)}, u32[]{:S(2)}) collective-permute-start(bf16[64,2048]{1,0:T(8,128)(2,1)} %collective-permute-done.65), channel_id=1, source_target_pairs={{0,1},{1,0},{2,3},{3,2},{4,5},{5,4},{6,7},{7,6},{8,9},{9,8},{10,11... | collective-permute-start | bytes 786440 | tf_op jit(solution)/shard_map/ppermute | solution.py:708
  423.5 55.6 %collective-permute-start.54 = (bf16[512,1024]{1,0:T(8,128)(2,1)S(1)}, bf16[512,1024]{1,0:T(8,128)(2,1)}, u32[]{:S(2)}, u32[]{:S(2)}) collective-permute-start(bf16[512,1024]{1,0:T(8,128)(2,1)S(1)} %add_convert_fusion), channel_id=1, source_target_pairs={{0,0},{1,4},{2,2},{3,6},{4,1},{5,5},{6,3},{7,7},{8,8},{9,12},{10,1... | collective-permute-start | bytes 3145736 | tf_op jit(solution)/shard_map/ppermute | solution.py:708
  (168 other events, 3474.6 us)

commit v2 on v0

--- a/solution.py
+++ b/solution.py
@@ -1,6 +1,12 @@
+import functools
+import math
+import typing
+
 import jax
 import jax.numpy as jnp
 from jax import lax
+from jax.experimental import pallas as pl
+from jax.experimental.pallas import tpu as pltpu
 from jax.sharding import PartitionSpec as P
 
 HD = 64
@@ -435,6 +441,1011 @@
     return (output, grad_input, grad_memory, prefix_grad, down_grad, up_grad)
 
 
+QB = 256
+KB = 256
+LOG2E = math.log2(math.e)
+NEG = -1e30
+
+
+def nt(a, b):
+    return lax.dot_general(a, b, (((1,), (1,)), ((), ())), preferred_element_type=jnp.float32)
+
+
+def nn(a, b):
+    return lax.dot_general(a, b, (((1,), (0,)), ((), ())), preferred_element_type=jnp.float32)
+
+
+def tn(a, b):
+    return lax.dot_general(a, b, (((0,), (0,)), ((), ())), preferred_element_type=jnp.float32)
+
+
+def half_lanes(v, h):
+    lane = lax.broadcasted_iota(jnp.int32, v.shape, 1)
+    keep = (lane < 64) if h == 0 else (lane >= 64)
+    return jnp.where(keep, v, jnp.zeros_like(v))
+
+
+def prefix_rows(scores):
+    row = lax.broadcasted_iota(jnp.int32, scores.shape, 0)
+    return jnp.where(lax.rem(row, 64) < 30, scores, NEG)
+
+
+MESH = pl.DeviceIdType.MESH
+TILE = 256
+
+TOK, TOK_C, MEM, MEM_C, COT, SEG, MSEG, SO_C, CO_C, CQ_C, Q_C = range(11)
+A_X, A_Y, A_D = 11, 15, 19
+R_X, R_Y, R_D = 23, 25, 27
+C_X, C_Y, C_D = 29, 32, 35
+SELF_CTX, CROSS_CTX = 38, 42
+FEED_I, FEED_O, FEED_A = 46, 53, 60
+SLOTS = 67
+OWN, KEEP = 7, 24
+LOCAL_SLOTS = 44
+
+
+def prefix_block(rows):
+    nothing = jnp.zeros_like(rows)
+    return jnp.concatenate([half_lanes(rows, 0), nothing, half_lanes(rows, 1), nothing], axis=0)
+
+
+def attend_tile(q, k, vt, mask, kp, vpt):
+    scale = 0.125 * LOG2E
+    rows = q.shape[0]
+    if kp is not None:
+        sp = prefix_rows(nt(kp, q) * scale)
+    outs, tops, sums = [], [], []
+    for h in range(2):
+        s = jnp.where(mask, nt(k, half_lanes(q, h)) * scale, NEG)
+        m = jnp.max(s, axis=0, keepdims=True)
+        if kp is not None:
+            m = jnp.maximum(m, jnp.max(sp[h * 64 : h * 64 + 32], axis=0, keepdims=True))
+        e = jnp.exp2(s - m)
+        outs.append(nn(vt[h * 64 : h * 64 + 64], e.astype(jnp.bfloat16)))
+        sums.append(jnp.sum(e, axis=0, keepdims=True))
+        tops.append(m)
+    if kp is not None:
+        mm = jnp.concatenate([jnp.broadcast_to(t, (64, rows)) for t in tops], axis=0)
+        ep = jnp.exp2(sp - mm)
+        sums = [sums[h] + jnp.sum(ep[h * 64 : h * 64 + 32], axis=0, keepdims=True) for h in range(2)]
+        extra = nn(vpt, ep.astype(jnp.bfloat16))
+        outs = [outs[h] + extra[h * 64 : h * 64 + 64] for h in range(2)]
+    both = jnp.concatenate([outs[h] * (1.0 / sums[h]) for h in range(2)], axis=0)
+    return both.T.astype(jnp.bfloat16), [tops[h] + jnp.log2(sums[h]) for h in range(2)]
+
+
+def forward_kernel(
+    tokens, memory, cotangent, seg, mseg, prefix, w_self, w_so, w_cq, w_ckv, w_co, fc_in, fc_out, ad, gain, bias,
+    o_wself, o_qkv, o_sctx, o_slse, o_pre, o_wso_m, o_wso_o, o_wkv, o_wq_m, o_wq_o, o_wco_m, o_wco_o,
+    o_q, o_kv, o_cctx, o_clse, o_resid1, o_resid2, o_bounds, o_tok, o_cot, fin, fout, fad,
+    wself, qkv, sctx, slse, pre, wso_m, wso_o, wkv, wq_m, wq_o, wco_m, wco_o,
+    q_all, kv, cctx, clse, resid1, resid2, bounds, tok, mem, sctx_o, cctx_o, q_send, hidden, low_one, vt, seg_v, mseg_v,
+    send, recv, local,
+):
+    row = lax.axis_index("rows")
+    head = lax.axis_index("heads")
+    c, z = lax.rem(row, 2), lax.div(row, 2)
+    x, y = lax.rem(head, 2), lax.div(head, 2)
+    odd = lax.rem(z, 2)
+    to_x = (row, 2 * y + 1 - x)
+    to_y = (row, 2 * (1 - y) + x)
+    to_d = (row, 2 * (1 - y) + 1 - x)
+    to_z = (2 * (z + 1 - 2 * odd) + c, head)
+    to_c = (2 * z + 1 - c, head)
+    to_s = (2 * z + x, 2 * y + c)
+    stays = c == x
+    moves = c != x
+
+    barrier = pltpu.get_barrier_semaphore()
+    for device in (to_x, to_y, to_d, to_z, to_c):
+        pl.semaphore_signal(barrier, inc=1, device_id=device, device_id_type=MESH)
+
+    @pl.when(moves)
+    def _():
+        pl.semaphore_signal(barrier, inc=1, device_id=to_s, device_id_type=MESH)
+
+    pl.semaphore_wait(barrier, 5 + moves.astype(jnp.int32))
+
+    def there(slot, src, dst, device):
+        return pltpu.make_async_remote_copy(
+            src_ref=src, dst_ref=dst, send_sem=send.at[slot], recv_sem=recv.at[slot], device_id=device, device_id_type=MESH
+        )
+
+    def here(slot, src, dst):
+        return pltpu.make_async_copy(src, dst, local.at[slot])
+
+    half = tok.shape[0] // 2
+    mine = pl.ds(pl.multiple_of(c * half, half), half)
+    others = pl.ds(pl.multiple_of((1 - c) * half, half), half)
+    partner_rows = pl.ds(pl.multiple_of(x * half, half), half)
+    lanes = pl.ds(pl.multiple_of(c * 128, 128), 128)
+    other_lanes = pl.ds(pl.multiple_of((1 - c) * 128, 128), 128)
+
+    pending = []
+
+    def go(copy):
+        copy.start()
+        pending.append(copy)
+        return copy
+
+    def swap_start(slot, src, target, dst_there, dst_here):
+        pl.when(moves)(lambda: there(slot, src, target.at[dst_there], to_s).start())
+        pl.when(stays)(lambda: here(slot, src, target.at[dst_here]).start())
+
+    def swap_wait(slot, src, target, dst_here):
+        pl.when(moves)(lambda: there(slot, src, target.at[dst_here], to_s).wait())
+        pl.when(stays)(lambda: here(slot, src, target.at[dst_here]).wait())
+
+    def seg_start(slot, src, dst):
+        @pl.when(stays)
+        def _():
+            here(slot, src.at[y], dst).start()
+            there(slot, src.at[y], dst, to_c).start()
+
+    def seg_wait(slot, src, dst):
+        @pl.when(stays)
+        def _():
+            here(slot, src.at[y], dst).wait()
+            there(slot, src.at[y], dst, to_c).wait_send()
+
+        pl.when(moves)(lambda: there(slot, src.at[y], dst, to_c).wait_recv())
+
+    swap_start(TOK, tokens, tok, partner_rows, mine)
+    own_a = [here(OWN + i, w_self.at[i, :, lanes], wself.at[0, :, pl.ds(128 * i, 128)]) for i in range(3)]
+    own_a.append(here(OWN + 3, prefix.at[:, :, lanes], pre.at[0]))
+    for copy in own_a:
+        copy.start()
+
+    def send_a(base, piece, device):
+        out = [
+            there(base + i, w_self.at[i, :, lanes], wself.at[piece, :, pl.ds(128 * i, 128)], device) for i in range(3)
+        ]
+        return out + [there(base + 3, prefix.at[:, :, lanes], pre.at[piece], device)]
+
+    ax, ay = send_a(A_X, 1, to_x), send_a(A_Y, 2, to_y)
+    for copy in ax + ay:
+        go(copy)
+    ad_ = [there(A_D + i, wself.at[1, :, pl.ds(128 * i, 128)], wself.at[3, :, pl.ds(128 * i, 128)], to_y) for i in range(3)]
+    ad_.append(there(A_D + 3, pre.at[1], pre.at[3], to_y))
+
+    seg_start(SEG, seg, seg_v)
+    seg_start(MSEG, mseg, mseg_v)
+    rows_c = pl.ds(pl.multiple_of(c * 128, 128), 128)
+    rows_o = pl.ds(pl.multiple_of((1 - c) * 128, 128), 128)
+    own_b = [
+        here(OWN + 4, w_so.at[rows_c], wso_m.at[pl.ds(0, 128)]),
+        here(OWN + 5, w_so.at[rows_o], wso_o.at[pl.ds(0, 128)]),
+        here(OWN + 6, w_co.at[rows_c], wco_m.at[pl.ds(0, 128)]),
+        here(OWN + 7, w_co.at[rows_o], wco_o.at[pl.ds(0, 128)]),
+        here(OWN + 8, w_cq.at[:, lanes], wq_m.at[:, pl.ds(0, 128)]),
+        here(OWN + 9, w_cq.at[:, other_lanes], wq_o.at[:, pl.ds(0, 128)]),
+        here(OWN + 10, w_ckv.at[0, :, lanes], wkv.at[0, :, pl.ds(0, 128)]),
+        here(OWN + 11, w_ckv.at[1, :, lanes], wkv.at[0, :, pl.ds(128, 128)]),
+    ]
+    for copy in own_b:
+        copy.start()
+
+    def send_r(base, piece, device):
+        place = pl.ds(128 * piece, 128)
+        return [
+            there(base, w_so.at[rows_c], wso_m.at[place], device),
+            there(base + 1, w_co.at[rows_c], wco_m.at[place], device),
+        ]
+
+    rx, ry, rd = send_r(R_X, 1, to_x), send_r(R_Y, 2, to_y), send_r(R_D, 3, to_d)
+
+    def send_c(base, piece, device):
+        return [
+            there(base, w_cq.at[:, lanes], wq_m.at[:, pl.ds(128 * piece, 128)], device),
+            there(base + 1, w_ckv.at[0, :, lanes], wkv.at[piece, :, pl.ds(0, 128)], device),
+            there(base + 2, w_ckv.at[1, :, lanes], wkv.at[piece, :, pl.ds(128, 128)], device),
+        ]
+
+    cx, cy = send_c(C_X, 1, to_x), send_c(C_Y, 2, to_y)
+    cd = [
+        there(C_D, wq_m.at[:, pl.ds(128, 128)], wq_m.at[:, pl.ds(384, 128)], to_y),
+        there(C_D + 1, wkv.at[1, :, pl.ds(0, 128)], wkv.at[3, :, pl.ds(0, 128)], to_y),
+        there(C_D + 2, wkv.at[1, :, pl.ds(128, 128)], wkv.at[3, :, pl.ds(128, 128)], to_y),
+    ]
+
+    hid = fc_in.shape[1]
+    units = ad.shape[1]
+    at_cols = lambda start, size: (slice(None), pl.ds(pl.multiple_of(start, 256), size))
+    at_rows = lambda start, size: (pl.ds(pl.multiple_of(start, 256), size), slice(None))
+    at_units = lambda start, size: (slice(None), pl.ds(pl.multiple_of(start, 32), size), slice(None))
+    def part(ref, lead, index):
+        return ref.at[index] if lead is None else ref.at[(lead,) + index]
+
+    class Feed:
+        def __init__(self, base, src, dst, size, at, through_x):
+            quarter = at(c * (size // 2) + odd * (size // 4), size // 4)
+            half_of = (slice(None),) + at(c * (size // 2), size // 2)
+            self.x = there(base, part(src, None, quarter), part(dst, 0, quarter), to_x)
+            self.y = there(base + 1, part(src, None, quarter), part(dst, 1, quarter), to_y)
+            if through_x:
+                self.d = there(base + 2, part(dst, 1, quarter), part(dst, 2, quarter), to_x)
+            else:
+                self.d = there(base + 2, part(dst, 0, quarter), part(dst, 2, quarter), to_y)
+            self.zx, self.zy, self.zd = [
+                there(base + 3 + i, part(dst, i, quarter), part(dst, i, quarter), to_z) for i in range(3)
+            ]
+            self.c = there(base + 6, dst.at[half_of], dst.at[half_of], to_c)
+
+    fi = Feed(FEED_I, fc_in, fin, hid, at_cols, True)
+    fo = Feed(FEED_O, fc_out, fout, hid, at_rows, False)
+    fa = Feed(FEED_A, ad, fad, units, at_units, False)
+
+    swap_wait(TOK, tokens, tok, mine)
+    tok_c = go(there(TOK_C, tok.at[mine], tok.at[mine], to_c))
+    saves = []
+
+    def keep(src, dst):
+        copy = here(KEEP + len(saves), src, dst)
+        copy.start()
+        saves.append(copy)
+
+    keep(tok.at[mine], o_tok)
+    seg_wait(SEG, seg, seg_v)
+    seg_wait(MSEG, mseg, mseg_v)
+    dec, men = seg_v[...], mseg_v[...]
+
+    def below(values, d):
+        return jnp.sum((values < d).astype(jnp.int32), axis=1, keepdims=True)
+
+    def pick(counts):
+        out = jnp.broadcast_to(counts[0], dec.shape)
+        for d in range(1, 4):
+            out = jnp.where(dec == d, counts[d], out)
+        return out
+
+    zero = jnp.zeros((1, 1), jnp.int32)
+    full = jnp.full((1, 1), MLEN, jnp.int32)
+    self_lo = pick([zero] + [below(dec, d) for d in range(1, 4)])
+    mem_counts = [zero] + [below(men, d) for d in range(1, 4)] + [full]
+    bounds[...] = jnp.concatenate(
+        [self_lo, lax.broadcasted_iota(jnp.int32, dec.shape, 1), pick(mem_counts[:4]), pick(mem_counts[1:]) - 1]
+        + [jnp.zeros_like(dec)] * 4,
+        axis=0,
+    )
+    keep(bounds, o_bounds)
+    for copy in own_a:
+        copy.wait()
+    tok_c.wait_recv()
+
+    def first_piece(p, _):
+        @pl.when(p == 1)
+        def _():
+            for copy in ax:
+                copy.wait_recv()
+            for copy in ad_ + rx + rd:
+                copy.start()
+            swap_start(MEM, memory, mem, partner_rows, mine)
+            for copy in cx:
+                copy.start()
+
+        @pl.when(p == 2)
+        def _():
+            for copy in ay:
+                copy.wait_recv()
+            for copy in ry + [fi.y, fi.x] + cy:
+                copy.start()
+
+        @pl.when(p == 3)
+        def _():
+            for copy in ad_:
+                copy.wait_recv()
+
+        def rows_of(t, _):
+            rows = pl.ds(pl.multiple_of(t * TILE, TILE), TILE)
+            qkv[p, rows, :] = nn(tok[rows, :], wself[p]).astype(jnp.bfloat16)
+            return 0
+
+        lax.fori_loop(0, SEQ // TILE, rows_of, 0)
+        vt[...] = qkv[p, :, 256:384].astype(jnp.float32).T.astype(jnp.bfloat16)
+        kp = prefix_block(pre[p, 0])
+        vpt = prefix_block(pre[p, 1]).astype(jnp.float32).T.astype(jnp.bfloat16)
+        place = pl.ds(pl.multiple_of(p * 128, 128), 128)
+        for qi in range(SEQ // QB):
+            width = (qi + 1) * QB
+            span = slice(qi * QB, (qi + 1) * QB)
+            pos = lax.broadcasted_iota(jnp.int32, (width, QB), 0)
+            mask = (pos >= bounds[0:1, span]) & (pos <= bounds[1:2, span])
+            out, lse = attend_tile(qkv[p, span, 0:128], qkv[p, 0:width, 128:256], vt[:, 0:width], mask, kp, vpt)
+            sctx[span, place] = out
+            for h in range(2):
+                slse[p, h : h + 1, span] = lse[h]
+        there(SELF_CTX + p, sctx.at[others, place], sctx_o.at[:, place], to_c).start()
+        return 0
+
+    lax.fori_loop(0, 4, first_piece, 0)
+    pending.extend(ad_ + rx + rd + cx + ry + cy + [fi.x, fi.y])
+    for i in range(4):
+        copy = there(SELF_CTX + i, sctx.at[others, pl.ds(128 * i, 128)], sctx_o.at[:, pl.ds(128 * i, 128)], to_c)
+        pending.append(copy)
+    sctx_in = pending[-4:]
+    keep(qkv, o_qkv)
+    keep(wself, o_wself)
+    keep(sctx, o_sctx)
+    keep(slse, o_slse)
+    keep(pre, o_pre)
+
+    for copy in rx + ry + rd:
+        copy.wait_recv()
+    for copy in own_b:
+        copy.wait()
+    foreign = pl.ds(128, 384)
+    so_c = go(there(SO_C, wso_m.at[foreign], wso_o.at[foreign], to_c))
+    co_c = go(there(CO_C, wco_m.at[foreign], wco_o.at[foreign], to_c))
+    fi.y.wait_recv()
+    go(fi.d)
+    go(fi.zy)
+    for copy in sctx_in + [so_c]:
+        copy.wait_recv()
+    keep(wso_m, o_wso_m)
+    keep(wso_o, o_wso_o)
+
+    def out_rows(t, resid_before, ctx_m, ctx_o, w_m, w_o):
+        rows = pl.ds(pl.multiple_of(t * TILE, TILE), TILE)
+        rows_all = pl.ds(pl.multiple_of(c * half + t * TILE, TILE), TILE)
+        return rows, rows_all, resid_before + nn(ctx_m[rows_all, :], w_m[...]) + nn(ctx_o[rows, :], w_o[...])
+
+    def out_one(t, _):
+        rows_all = pl.ds(pl.multiple_of(c * half + t * TILE, TILE), TILE)
+        rows, _, resid = out_rows(t, tok[rows_all, :].astype(jnp.float32), sctx, sctx_o, wso_m, wso_o)
+        resid1[rows, :] = resid
+        normed = norm_forward(resid, gain[0:1, :], bias[0:1, :])
+        hidden[rows, :] = normed
+        low_one[rows, :] = normed.astype(jnp.bfloat16)
+        return 0
+
+    lax.fori_loop(0, half // TILE, out_one, 0)
+    keep(resid1, o_resid1)
+
+    fi.x.wait_recv()
+    go(fi.zx)
+    for copy in cx:
+        copy.wait_recv()
+    for copy in cd:
+        go(copy)
+    go(fo.x)
+    go(fa.x)
+    swap_wait(MEM, memory, mem, mine)
+    mem_c = go(there(MEM_C, mem.at[mine], mem.at[mine], to_c))
+    for copy in cy:
+        copy.wait_recv()
+    go(fo.y)
+    go(fa.y)
+    for copy in cd:
+        copy.wait_recv()
+    cq_c = go(there(CQ_C, wq_m.at[:, foreign], wq_o.at[:, foreign], to_c))
+    mem_c.wait_recv()
+
+    def kv_rows(step, _):
+        p, t = lax.div(step, SEQ // TILE), lax.rem(step, SEQ // TILE)
+        rows = pl.ds(pl.multiple_of(t * TILE, TILE), TILE)
+        kv[p, rows, :] = nn(mem[rows, :], wkv[p]).astype(jnp.bfloat16)
+        return 0
+
+    lax.fori_loop(0, 4 * (MLEN // TILE), kv_rows, 0)
+    keep(kv, o_kv)
+    keep(wkv, o_wkv)
+    fi.d.wait_recv()
+    go(fi.zd)
+    cq_c.wait_recv()
+    keep(wq_m, o_wq_m)
+    keep(wq_o, o_wq_o)
+
+    def q_rows(t, _):
+        rows = pl.ds(pl.multiple_of(t * TILE, TILE), TILE)
+        rows_all = pl.ds(pl.multiple_of(c * half + t * TILE, TILE), TILE)
+        q_send[rows, :] = nn(low_one[rows, :], wq_o[...]).astype(jnp.bfloat16)
+        q_all[rows_all, :] = nn(low_one[rows, :], wq_m[...]).astype(jnp.bfloat16)
+        return 0
+
+    lax.fori_loop(0, half // TILE, q_rows, 0)
+    q_c = go(there(Q_C, q_send, q_all.at[mine], to_c))
+    q_c.wait_recv()
+    keep(q_all, o_q)
+
+    def second_piece(p, _):
+        @pl.when(p == 2)
+        def _():
+            fo.x.wait_recv()
+            fa.x.wait_recv()
+            for copy in (fo.d, fa.d, fo.zx, fa.zx):
+                copy.start()
+
+        vt[...] = kv[p, :, 128:256].astype(jnp.float32).T.astype(jnp.bfloat16)
+        place = pl.ds(pl.multiple_of(p * 128, 128), 128)
+
+        def block(qi, _):
+            span = pl.ds(pl.multiple_of(qi * QB, QB), QB)
+            pos = lax.broadcasted_iota(jnp.int32, (MLEN, QB), 0)
+            mask = (pos >= bounds[2:3, span]) & (pos <= bounds[3:4, span])
+            out, lse = attend_tile(q_all[span, place], kv[p, :, 0:128], vt[...], mask, None, None)
+            cctx[span, place] = out
+            for h in range(2):
+                clse[p, h : h + 1, span] = lse[h]
+            return 0
+
+        lax.fori_loop(0, SEQ // QB, block, 0)
+        there(CROSS_CTX + p, cctx.at[others, place], cctx_o.at[:, place], to_c).start()
+        return 0
+
+    lax.fori_loop(0, 4, second_piece, 0)
+    pending.extend([fo.d, fa.d, fo.zx, fa.zx])
+    for i in range(4):
+        copy = there(CROSS_CTX + i, cctx.at[others, pl.ds(128 * i, 128)], cctx_o.at[:, pl.ds(128 * i, 128)], to_c)
+        pending.append(copy)
+    cctx_in = pending[-4:]
+    keep(cctx, o_cctx)
+    keep(clse, o_clse)
+    for copy in (fo.y, fa.y):
+        copy.wait_recv()
+    go(fo.zy)
+    go(fa.zy)
+    swap_start(COT, cotangent, o_cot, slice(None), slice(None))
+    for copy in (fi.zx, fi.zy, fi.zd):
+        copy.wait_recv()
+    go(fi.c)
+    for copy in cctx_in + [co_c]:
+        copy.wait_recv()
+    keep(wco_m, o_wco_m)
+    keep(wco_o, o_wco_o)
+
+    def out_two(t, _):
+        rows = pl.ds(pl.multiple_of(t * TILE, TILE), TILE)
+        rows, _, resid = out_rows(t, hidden[rows, :], cctx, cctx_o, wco_m, wco_o)
+        resid2[rows, :] = resid
+        return 0
+
+    lax.fori_loop(0, half // TILE, out_two, 0)
+    keep(resid2, o_resid2)
+    for copy in (fo.d, fa.d):
+        copy.wait_recv()
+    go(fo.zd)
+    go(fa.zd)
+    for group in (fo, fa):
+        for copy in (group.zx, group.zy, group.zd):
+            copy.wait_recv()
+    go(fo.c)
+    go(fa.c)
+    for group in (fi, fo, fa):
+        group.c.wait_recv()
+    swap_wait(COT, cotangent, o_cot, slice(None))
+    for copy in pending:
+        copy.wait_send()
+    for copy in saves:
+        copy.wait()
+
+
+class Held(typing.NamedTuple):
+    wself: jax.Array
+    qkv: jax.Array
+    sctx: jax.Array
+    slse: jax.Array
+    pre: jax.Array
+    wso_m: jax.Array
+    wso_o: jax.Array
+    wkv: jax.Array
+    wq_m: jax.Array
+    wq_o: jax.Array
+    wco_m: jax.Array
+    wco_o: jax.Array
+    q: jax.Array
+    kv: jax.Array
+    cctx: jax.Array
+    clse: jax.Array
+    resid1: jax.Array
+    resid2: jax.Array
+    bounds: jax.Array
+    tok: jax.Array
+    cot: jax.Array
+    fin: jax.Array
+    fout: jax.Array
+    fad: jax.Array
+
+
+def forward_call(tokens, memory, cotangent, seg, mseg, prefix, w_self, w_so, w_cq, w_ckv, w_co, fc_in, fc_out, ad, gain, bias):
+    bf16, f32 = jnp.bfloat16, jnp.float32
+    half, deep = tokens.shape
+    shape = jax.ShapeDtypeStruct
+    held = dict(
+        wself=((4, deep, 384), bf16),
+        qkv=((4, SEQ, 384), bf16),
+        sctx=((SEQ, 512), bf16),
+        slse=((4, 8, SEQ), f32),
+        pre=((4, 2, 32, 128), bf16),
+        wso_m=((512, deep), bf16),
+        wso_o=((512, deep), bf16),
+        wkv=((4, deep, 256), bf16),
+        wq_m=((deep, 512), bf16),
+        wq_o=((deep, 512), bf16),
+        wco_m=((512, deep), bf16),
+        wco_o=((512, deep), bf16),
+        q=((SEQ, 512), bf16),
+        kv=((4, MLEN, 256), bf16),
+        cctx=((SEQ, 512), bf16),
+        clse=((4, 8, SEQ), f32),
+        resid1=((half, deep), f32),
+        resid2=((half, deep), f32),
+        bounds=((8, SEQ), jnp.int32),
+    )
+    outs = [shape(*value) for value in held.values()]
+    outs += [shape((half, deep), bf16), shape((half, deep), bf16)]
+    outs += [shape((3,) + fc_in.shape, bf16), shape((3,) + fc_out.shape, bf16), shape((3,) + ad.shape, bf16)]
+    scratch = [pltpu.VMEM(*value) for value in held.values()] + [
+        pltpu.VMEM((SEQ, deep), bf16),
+        pltpu.VMEM((MLEN, deep), bf16),
+        pltpu.VMEM((half, 512), bf16),
+        pltpu.VMEM((half, 512), bf16),
+        pltpu.VMEM((half, 512), bf16),
+        pltpu.VMEM((half, deep), f32),
+        pltpu.VMEM((half, deep), bf16),
+        pltpu.VMEM((128, SEQ), bf16),
+        pltpu.VMEM((1, SEQ), jnp.int32),
+        pltpu.VMEM((1, SEQ), jnp.int32),
+        pltpu.SemaphoreType.DMA((SLOTS,)),
+        pltpu.SemaphoreType.DMA((SLOTS,)),
+        pltpu.SemaphoreType.DMA((LOCAL_SLOTS,)),
+    ]
+    anywhere = pl.BlockSpec(memory_space=pl.ANY)
+    vmem = pl.BlockSpec(memory_space=pltpu.VMEM)
+    results = pl.pallas_call(
+        forward_kernel,
+        out_shape=outs,
+        in_specs=[anywhere] * 14 + [vmem] * 2,
+        out_specs=[anywhere] * len(outs),
+        scratch_shapes=scratch,
+        compiler_params=pltpu.CompilerParams(
+            collective_id=0, has_side_effects=True, vmem_limit_bytes=58 * 2**20
+        ),
+        name="layer_forward",
+    )(tokens, memory, cotangent, seg, mseg, prefix, w_self, w_so, w_cq, w_ckv, w_co, fc_in, fc_out, ad, gain, bias)
+    return Held(*results)
+
+
+def backward_kernel(has_prefix, first_bound, bounds_s, *refs):
+    if has_prefix:
+        qkv_ref, bounds, ctx_ref, dctx_ref, lse_ref, pre_ref, dqkv_ref, dpre_ref, kt_ref, dk_acc, dv_acc, dq_acc, dpre_acc = refs
+        q_at = lambda rows: qkv_ref[0, rows, 0:128]
+        k_at = lambda rows: qkv_ref[0, rows, 128:256]
+        v_at = lambda rows: qkv_ref[0, rows, 256:384]
+    else:
+        q_ref, kv_ref, bounds, ctx_ref, dctx_ref, lse_ref, dq_ref, dkv_ref, kt_ref, dk_acc, dv_acc, dq_acc = refs
+        q_at = lambda rows: q_ref[rows, :]
+        k_at = lambda rows: kv_ref[0, rows, 0:128]
+        v_at = lambda rows: kv_ref[0, rows, 128:256]
+    scale = 0.125 * LOG2E
+    kt_ref[...] = k_at(slice(None)).astype(jnp.float32).T.astype(jnp.bfloat16)
+    dk_acc[...] = jnp.zeros_like(dk_acc)
+    dv_acc[...] = jnp.zeros_like(dv_acc)
+    if has_prefix:
+        dpre_acc[...] = jnp.zeros_like(dpre_acc)
+        kp = prefix_block(pre_ref[0, 0])
+        vp = prefix_block(pre_ref[0, 1])
+        kpt = kp.astype(jnp.float32).T.astype(jnp.bfloat16)
+
+    def one(qi, _):
+        q0 = pl.multiple_of(qi * QB, QB)
+        span = pl.ds(q0, QB)
+        q = q_at(span)
+        dctx = dctx_ref[span, :]
+        lo = bounds[first_bound : first_bound + 1, span]
+        hi = bounds[first_bound + 1 : first_bound + 2, span]
+        prod = (dctx.astype(jnp.float32) * ctx_ref[span, :].astype(jnp.float32)).T
+        inner = [jnp.sum(prod[h * 64 : h * 64 + 64], axis=0, keepdims=True) for h in range(2)]
+        lse = [lse_ref[0, h : h + 1, span] for h in range(2)]
+        qh = [half_lanes(q, h) for h in range(2)]
+        dh = [half_lanes(dctx, h) for h in range(2)]
+        if has_prefix:
+            sp = prefix_rows(nt(kp, q) * scale)
+            rows = lambda pair: jnp.concatenate([jnp.broadcast_to(t, (64, QB)) for t in pair], axis=0)
+            pp = jnp.exp2(sp - rows(lse))
+            dpp = nt(vp, dctx)
+            dsp = (pp * (dpp - rows(inner))).astype(jnp.bfloat16)
+            dpre_acc[0] += nn(dsp, q)
+            dpre_acc[1] += nn(pp.astype(jnp.bfloat16), dctx)
+            dq_acc[...] = nn(kpt, dsp)
+        else:
+            dq_acc[...] = jnp.zeros_like(dq_acc)
+
+        def chunk(ki, _):
+            k0 = pl.multiple_of(ki * KB, KB)
+            keys = pl.ds(k0, KB)
+            k = k_at(keys)
+            v = v_at(keys)
+            pos = k0 + lax.broadcasted_iota(jnp.int32, (KB, QB), 0)
+            mask = (pos >= lo) & (pos <= hi)
+            ps, dss = [], []
+            for h in range(2):
+                s = nt(k, qh[h]) * scale
+                p = jnp.exp2(jnp.where(mask, s, NEG) - lse[h])
+                dp = nt(v, dh[h])
+                ds = (p * (dp - inner[h])).astype(jnp.bfloat16)
+                ps.append(p.astype(jnp.bfloat16))
+                dss.append(ds)
+                dq_acc[h * 64 : h * 64 + 64, :] += nn(kt_ref[h * 64 : h * 64 + 64, keys], ds)
+            dv_acc[keys, :] += nn(ps[0], dh[0]) + nn(ps[1], dh[1])
+            dk_acc[keys, :] += nn(dss[0], qh[0]) + nn(dss[1], qh[1])
+            return 0
+
+        lowest = lax.div(bounds_s[first_bound, q0], KB)
+        highest = lax.div(bounds_s[first_bound + 1, q0 + QB - 1], KB) + 1
+        lax.fori_loop(lowest, highest, chunk, 0)
+        dq = (dq_acc[...].T * 0.125).astype(jnp.bfloat16)
+        if has_prefix:
+            dqkv_ref[0, span, 0:128] = dq
+        else:
+            dq_ref[span, :] = dq
+        return 0
+
+    lax.fori_loop(0, SEQ // QB, one, 0)
+    dk = (dk_acc[...] * 0.125).astype(jnp.bfloat16)
+    dv = dv_acc[...].astype(jnp.bfloat16)
+    if has_prefix:
+        dqkv_ref[0, :, 128:256] = dk
+        dqkv_ref[0, :, 256:384] = dv
+        lane = lax.broadcasted_iota(jnp.int32, (32, 128), 1)
+        for i, factor in ((0, 0.125), (1, 1.0)):
+            dpre_ref[0, i] = jnp.where(lane < 64, dpre_acc[i, 0:32], dpre_acc[i, 64:96]) * factor
+    else:
+        dkv_ref[0, :, 0:128] = dk
+        dkv_ref[0, :, 128:256] = dv
+
+
+def backward_call(has_prefix, arrays, bounds, ctx, dctx, lse, pre=None):
+    col = pl.BlockSpec((SEQ, 128), lambda j, *_: (0, j))
+    piece = lambda width: pl.BlockSpec((1, SEQ, width), lambda j, *_: (j, 0, 0))
+    shape = jax.ShapeDtypeStruct
+    bf16, f32 = jnp.bfloat16, jnp.float32
+    if has_prefix:
+        in_specs = [piece(384)]
+        out_specs = [piece(384), pl.BlockSpec((1, 2, 32, 128), lambda j, *_: (j, 0, 0, 0))]
+        out_shape = [shape((4, SEQ, 384), bf16), shape((4, 2, 32, 128), f32)]
+    else:
+        in_specs = [col, piece(256)]
+        out_specs = [col, piece(256)]
+        out_shape = [shape((SEQ, 512), bf16), shape((4, SEQ, 256), bf16)]
+    in_specs += [
+        pl.BlockSpec((8, SEQ), lambda j, *_: (0, 0)),
+        col,
+        col,
+        pl.BlockSpec((1, 8, SEQ), lambda j, *_: (j, 0, 0)),
+    ]
+    args = list(arrays) + [bounds, ctx, dctx, lse]
+    scratch = [
+        pltpu.VMEM((128, SEQ), bf16),
+        pltpu.VMEM((SEQ, 128), f32),
+        pltpu.VMEM((SEQ, 128), f32),
+        pltpu.VMEM((128, QB), f32),
+    ]
+    if has_prefix:
+        in_specs.append(pl.BlockSpec((1, 2, 32, 128), lambda j, *_: (j, 0, 0, 0)))
+        args.append(pre)
+        scratch.append(pltpu.VMEM((2, 128, 128), f32))
+    return pl.pallas_call(
+        functools.partial(backward_kernel, has_prefix, 0 if has_prefix else 2),
+        grid_spec=pltpu.PrefetchScalarGridSpec(
+            num_scalar_prefetch=1, grid=(4,), in_specs=in_specs, out_specs=out_specs, scratch_shapes=scratch
+        ),
+        out_shape=out_shape,
+        compiler_params=pltpu.CompilerParams(vmem_limit_bytes=40 * 2**20),
+        cost_estimate=pl.CostEstimate(flops=10 * 8 * SEQ * SEQ * 64, bytes_accessed=10 * 2**20, transcendentals=8 * SEQ * SEQ),
+        name="self_backward" if has_prefix else "cross_backward",
+    )(bounds, *args)
+
+
+HIDDEN = 512
+
+
+def feed_kernel(
+    resid2, cot, gain, bias, wco_m, wco_o, fc_in, fin, fc_out, fout, ad, fad,
+    out, grad_two, units, dctx_m, dctx_s,
+    win, wout, down, up, slope, low, hidden, acc, gate, ada, branch_low, sem,
+):
+    bf16 = jnp.bfloat16
+    per = fc_in.shape[1] // HIDDEN
+    steps = 4 * per
+    group = ad.shape[1]
+    loads = []
+    for j in range(steps):
+        piece, part = divmod(j, per)
+        cols = pl.ds(part * HIDDEN, HIDDEN)
+        src = fc_in.at[:, cols] if piece == 0 else fin.at[piece - 1, :, cols]
+        loads.append(pltpu.make_async_copy(src, win.at[j], sem.at[0, j]))
+        src = fc_out.at[cols] if piece == 0 else fout.at[piece - 1, cols]
+        loads.append(pltpu.make_async_copy(src, wout.at[j], sem.at[1, j]))
+    ad_loads = []
+    for piece in range(4):
+        for i, dst in enumerate((down, up)):
+            src = ad.at[i] if piece == 0 else fad.at[piece - 1, i]
+            ad_loads.append(pltpu.make_async_copy(src, dst.at[pl.ds(group * piece, group)], sem.at[2, 2 * piece + i]))
+    for copy in loads + ad_loads:
+        copy.start()
+
+    rows_all = resid2.shape[0]
+    tiles = rows_all // TILE
+    at = lambda t: pl.ds(pl.multiple_of(t * TILE, TILE), TILE)
+
+    def begin(t, _):
+        rows = at(t)
+        normed = norm_forward(resid2[rows, :], gain[1:2, :], bias[1:2, :])
+        hidden[rows, :] = normed
+        low[rows, :] = normed.astype(bf16)
+        return 0
+
+    lax.fori_loop(0, tiles, begin, 0)
+    for copy in ad_loads:
+        copy.wait()
+    pre = nt(low[...], down[...])
+    sigma = jax.nn.sigmoid(pre)
+    gate[...] = sigma * (1.0 + pre * (1.0 - sigma))
+    ada[...] = (pre * sigma).astype(bf16)
+    acc[...] = adapter_scale * nn(ada[...], up[...])
+
+    def ahead(j, _):
+        for i, buf in enumerate((win, wout)):
+            pltpu.make_async_copy(buf.at[j], buf.at[j], sem.at[i, j]).wait()
+        pre = nn(low[...], win[j])
+        phi = 0.5 * (1.0 + lax.erf(pre * 0.7071067811865476))
+        slope[j] = phi + pre * jnp.exp(-0.5 * pre * pre) * 0.3989422804014327
+        acc[...] += nn((pre * phi).astype(bf16), wout[j])
+        return 0
+
+    lax.fori_loop(0, steps, ahead, 0)
+
+    def middle(t, _):
+        rows = at(t)
+        resid = hidden[rows, :] + acc[rows, :]
+        normed, inv = norm_parts(resid)
+        out[rows, :] = (normed * gain[2:3, :] + bias[2:3, :]).astype(bf16)
+        scaled = cot[rows, :].astype(jnp.float32) * gain[2:3, :]
+        grad = inv * (
+            scaled
+            - jnp.mean(scaled, axis=-1, keepdims=True)
+            - normed * jnp.mean(scaled * normed, axis=-1, keepdims=True)
+        )
+        acc[rows, :] = grad
+        branch_low[rows, :] = grad.astype(bf16)
+        return 0
+
+    lax.fori_loop(0, tiles, middle, 0)
+    grelu = (adapter_scale * nt(branch_low[...], up[...]) * gate[...]).astype(bf16)
+    features = low.shape[1]
+    units[:, 0:features] = tn(grelu, low[...])
+    units[:, features : 2 * features] = adapter_scale * tn(ada[...], branch_low[...])
+    acc[...] += nn(grelu, down[...])
+
+    def behind(j, _):
+        grad = (nt(branch_low[...], wout[j]) * slope[j]).astype(bf16)
+        acc[...] += nt(grad, win[j])
+        return 0
+
+    lax.fori_loop(0, steps, behind, 0)
+
+    def finish(t, _):
+        rows = at(t)
+        grad = norm_backward(resid2[rows, :], gain[1:2, :], acc[rows, :])
+        grad_two[rows, :] = grad
+        small = grad.astype(bf16)
+        dctx_m[rows, :] = nt(small, wco_m[...]).astype(bf16)
+        dctx_s[rows, :] = nt(small, wco_o[...]).astype(bf16)
+        return 0
+
+    lax.fori_loop(0, tiles, finish, 0)
+
+
+def feed_call(resid2, cot, gain, bias, wco_m, wco_o, fc_in, fin, fc_out, fout, ad, fad):
+    bf16, f32 = jnp.bfloat16, jnp.float32
+    rows, deep = resid2.shape
+    shape = jax.ShapeDtypeStruct
+    anywhere = pl.BlockSpec(memory_space=pl.ANY)
+    vmem = pl.BlockSpec(memory_space=pltpu.VMEM)
+    steps = 4 * fc_in.shape[1] // HIDDEN
+    units = 4 * ad.shape[1]
+    return pl.pallas_call(
+        feed_kernel,
+        out_shape=[
+            shape((rows, deep), bf16),
+            shape((rows, deep), f32),
+            shape((units, 2 * deep), f32),
+            shape((rows, 512), bf16),
+            shape((rows, 512), bf16),
+        ],
+        in_specs=[vmem] * 6 + [anywhere] * 6,
+        out_specs=[vmem] * 5,
+        scratch_shapes=[
+            pltpu.VMEM((steps, deep, HIDDEN), bf16),
+            pltpu.VMEM((steps, HIDDEN, deep), bf16),
+            pltpu.VMEM((units, deep), bf16),
+            pltpu.VMEM((units, deep), bf16),
+            pltpu.VMEM((steps, rows, HIDDEN), f32),
+            pltpu.VMEM((rows, deep), bf16),
+            pltpu.VMEM((rows, deep), f32),
+            pltpu.VMEM((rows, deep), f32),
+            pltpu.VMEM((rows, units), f32),
+            pltpu.VMEM((rows, units), bf16),
+            pltpu.VMEM((rows, deep), bf16),
+            pltpu.SemaphoreType.DMA((3, 8)),
+        ],
+        compiler_params=pltpu.CompilerParams(vmem_limit_bytes=60 * 2**20),
+        name="feed_forward",
+    )(resid2, cot, gain, bias, wco_m, wco_o, fc_in, fin, fc_out, fout, ad, fad)
+
+
+AXES = ("rows", "heads")
+
+
+def fast_fits(mesh):
+    rows, heads = mesh.shape["rows"], mesh.shape["heads"]
+    return heads == 4 and rows % 4 == 0 and (rows & (rows - 1)) == 0
+
+
+def pairs_of(rows, move):
+    def number(z, c, y, x):
+        return (z * 2 + c) * 4 + y * 2 + x
+
+    found = []
+    for z in range(rows // 2):
+        for c in range(2):
+            for y in range(2):
+                for x in range(2):
+                    found.append((number(z, c, y, x), number(*move(z, c, y, x))))
+    return found
+
+
+class Moves:
+    def __init__(self, rows):
+        def perm(move):
+            table = pairs_of(rows, move)
+            return lambda value: lax.ppermute(value, AXES, table)
+
+        self.core = perm(lambda z, c, y, x: (z, 1 - c, y, x))
+        self.x = perm(lambda z, c, y, x: (z, c, y, 1 - x))
+        self.y = perm(lambda z, c, y, x: (z, c, 1 - y, x))
+        self.d = perm(lambda z, c, y, x: (z, c, 1 - y, 1 - x))
+        crossing = [pair for pair in pairs_of(rows, lambda z, c, y, x: (z, x, y, c)) if pair[0] != pair[1]]
+
+        def swap(value):
+            stays = lax.axis_index("rows") % 2 == lax.axis_index("heads") % 2
+            return jnp.where(stays, value, lax.ppermute(value, AXES, crossing))
+
+        self.swap = swap
+        self.z = []
+        step = 1
+        while step < rows // 2:
+            self.z.append(perm(lambda z, c, y, x, step=step: (z ^ step, c, y, x)))
+            step *= 2
+
+
+def fast_body(
+    rows,
+    tokens,
+    memory,
+    cotangent,
+    dec_seg,
+    mem_seg,
+    w_self,
+    w_self_out,
+    w_cross_q,
+    w_cross_kv,
+    w_cross_out,
+    fc_in,
+    fc_out,
+    ad_down,
+    ad_up,
+    prefix,
+    ln_gain,
+    ln_bias,
+):
+    bf16 = jnp.bfloat16
+    f32 = jnp.float32
+    move = Moves(rows)
+    core = lax.axis_index("rows") % 2
+    count = prefix.shape[1]
+    ad = jnp.stack([ad_down.T, ad_up])
+    held = forward_call(
+        tokens,
+        memory,
+        cotangent,
+        dec_seg.reshape(2, 1, SEQ),
+        mem_seg.reshape(2, 1, MLEN),
+        jnp.pad(prefix, ((0, 0), (0, 32 - count), (0, 0))),
+        w_self,
+        w_self_out,
+        w_cross_q,
+        w_cross_kv,
+        w_cross_out,
+        fc_in,
+        fc_out,
+        ad,
+        ln_gain,
+        ln_bias,
+    )
+    half = tokens.shape[0]
+
+    def own_rows(value):
+        return lax.dynamic_slice_in_dim(value, core * half, half, 0)
+
+    def other_rows(value):
+        return lax.dynamic_slice_in_dim(value, (1 - core) * half, half, 0)
+
+    def whole(mine, others):
+        return jnp.where(
+            core == 0,
+            jnp.concatenate([mine, others], axis=0),
+            jnp.concatenate([others, mine], axis=0),
+        )
+
+    def after(value, *earlier):
+        return lax.optimization_barrier((value,) + earlier)[0]
+
+    out, grad_two, unit_grads, dctx_m, dctx_s = feed_call(
+        held.resid2, held.cot, ln_gain, ln_bias, held.wco_m, held.wco_o,
+        fc_in, held.fin, fc_out, held.fout, ad, held.fad,
+    )
+    output = move.swap(out)
+    units = ad.shape[1] // 2
+    unit_grads = unit_grads.reshape(4, 2, units, -1)
+    unit_mine = lax.dynamic_index_in_dim(unit_grads, core, 1, keepdims=False)
+    unit_other = lax.dynamic_index_in_dim(unit_grads, 1 - core, 1, keepdims=False)
+    unit_mine = unit_mine + move.core(unit_other.astype(bf16)).astype(f32)
+    low_pieces = unit_mine.astype(bf16)
+    unit_sum = (
+        unit_mine[0]
+        + move.x(low_pieces[1]).astype(f32)
+        + move.y(low_pieces[2]).astype(f32)
+        + move.d(low_pieces[3]).astype(f32)
+    )
+
+    cross_dctx = whole(dctx_m, move.core(dctx_s))
+    cross_dctx = after(cross_dctx, unit_sum)
+    cross_dq, cross_dkv = backward_call(
+        False, (held.q, held.kv), held.bounds, held.cctx, cross_dctx, held.clse
+    )
+    got = move.core(other_rows(cross_dq))
+    resid_one = held.resid1
+    grad_one_in = grad_two + dot_right(own_rows(cross_dq), held.wq_m) + dot_right(got, held.wq_o)
+    memory_part = sum(dot_right(cross_dkv[i], held.wkv[i]) for i in range(4))
+    memory_sum = own_rows(memory_part) + move.core(other_rows(memory_part).astype(bf16)).astype(f32)
+    grad_memory = move.swap(memory_sum.astype(bf16)).astype(f32)
+    grad_one = norm_backward(resid_one, ln_gain[0], grad_one_in)
+
+    low_grad_one = grad_one.astype(bf16)
+    d_send = dot_right(low_grad_one, held.wso_o).astype(bf16)
+    self_dctx = whole(dot_right(low_grad_one, held.wso_m).astype(bf16), move.core(d_send))
+    self_dqkv, prefix_blocks = backward_call(
+        True, (held.qkv,), held.bounds, held.sctx, self_dctx, held.slse, held.pre
+    )
+    input_part = sum(dot_right(self_dqkv[i], held.wself[i]) for i in range(4))
+    input_sum = own_rows(input_part) + move.core(other_rows(input_part).astype(bf16)).astype(f32) + grad_one
+    grad_input = move.swap(input_sum.astype(bf16)).astype(f32)
+    unit_sum = after(unit_sum, self_dqkv)
+    for step in move.z:
+        unit_sum = unit_sum + step(unit_sum.astype(bf16)).astype(f32)
+    unit_all = whole(unit_sum, move.core(unit_sum.astype(bf16)).astype(f32))
+    features = tokens.shape[1]
+    down_grad = unit_all[:, :features].T
+    up_grad = unit_all[:, features:]
+
+    prefix_sum = (
+        prefix_blocks[0]
+        + move.x(prefix_blocks[1])
+        + move.y(prefix_blocks[2])
+        + move.d(prefix_blocks[3])
+    )
+    for step in move.z:
+        prefix_sum = prefix_sum + step(prefix_sum)
+    prefix_other = move.core(prefix_sum)
+    prefix_grad = jnp.where(
+        core == 0,
+        jnp.concatenate([prefix_sum, prefix_other], axis=2),
+        jnp.concatenate([prefix_other, prefix_sum], axis=2),
+    )[:, :count]
+    return (output, grad_input, grad_memory, prefix_grad, down_grad, up_grad)
+
+
 def solution(mesh):
     in_specs = (
         P(("rows", "heads"), None),
@@ -463,4 +1474,5 @@
         P(None, "heads"),
         P("heads", None),
     )
-    return jax.shard_map(body, mesh=mesh, in_specs=in_specs, out_specs=out_specs, check_vma=False)
+    chosen = functools.partial(fast_body, mesh.shape["rows"]) if fast_fits(mesh) else body
+    return jax.shard_map(chosen, mesh=mesh, in_specs=in_specs, out_specs=out_specs, check_vma=False)

time: 1460 us -> 420 us (0.29)
  waiting for transfers between devices: 822 us -> 31.6 us
  Pallas kernels: 0 us -> 301 us
  matrix products: 299 us -> 12.1 us
  local copies, waits for them, and re-layouts: 178 us -> 11.9 us
  other arithmetic: 97.1 us -> 15.9 us
  starting transfers between devices: 1.02 us -> 44.9 us
  blocking collectives: 26.4 us -> 0 us
    reduce_scatter x7 -> x0, waiting for transfers between devices: 483 us -> none  [the longest x3 257 us: sum_rows(): lax.psum_scatter(partial_value, 'heads', scatter_dimension=0, tiled=True)]
    all_gather x7 -> x0, waiting for transfers between devices: 337 us -> none  [the longest x3 148 us: gather_rows(): return lax.all_gather(row_share, 'heads', axis=0, tiled=True)]
    pallas_call x0 -> x4, Pallas kernels: none -> 301 us  [the longest x1 196 us: forward_call(): pl.pallas_call(forward_kernel, out_shape=outs, in_specs=[anywhere] * 14 +...]
    dot_general x97 -> x0, matrix products: 260 us -> none  [the longest x8 35.8 us: attend_back(): jnp.einsum('hqk,hqe->hke', token_probs.astype(jnp.bfloat16), context_grad...]
    another operation x29 -> x0, local copies, waits for them, and re-layouts: 48.8 us -> none  [the longest x9 15.5 us: to_heads(): arrays.reshape(arrays.shape[0], arrays.shape[1], heads_here, HD)]
    ppermute x0 -> x21, starting transfers between devices: none -> 44.9 us  [the longest x18 36 us: perm(): return lambda value: lax.ppermute(value, AXES, table)]
    squeeze x25 -> x2, local copies, waits for them, and re-layouts: 33.2 us -> 0.08 us  [the longest x1 0.07 us: fast_body(): low_pieces[1]]
    convert_element_type x20 -> x9, other arithmetic: 40.1 us -> 8.44 us  [the longest x2 3.32 us: fast_body(): grad_input = move.swap(input_sum.astype(bf16)).astype(f32)]
  transfers between devices with their start and end apart: 15 -> 21, of which waited for: 13 -> 5; matrix products, arithmetic and copies ran while one was open for 13% -> 6% of each run, Pallas kernels for 0% -> 15%
where the time goes in v2:
time: 420 us; the launch traced here: 418 us
  Pallas kernels  301 us (72%)
  starting transfers between devices  44.9 us (11%)
  waiting for transfers between devices  31.6 us (8%)
  other arithmetic  15.9 us (4%)
  matrix products  12.1 us (3%)
  local copies, waits for them, and re-layouts  11.9 us (3%)
    pallas_call x1, Pallas kernels, forward_call(): pl.pallas_call(forward_kernel, out_shape=outs, in_specs=[anywhere] * 14 +...  196 us
    pallas_call x2, Pallas kernels, backward_call(): pl.pallas_call(functools.partial(backward_kernel, has_prefix, 0 if has_pr...  62.8 us
    pallas_call x1, Pallas kernels, feed_call(): pl.pallas_call(feed_kernel, out_shape=[shape((rows, deep), bf16), shape((...  41.6 us
    ppermute x18, starting transfers between devices, perm(): return lambda value: lax.ppermute(value, AXES, table)  36 us
    ppermute x18, waiting for transfers between devices, perm(): return lambda value: lax.ppermute(value, AXES, table)  24.1 us
    dot_general x12, matrix products, dot_right(): lax.dot_general(left, right, (((1,), (1,)), ((), ())), preferred_element_...  12.1 us
    ppermute x3, starting transfers between devices, swap(): return jnp.where(stays, value, lax.ppermute(value, AXES, crossing))  8.93 us
  transfers between devices with their start and end apart: 21, of which 5 were waited for; matrix products, arithmetic and copies ran while one was open for 6% of the time, Pallas kernels for 15%

profile of v2, /device:TPU:1, one launch (start us, length us, event | category | flops | bytes accessed | tf_op | source)
XLA Modules:
  0.0 418.1 jit_solution(1020727644330332383)
XLA Ops:
  3.1 1.8 pad_maximum_fusion.ad
  4.9 196.0 %layer_forward.1 = (bf16[4,1024,384]{2,1,0:T(8,128)(2,1)}, bf16[4,1024,384]{2,1,0:T(8,128)(2,1)}, bf16[1024,512]{1,0:T(8,128)(2,1)}, f32[4,8,1024]{2,1,0:T(8,128...) custom-call(bf16[512,1024]{1,0:T(8,128)(2,1)} %tokens.1, ...), custom_call_target="tpu_custom_call" | custom-call | tf_op jit(solution)/shard_map/layer_forward/pallas_call | solution.py:994
  201.0 41.6 %feed_forward.1 = (bf16[512,1024]{1,0:T(8,128)(2,1)}, f32[512,1024]{1,0:T(8,128)}, f32[512,2048]{1,0:T(8,128)}, bf16[512,512]{1,0:T(8,128)(2,1)}, bf16[512,512]{1,0:T(8,128)(2,1)}) custom-call(f32[512,1024]{1,0:T(8,128)} %get-tuple-element.40.resid2, bf16[512,1024]{1,0:T(8,128)(2,1)} %get-tuple-element.41.cot, f32[3,1024]{1,0:T(4,128)} %gain.3, ...), custom_call_target="tpu_custom_call" | custom-call | tf_op jit(solution)/shard_map/feed_forward/pallas_call | solution.py:1247
  242.6 2.9 fusion
  246.0 2.8 collective-permute-start
  249.4 2.1 fusion.53
  254.4 1.6 maximum_select_fusion.refs_4_
  256.0 13.1 %collective-permute-done.5 = bf16[64,2048]{1,0:T(8,128)(2,1)S(1)} collective-permute-done((bf16[64,2048]{1,0:T(8,128)(2,1)S(1)}, bf16[64,2048]{1,0:T(8,128)(2,1)S(1)}, u32[]{:S(2)}, u32[]{:S(2)}) %collective-permute-start.5) | collective-permute-done | bytes 262176 | tf_op jit(solution)/shard_map/ppermute | solution.py:1302
  269.1 2.8 collective-permute-done.3
  272.1 27.9 %cross_backward.1 = (bf16[1024,512]{1,0:T(8,128)(2,1)S(1)}, bf16[4,1024,256]{2,1,0:T(8,128)(2,1)S(1)}) custom-call(s32[8,1024]{1,0:T(8,128)S(1)} %copy-done.8, bf16[1024,512]{1,0:T(8,128)(2,1)S(1)} %copy-done.3, bf16[4,1024,256]{2,1,0:T(8,128)(2,1)S(1)} %copy-done.1, s32[8,1024]{1,0:T(8,128)S(1)} %copy-done.8, bf16[1024,512]{1,0:T(8,128)(2,1)S(1)} %copy-done.4, ...), custom_call_target="tpu_custom_call" | custom-call | flops 5368709120 | bytes 10485760 | tf_op jit(solution)/shard_map/cross_backward/pallas_call | solution.py:1127
  301.6 2.4 collective-permute-start.6
  314.7 34.9 %self_backward.1 = (bf16[4,1024,384]{2,1,0:T(8,128)(2,1)S(1)}, f32[4,2,32,128]{3,2,1,0:T(8,128)S(1)}) custom-call(s32[8,1024]{1,0:T(8,128)S(1)} %copy-done.8, bf16[4,1024,384]{2,1,0:T(8,128)(2,1)S(1)} %copy-done, s32[8,1024]{1,0:T(8,128)S(1)} %copy-done.8, bf16[1024,512]{1,0:T(8,128)(2,1)S(1)} %copy-done.2, ...), custom_call_target="tpu_custom_call" | custom-call | flops 5368709120 | bytes 10485760 | tf_op jit(solution)/shard_map/self_backward/pallas_call | solution.py:1127
  353.6 7.0 %collective-permute-start.13 = (f32[2,32,128]{2,1,0:T(8,128)S(1)}, f32[2,32,128]{2,1,0:T(8,128)S(1)}, u32[]{:S(2)}, u32[]{:S(2)}) collective-permute-start(f32[2,32,128]{2,1,0:T(8,128)S(1)} %get-tuple-element.93), channel_id=1, source_target_pairs={{0,2},{1,3},{2,0},{3,1},{4,6},{5,7},{6,4},{7,5},{8,10},{9,11},{10,... | collective-permute-start | bytes 98312 | tf_op jit(solution)/shard_map/ppermute | solution.py:1302
  362.2 9.6 %collective-permute-start.18 = (bf16[64,2048]{1,0:T(8,128)(2,1)S(1)}, bf16[64,2048]{1,0:T(8,128)(2,1)S(1)}, u32[]{:S(2)}, u32[]{:S(2)}) collective-permute-start(bf16[64,2048]{1,0:T(8,128)(2,1)S(1)} %convert_element_type.92), channel_id=1, source_target_pairs={{0,8},{1,9},{2,10},{3,11},{4,12},{5,13},{6,14},{7,15},{8,0},{9,1},... | collective-permute-start | bytes 786440 | tf_op jit(solution)/shard_map/ppermute | solution.py:1302
  373.1 2.3 collective-permute-start.8
  375.4 2.9 collective-permute-done.15
  378.4 4.6 %collective-permute-start.16 = (f32[2,32,128]{2,1,0:T(8,128)S(1)}, f32[2,32,128]{2,1,0:T(8,128)S(1)}, u32[]{:S(2)}, u32[]{:S(2)}) collective-permute-start(f32[2,32,128]{2,1,0:T(8,128)S(1)} %add.135), channel_id=1, source_target_pairs={{0,16},{1,17},{2,18},{3,19},{4,20},{5,21},{6,22},{7,23},{8,24},{9,... | collective-permute-start | bytes 98312 | tf_op jit(solution)/shard_map/ppermute | solution.py:1302
  384.5 4.0 collective-permute-start.11
  388.5 4.3 %collective-permute-start.17 = (f32[2,32,128]{2,1,0:T(8,128)S(1)}, f32[2,32,128]{2,1,0:T(8,128)S(1)}, u32[]{:S(2)}, u32[]{:S(2)}) collective-permute-start(f32[2,32,128]{2,1,0:T(8,128)S(1)} %add.136), channel_id=1, source_target_pairs={{0,4},{1,5},{2,6},{3,7},{4,0},{5,1},{6,2},{7,3},{8,12},{9,13},{10,... | collective-permute-start | bytes 98312 | tf_op jit(solution)/shard_map/ppermute | solution.py:1302
  392.8 5.2 %collective-permute-done.19 = bf16[64,2048]{1,0:T(8,128)(2,1)S(1)} collective-permute-done((bf16[64,2048]{1,0:T(8,128)(2,1)S(1)}, bf16[64,2048]{1,0:T(8,128)(2,1)S(1)}, u32[]{:S(2)}, u32[]{:S(2)}) %collective-permute-start.19) | collective-permute-done | bytes 262176 | tf_op jit(solution)/shard_map/ppermute | solution.py:1302
  399.2 2.2 collective-permute-start.9
  401.4 2.3 broadcast_select_fusion
  407.9 7.5 %collective-permute-done.9 = bf16[512,1024]{1,0:T(8,128)(2,1)} collective-permute-done((bf16[512,1024]{1,0:T(8,128)(2,1)S(1)}, bf16[512,1024]{1,0:T(8,128)(2,1)}, u32[]{:S(2)}, u32[]{:S(2)}) %collective-permute-start.9) | collective-permute-done | bytes 1048608 | tf_op jit(solution)/shard_map/ppermute | solution.py:1312
  415.4 2.7 select_convert_fusion.1
  (111 shorter events, 32.4 us)
Async XLA Ops:
  245.5 3.9 collective-permute-start.2
  246.0 155.4 %collective-permute-start = (bf16[512,1024]{1,0:T(8,128)(2,1)}, bf16[512,1024]{1,0:T(8,128)(2,1)}, u32[]{:S(2)}, u32[]{:S(2)}) collective-permute-start(bf16[512,1024]{1,0:T(8,128)(2,1)} %get-tuple-element.47), channel_id=1, source_target_pairs={{1,4},{3,6},{4,1},{6,3},{9,12},{11,14},{12,9},{14,11},{17,20},{19,... | collective-permute-start | bytes 3145736 | tf_op jit(solution)/shard_map/ppermute | solution.py:1312
  248.8 5.6 %collective-permute-start.1 = (bf16[512,512]{1,0:T(8,128)(2,1)}, bf16[512,512]{1,0:T(8,128)(2,1)}, u32[]{:S(2)}, u32[]{:S(2)}) collective-permute-start(bf16[512,512]{1,0:T(8,128)(2,1)} %get-tuple-element.57), channel_id=1, source_target_pairs={{0,4},{1,5},{2,6},{3,7},{4,0},{5,1},{6,2},{7,3},{8,12},{9,13},{10,... | collective-permute-start | bytes 1572872 | tf_op jit(solution)/shard_map/ppermute | solution.py:1302
  251.6 20.5 %copy-start.4 = (bf16[1024,512]{1,0:T(8,128)(2,1)S(1)}, bf16[1024,512]{1,0:T(8,128)(2,1)}, u32[]{:S(2)}) copy-start(bf16[1024,512]{1,0:T(8,128)(2,1)} %get-tuple-element.55.refs_3_) | copy-start | bytes 3145732
  251.7 17.4 %collective-permute-start.5 = (bf16[64,2048]{1,0:T(8,128)(2,1)S(1)}, bf16[64,2048]{1,0:T(8,128)(2,1)S(1)}, u32[]{:S(2)}, u32[]{:S(2)}) collective-permute-start(bf16[64,2048]{1,0:T(8,128)(2,1)S(1)} %get-tuple-element.89), channel_id=1, source_target_pairs={{0,3},{1,2},{2,1},{3,0},{4,7},{5,6},{6,5},{7,4},{8,11},{9,10},{10,... | collective-permute-start | bytes 786440 | tf_op jit(solution)/shard_map/ppermute | solution.py:1302
  253.2 15.9 %collective-permute-start.4 = (bf16[64,2048]{1,0:T(8,128)(2,1)S(1)}, bf16[64,2048]{1,0:T(8,128)(2,1)S(1)}, u32[]{:S(2)}, u32[]{:S(2)}) collective-permute-start(bf16[64,2048]{1,0:T(8,128)(2,1)S(1)} %get-tuple-element.90), channel_id=1, source_target_pairs={{0,2},{1,3},{2,0},{3,1},{4,6},{5,7},{6,4},{7,5},{8,10},{9,11},{10,... | collective-permute-start | bytes 786440 | tf_op jit(solution)/shard_map/ppermute | solution.py:1302
  253.9 18.1 %collective-permute-start.3 = (bf16[64,2048]{1,0:T(8,128)(2,1)S(1)}, bf16[64,2048]{1,0:T(8,128)(2,1)S(1)}, u32[]{:S(2)}, u32[]{:S(2)}) collective-permute-start(bf16[64,2048]{1,0:T(8,128)(2,1)S(1)} %get-tuple-element.88), channel_id=1, source_target_pairs={{0,1},{1,0},{2,3},{3,2},{4,5},{5,4},{6,7},{7,6},{8,9},{9,8},{10,11... | collective-permute-start | bytes 786440 | tf_op jit(solution)/shard_map/ppermute | solution.py:1302
  272.1 28.0 %copy-start.11 = (bf16[4,1024,256]{2,1,0:T(8,128)(2,1)S(1)}, bf16[4,1024,256]{2,1,0:T(8,128)(2,1)}, u32[]{:S(2)}) copy-start(bf16[4,1024,256]{2,1,0:T(8,128)(2,1)} %get-tuple-element.71) | copy-start | bytes 6291460
  301.6 3.9 collective-permute-start.6
  309.8 3.5 collective-permute-start.7
  311.4 71.7 %collective-permute-start.10 = (bf16[512,1024]{1,0:T(8,128)(2,1)S(1)}, bf16[512,1024]{1,0:T(8,128)(2,1)S(1)}, u32[]{:S(2)}, u32[]{:S(2)}) collective-permute-start(bf16[512,1024]{1,0:T(8,128)(2,1)S(1)} %dynamic-slice_convert_fusion), channel_id=1, source_target_pairs={{0,4},{1,5},{2,6},{3,7},{4,0},{5,1},{6,2},{7,3},{8,12},{9,13},{10,... | collective-permute-start | bytes 3145736 | tf_op jit(solution)/shard_map/ppermute | solution.py:1302
  314.7 34.9 %copy-start.10 = (bf16[4,1024,384]{2,1,0:T(8,128)(2,1)S(1)}, bf16[4,1024,384]{2,1,0:T(8,128)(2,1)}, u32[]{:S(2)}) copy-start(bf16[4,1024,384]{2,1,0:T(8,128)(2,1)} %get-tuple-element.69) | copy-start | bytes 9437188
  353.4 8.7 %collective-permute-start.14 = (f32[2,32,128]{2,1,0:T(8,128)S(1)}, f32[2,32,128]{2,1,0:T(8,128)S(1)}, u32[]{:S(2)}, u32[]{:S(2)}) collective-permute-start(f32[2,32,128]{2,1,0:T(8,128)S(1)} %get-tuple-element.92), channel_id=1, source_target_pairs={{0,3},{1,2},{2,1},{3,0},{4,7},{5,6},{6,5},{7,4},{8,11},{9,10},{10,... | collective-permute-start | bytes 98312 | tf_op jit(solution)/shard_map/ppermute | solution.py:1302
  353.6 18.2 %collective-permute-start.13 = (f32[2,32,128]{2,1,0:T(8,128)S(1)}, f32[2,32,128]{2,1,0:T(8,128)S(1)}, u32[]{:S(2)}, u32[]{:S(2)}) collective-permute-start(f32[2,32,128]{2,1,0:T(8,128)S(1)} %get-tuple-element.93), channel_id=1, source_target_pairs={{0,2},{1,3},{2,0},{3,1},{4,6},{5,7},{6,4},{7,5},{8,10},{9,11},{10,... | collective-permute-start | bytes 98312 | tf_op jit(solution)/shard_map/ppermute | solution.py:1302
  360.6 11.2 %collective-permute-start.12 = (f32[2,32,128]{2,1,0:T(8,128)S(1)}, f32[2,32,128]{2,1,0:T(8,128)S(1)}, u32[]{:S(2)}, u32[]{:S(2)}) collective-permute-start(f32[2,32,128]{2,1,0:T(8,128)S(1)} %get-tuple-element.91), channel_id=1, source_target_pairs={{0,1},{1,0},{2,3},{3,2},{4,5},{5,4},{6,7},{7,6},{8,9},{9,8},{10,11... | collective-permute-start | bytes 98312 | tf_op jit(solution)/shard_map/ppermute | solution.py:1302
  362.2 20.8 %collective-permute-start.18 = (bf16[64,2048]{1,0:T(8,128)(2,1)S(1)}, bf16[64,2048]{1,0:T(8,128)(2,1)S(1)}, u32[]{:S(2)}, u32[]{:S(2)}) collective-permute-start(bf16[64,2048]{1,0:T(8,128)(2,1)S(1)} %convert_element_type.92), channel_id=1, source_target_pairs={{0,8},{1,9},{2,10},{3,11},{4,12},{5,13},{6,14},{7,15},{8,0},{9,1},... | collective-permute-start | bytes 786440 | tf_op jit(solution)/shard_map/ppermute | solution.py:1302
  371.8 6.6 %collective-permute-start.15 = (f32[2,32,128]{2,1,0:T(8,128)S(1)}, f32[2,32,128]{2,1,0:T(8,128)S(1)}, u32[]{:S(2)}, u32[]{:S(2)}) collective-permute-start(f32[2,32,128]{2,1,0:T(8,128)S(1)} %fusion.49), channel_id=1, source_target_pairs={{0,8},{1,9},{2,10},{3,11},{4,12},{5,13},{6,14},{7,15},{8,0},{9,1},... | collective-permute-start | bytes 98312 | tf_op jit(solution)/shard_map/ppermute | solution.py:1302
  373.1 25.4 %collective-permute-start.8 = (bf16[512,1024]{1,0:T(8,128)(2,1)S(1)}, bf16[512,1024]{1,0:T(8,128)(2,1)S(1)}, u32[]{:S(2)}, u32[]{:S(2)}) collective-permute-start(bf16[512,1024]{1,0:T(8,128)(2,1)S(1)} %dynamic-slice_convert_fusion.1), channel_id=1, source_target_pairs={{0,4},{1,5},{2,6},{3,7},{4,0},{5,1},{6,2},{7,3},{8,12},{9,13},{10,... | collective-permute-start | bytes 3145736 | tf_op jit(solution)/shard_map/ppermute | solution.py:1302
  378.4 10.1 %collective-permute-start.16 = (f32[2,32,128]{2,1,0:T(8,128)S(1)}, f32[2,32,128]{2,1,0:T(8,128)S(1)}, u32[]{:S(2)}, u32[]{:S(2)}) collective-permute-start(f32[2,32,128]{2,1,0:T(8,128)S(1)} %add.135), channel_id=1, source_target_pairs={{0,16},{1,17},{2,18},{3,19},{4,20},{5,21},{6,22},{7,23},{8,24},{9,... | collective-permute-start | bytes 98312 | tf_op jit(solution)/shard_map/ppermute | solution.py:1302
  383.0 14.9 %collective-permute-start.19 = (bf16[64,2048]{1,0:T(8,128)(2,1)S(1)}, bf16[64,2048]{1,0:T(8,128)(2,1)S(1)}, u32[]{:S(2)}, u32[]{:S(2)}) collective-permute-start(bf16[64,2048]{1,0:T(8,128)(2,1)S(1)} %fusion.46), channel_id=1, source_target_pairs={{0,16},{1,17},{2,18},{3,19},{4,20},{5,21},{6,22},{7,23},{8,24},{9,... | collective-permute-start | bytes 786440 | tf_op jit(solution)/shard_map/ppermute | solution.py:1302
  384.5 22.0 %collective-permute-start.11 = (bf16[512,1024]{1,0:T(8,128)(2,1)}, bf16[512,1024]{1,0:T(8,128)(2,1)S(1)}, u32[]{:S(2)}, u32[]{:S(2)}) collective-permute-start(bf16[512,1024]{1,0:T(8,128)(2,1)} %add_convert_fusion), channel_id=1, source_target_pairs={{1,4},{3,6},{4,1},{6,3},{9,12},{11,14},{12,9},{14,11},{17,20},{19,... | collective-permute-start | bytes 3145736 | tf_op jit(solution)/shard_map/ppermute | solution.py:1312
  388.5 15.3 %collective-permute-start.17 = (f32[2,32,128]{2,1,0:T(8,128)S(1)}, f32[2,32,128]{2,1,0:T(8,128)S(1)}, u32[]{:S(2)}, u32[]{:S(2)}) collective-permute-start(f32[2,32,128]{2,1,0:T(8,128)S(1)} %add.136), channel_id=1, source_target_pairs={{0,4},{1,5},{2,6},{3,7},{4,0},{5,1},{6,2},{7,3},{8,12},{9,13},{10,... | collective-permute-start | bytes 98312 | tf_op jit(solution)/shard_map/ppermute | solution.py:1302
  398.1 6.4 %collective-permute-start.20 = (bf16[64,2048]{1,0:T(8,128)(2,1)S(1)}, bf16[64,2048]{1,0:T(8,128)(2,1)S(1)}, u32[]{:S(2)}, u32[]{:S(2)}) collective-permute-start(bf16[64,2048]{1,0:T(8,128)(2,1)S(1)} %get-tuple-element.82), channel_id=1, source_target_pairs={{0,4},{1,5},{2,6},{3,7},{4,0},{5,1},{6,2},{7,3},{8,12},{9,13},{10,... | collective-permute-start | bytes 786440 | tf_op jit(solution)/shard_map/ppermute | solution.py:1302
  399.2 16.2 %collective-permute-start.9 = (bf16[512,1024]{1,0:T(8,128)(2,1)S(1)}, bf16[512,1024]{1,0:T(8,128)(2,1)}, u32[]{:S(2)}, u32[]{:S(2)}) collective-permute-start(bf16[512,1024]{1,0:T(8,128)(2,1)S(1)} %add_convert_fusion.1), channel_id=1, source_target_pairs={{1,4},{3,6},{4,1},{6,3},{9,12},{11,14},{12,9},{14,11},{17,20},{19,... | collective-permute-start | bytes 3145736 | tf_op jit(solution)/shard_map/ppermute | solution.py:1312
  (17 other events, 115.5 us)

commit v3 on v2

--- a/solution.py
+++ b/solution.py
@@ -473,15 +473,41 @@
 MESH = pl.DeviceIdType.MESH
 TILE = 256
 
-TOK, TOK_C, MEM, MEM_C, COT, SEG, MSEG, SO_C, CO_C, CQ_C, Q_C = range(11)
-A_X, A_Y, A_D = 11, 15, 19
-R_X, R_Y, R_D = 23, 25, 27
-C_X, C_Y, C_D = 29, 32, 35
-SELF_CTX, CROSS_CTX = 38, 42
-FEED_I, FEED_O, FEED_A = 46, 53, 60
-SLOTS = 67
-OWN, KEEP = 7, 24
-LOCAL_SLOTS = 44
+TOK, TOK_C, MEM, MEM_C = 112, 113, 114, 115
+SELF_PIECE, OUT_ONE, CROSS_Q, CROSS_PIECE, OUT_TWO = 128, 132, 133, 134, 138
+SLOTS, LOCAL_SLOTS = 128, 48
+GROUPS = ((1, 0), (1, 0), (1, 0), (0, 1), (1, 1), (0, 0), (1, 0))
+SCHEDULE = (16, 17, 65, 64, 20, 33, 32, 68, 97, 112, 35, 67, 36, 19, 114, 113, 18, 100, 49, 128, 0, 115, 21, 1, 22, 96, 3, 2, 4, 129, 48, 34, 98, 5, 130, 80, 37, 131, 81, 99, 38, 132, 133, 101, 134, 66, 50, 82, 135, 69, 102, 136, 70, 137, 86, 138)
+
+
+class Place:
+    def __init__(self):
+        self.row, self.head = lax.axis_index("rows"), lax.axis_index("heads")
+        self.c, self.z = lax.rem(self.row, 2), lax.div(self.row, 2)
+        self.x, self.y = lax.rem(self.head, 2), lax.div(self.head, 2)
+        self.odd = lax.rem(self.z, 2)
+        c, x, y, z = self.c, self.x, self.y, self.z
+        self.to_x = (self.row, 2 * y + 1 - x)
+        self.to_y = (self.row, 2 * (1 - y) + x)
+        self.to_d = (self.row, 2 * (1 - y) + 1 - x)
+        self.to_z = (2 * (z + 1 - 2 * self.odd) + c, self.head)
+        self.to_c = (2 * z + 1 - c, self.head)
+        self.to_s = (2 * z + x, 2 * y + c)
+
+    def greet(self, devices, swaps):
+        barrier = pltpu.get_barrier_semaphore()
+        for device in devices:
+            pl.semaphore_signal(barrier, inc=1, device_id=device, device_id_type=MESH)
+        count = len(devices)
+        if swaps:
+            moves = self.c != self.x
+
+            @pl.when(moves)
+            def _():
+                pl.semaphore_signal(barrier, inc=1, device_id=self.to_s, device_id_type=MESH)
+
+            count = count + moves.astype(jnp.int32)
+        pl.semaphore_wait(barrier, count)
 
 
 def prefix_block(rows):
@@ -515,404 +541,400 @@
 
 
 def forward_kernel(
-    tokens, memory, cotangent, seg, mseg, prefix, w_self, w_so, w_cq, w_ckv, w_co, fc_in, fc_out, ad, gain, bias,
+    tokens, memory, seg, mseg, prefix, w_self, w_so, w_cq, w_ckv, w_co, fc_in, fc_out, ad, gain, bias,
     o_wself, o_qkv, o_sctx, o_slse, o_pre, o_wso_m, o_wso_o, o_wkv, o_wq_m, o_wq_o, o_wco_m, o_wco_o,
-    o_q, o_kv, o_cctx, o_clse, o_resid1, o_resid2, o_bounds, o_tok, o_cot, fin, fout, fad,
+    o_q, o_kv, o_cctx, o_clse, o_resid1, o_resid2, o_bounds, fin, fout, fad,
     wself, qkv, sctx, slse, pre, wso_m, wso_o, wkv, wq_m, wq_o, wco_m, wco_o,
     q_all, kv, cctx, clse, resid1, resid2, bounds, tok, mem, sctx_o, cctx_o, q_send, hidden, low_one, vt, seg_v, mseg_v,
     send, recv, local,
 ):
-    row = lax.axis_index("rows")
-    head = lax.axis_index("heads")
-    c, z = lax.rem(row, 2), lax.div(row, 2)
-    x, y = lax.rem(head, 2), lax.div(head, 2)
-    odd = lax.rem(z, 2)
-    to_x = (row, 2 * y + 1 - x)
-    to_y = (row, 2 * (1 - y) + x)
-    to_d = (row, 2 * (1 - y) + 1 - x)
-    to_z = (2 * (z + 1 - 2 * odd) + c, head)
-    to_c = (2 * z + 1 - c, head)
-    to_s = (2 * z + x, 2 * y + c)
-    stays = c == x
-    moves = c != x
-
-    barrier = pltpu.get_barrier_semaphore()
-    for device in (to_x, to_y, to_d, to_z, to_c):
-        pl.semaphore_signal(barrier, inc=1, device_id=device, device_id_type=MESH)
-
-    @pl.when(moves)
-    def _():
-        pl.semaphore_signal(barrier, inc=1, device_id=to_s, device_id_type=MESH)
-
-    pl.semaphore_wait(barrier, 5 + moves.astype(jnp.int32))
-
-    def there(slot, src, dst, device):
+    place_of = Place()
+    c, x, y, odd = place_of.c, place_of.x, place_of.y, place_of.odd
+    to_x, to_y, to_z, to_c, to_s = place_of.to_x, place_of.to_y, place_of.to_z, place_of.to_c, place_of.to_s
+    stays, moves = c == x, c != x
+    place_of.greet((to_x, to_y, to_z, to_c), True)
+
+    taken = []
+
+    def there(src, dst, device):
+        slot = len(taken)
+        taken.append(slot)
         return pltpu.make_async_remote_copy(
             src_ref=src, dst_ref=dst, send_sem=send.at[slot], recv_sem=recv.at[slot], device_id=device, device_id_type=MESH
         )
 
-    def here(slot, src, dst):
+    used = []
+
+    def here(src, dst):
+        slot = len(used)
+        used.append(slot)
         return pltpu.make_async_copy(src, dst, local.at[slot])
 
+    deep = w_self.shape[1]
     half = tok.shape[0] // 2
-    mine = pl.ds(pl.multiple_of(c * half, half), half)
-    others = pl.ds(pl.multiple_of((1 - c) * half, half), half)
-    partner_rows = pl.ds(pl.multiple_of(x * half, half), half)
-    lanes = pl.ds(pl.multiple_of(c * 128, 128), 128)
-    other_lanes = pl.ds(pl.multiple_of((1 - c) * 128, 128), 128)
-
-    pending = []
-
-    def go(copy):
-        copy.start()
-        pending.append(copy)
-        return copy
-
-    def swap_start(slot, src, target, dst_there, dst_here):
-        pl.when(moves)(lambda: there(slot, src, target.at[dst_there], to_s).start())
-        pl.when(stays)(lambda: here(slot, src, target.at[dst_here]).start())
-
-    def swap_wait(slot, src, target, dst_here):
-        pl.when(moves)(lambda: there(slot, src, target.at[dst_here], to_s).wait())
-        pl.when(stays)(lambda: here(slot, src, target.at[dst_here]).wait())
-
-    def seg_start(slot, src, dst):
-        @pl.when(stays)
-        def _():
-            here(slot, src.at[y], dst).start()
-            there(slot, src.at[y], dst, to_c).start()
-
-    def seg_wait(slot, src, dst):
-        @pl.when(stays)
-        def _():
-            here(slot, src.at[y], dst).wait()
-            there(slot, src.at[y], dst, to_c).wait_send()
-
-        pl.when(moves)(lambda: there(slot, src.at[y], dst, to_c).wait_recv())
-
-    swap_start(TOK, tokens, tok, partner_rows, mine)
-    own_a = [here(OWN + i, w_self.at[i, :, lanes], wself.at[0, :, pl.ds(128 * i, 128)]) for i in range(3)]
-    own_a.append(here(OWN + 3, prefix.at[:, :, lanes], pre.at[0]))
-    for copy in own_a:
-        copy.start()
-
-    def send_a(base, piece, device):
-        out = [
-            there(base + i, w_self.at[i, :, lanes], wself.at[piece, :, pl.ds(128 * i, 128)], device) for i in range(3)
-        ]
-        return out + [there(base + 3, prefix.at[:, :, lanes], pre.at[piece], device)]
-
-    ax, ay = send_a(A_X, 1, to_x), send_a(A_Y, 2, to_y)
-    for copy in ax + ay:
-        go(copy)
-    ad_ = [there(A_D + i, wself.at[1, :, pl.ds(128 * i, 128)], wself.at[3, :, pl.ds(128 * i, 128)], to_y) for i in range(3)]
-    ad_.append(there(A_D + 3, pre.at[1], pre.at[3], to_y))
-
-    seg_start(SEG, seg, seg_v)
-    seg_start(MSEG, mseg, mseg_v)
-    rows_c = pl.ds(pl.multiple_of(c * 128, 128), 128)
-    rows_o = pl.ds(pl.multiple_of((1 - c) * 128, 128), 128)
-    own_b = [
-        here(OWN + 4, w_so.at[rows_c], wso_m.at[pl.ds(0, 128)]),
-        here(OWN + 5, w_so.at[rows_o], wso_o.at[pl.ds(0, 128)]),
-        here(OWN + 6, w_co.at[rows_c], wco_m.at[pl.ds(0, 128)]),
-        here(OWN + 7, w_co.at[rows_o], wco_o.at[pl.ds(0, 128)]),
-        here(OWN + 8, w_cq.at[:, lanes], wq_m.at[:, pl.ds(0, 128)]),
-        here(OWN + 9, w_cq.at[:, other_lanes], wq_o.at[:, pl.ds(0, 128)]),
-        here(OWN + 10, w_ckv.at[0, :, lanes], wkv.at[0, :, pl.ds(0, 128)]),
-        here(OWN + 11, w_ckv.at[1, :, lanes], wkv.at[0, :, pl.ds(128, 128)]),
-    ]
-    for copy in own_b:
-        copy.start()
-
-    def send_r(base, piece, device):
-        place = pl.ds(128 * piece, 128)
-        return [
-            there(base, w_so.at[rows_c], wso_m.at[place], device),
-            there(base + 1, w_co.at[rows_c], wco_m.at[place], device),
-        ]
-
-    rx, ry, rd = send_r(R_X, 1, to_x), send_r(R_Y, 2, to_y), send_r(R_D, 3, to_d)
-
-    def send_c(base, piece, device):
-        return [
-            there(base, w_cq.at[:, lanes], wq_m.at[:, pl.ds(128 * piece, 128)], device),
-            there(base + 1, w_ckv.at[0, :, lanes], wkv.at[piece, :, pl.ds(0, 128)], device),
-            there(base + 2, w_ckv.at[1, :, lanes], wkv.at[piece, :, pl.ds(128, 128)], device),
-        ]
-
-    cx, cy = send_c(C_X, 1, to_x), send_c(C_Y, 2, to_y)
-    cd = [
-        there(C_D, wq_m.at[:, pl.ds(128, 128)], wq_m.at[:, pl.ds(384, 128)], to_y),
-        there(C_D + 1, wkv.at[1, :, pl.ds(0, 128)], wkv.at[3, :, pl.ds(0, 128)], to_y),
-        there(C_D + 2, wkv.at[1, :, pl.ds(128, 128)], wkv.at[3, :, pl.ds(128, 128)], to_y),
-    ]
-
+    step = lambda start, size, unit: pl.ds(pl.multiple_of(start, unit), size)
+    mine = step(c * half, half, half)
+    others = step((1 - c) * half, half, half)
+    lanes = step(c * 128, 128, 128)
+    other_lanes = step((1 - c) * 128, 128, 128)
+    rows_c, rows_o = lanes, other_lanes
+    foreign = pl.ds(128, 384)
     hid = fc_in.shape[1]
     units = ad.shape[1]
-    at_cols = lambda start, size: (slice(None), pl.ds(pl.multiple_of(start, 256), size))
-    at_rows = lambda start, size: (pl.ds(pl.multiple_of(start, 256), size), slice(None))
-    at_units = lambda start, size: (slice(None), pl.ds(pl.multiple_of(start, 32), size), slice(None))
-    def part(ref, lead, index):
-        return ref.at[index] if lead is None else ref.at[(lead,) + index]
-
-    class Feed:
-        def __init__(self, base, src, dst, size, at, through_x):
-            quarter = at(c * (size // 2) + odd * (size // 4), size // 4)
-            half_of = (slice(None),) + at(c * (size // 2), size // 2)
-            self.x = there(base, part(src, None, quarter), part(dst, 0, quarter), to_x)
-            self.y = there(base + 1, part(src, None, quarter), part(dst, 1, quarter), to_y)
-            if through_x:
-                self.d = there(base + 2, part(dst, 1, quarter), part(dst, 2, quarter), to_x)
-            else:
-                self.d = there(base + 2, part(dst, 0, quarter), part(dst, 2, quarter), to_y)
-            self.zx, self.zy, self.zd = [
-                there(base + 3 + i, part(dst, i, quarter), part(dst, i, quarter), to_z) for i in range(3)
-            ]
-            self.c = there(base + 6, dst.at[half_of], dst.at[half_of], to_c)
-
-    fi = Feed(FEED_I, fc_in, fin, hid, at_cols, True)
-    fo = Feed(FEED_O, fc_out, fout, hid, at_rows, False)
-    fa = Feed(FEED_A, ad, fad, units, at_units, False)
-
-    swap_wait(TOK, tokens, tok, mine)
-    tok_c = go(there(TOK_C, tok.at[mine], tok.at[mine], to_c))
+    pending = []
+
+    def swap_of(src, target):
+        away = there(src, target.at[step(x * half, half, half)], to_s)
+        home = here(src, target.at[mine])
+        back = there(target.at[mine], target.at[mine], to_c)
+
+        def start():
+            pl.when(moves)(away.start)
+            pl.when(stays)(home.start)
+
+        def wait():
+            pl.when(moves)(away.wait)
+            pl.when(stays)(home.wait)
+
+        return start, wait, back
+
+    def seg_of(src, dst):
+        home = here(src.at[y], dst)
+        away = there(src.at[y], dst, to_c)
+
+        def start():
+            pl.when(stays)(home.start)
+            pl.when(stays)(away.start)
+
+        def wait():
+            pl.when(stays)(home.wait)
+            pl.when(stays)(away.wait_send)
+            pl.when(moves)(away.wait_recv)
+
+        return start, wait
+
+    def deep_rows(shared):
+        return step(odd * (deep // 2), deep // 2, deep // 2) if shared else pl.ds(0, deep)
+
+    def thin_rows(piece, shared):
+        return step(128 * piece + odd * 64, 64, 64) if shared else pl.ds(128 * piece, 128)
+
+    def thin_own(shared):
+        return step(128 * c + odd * 64, 64, 64) if shared else rows_c
+
+    def span(size, shared):
+        return step(c * (size // 2) + odd * (size // 4), size // 4, size // 4) if shared else step(c * (size // 2), size // 2, size // 2)
+
+    lane_of = lambda i: pl.ds(128 * i, 128)
+
+    def group_a(shared):
+        rows = deep_rows(shared)
+        first = lambda piece: [(w_self.at[i, rows, lanes], wself.at[piece, rows, lane_of(i)]) for i in range(3)] + [
+            (prefix.at[:, :, lanes], pre.at[piece])
+        ]
+        return first, lambda piece: [wself.at[piece, rows], pre.at[piece]], 1, []
+
+    def group_thin(src, dst_m, dst_o, shared):
+        first = lambda piece: [(src.at[thin_own(shared)], dst_m.at[thin_rows(piece, shared)])]
+        return first, lambda piece: [dst_m.at[thin_rows(piece, shared)]], 1, [(dst_m.at[foreign], dst_o.at[foreign])]
+
+    def group_q(shared):
+        rows = deep_rows(shared)
+        first = lambda piece: [(w_cq.at[rows, lanes], wq_m.at[rows, lane_of(piece)])]
+        return first, lambda piece: [wq_m.at[rows, lane_of(piece)]], 1, [(wq_m.at[:, foreign], wq_o.at[:, foreign])]
+
+    def group_v(shared):
+        rows = deep_rows(shared)
+        first = lambda piece: [(w_ckv.at[i, rows, lanes], wkv.at[piece, rows, lane_of(i)]) for i in range(2)]
+        return first, lambda piece: [wkv.at[piece, rows]], 1, []
+
+    def group_i(shared):
+        cols = span(hid, shared)
+        both = fin.at[:, :, span(hid, False)]
+        first = lambda piece: [(fc_in.at[:, cols], fin.at[piece - 1, :, cols])]
+        return first, lambda piece: [fin.at[piece - 1, :, cols]], 1, [(both, both)]
+
+    def group_o(shared):
+        rows, some = span(hid, shared), span(units, shared)
+        both, both_units = fout.at[:, span(hid, False)], fad.at[:, :, span(units, False)]
+        first = lambda piece: [(fc_out.at[rows], fout.at[piece - 1, rows]), (ad.at[:, some], fad.at[piece - 1, :, some])]
+        hold = lambda piece: [fout.at[piece - 1, rows], fad.at[piece - 1, :, some]]
+        return first, hold, 2, [(both, both), (both_units, both_units)]
+
+    makers = [
+        group_a,
+        functools.partial(group_thin, w_so, wso_m, wso_o),
+        group_q,
+        group_v,
+        functools.partial(group_thin, w_co, wco_m, wco_o),
+        group_i,
+        group_o,
+    ]
+    copies, needs = {}, {}
+    for index, (make, (shared, through_x)) in enumerate(zip(makers, GROUPS)):
+        first, hold, shared_count, cross = make(bool(shared))
+        base = 16 * index
+        copies[base] = [there(src, dst, to_x) for src, dst in first(1)]
+        copies[base + 1] = [there(src, dst, to_y) for src, dst in first(2)]
+        near, device = (2, to_x) if through_x else (1, to_y)
+        copies[base + 2] = [there(src, dst, device) for src, dst in zip(hold(near), hold(3))]
+        needs[base], needs[base + 1], needs[base + 2] = [], [], [base + near - 1]
+        arrived = [base, base + 1, base + 2]
+        if shared:
+            for i in range(3):
+                copies[base + 3 + i] = [there(ref, ref, to_z) for ref in hold(i + 1)[:shared_count]]
+                needs[base + 3 + i] = [base + i]
+                arrived.append(base + 3 + i)
+        if cross:
+            copies[base + 6] = [there(src, dst, to_c) for src, dst in cross]
+            needs[base + 6] = arrived
+    tok_start, tok_wait, tok_back = swap_of(tokens, tok)
+    mem_start, mem_wait, mem_back = swap_of(memory, mem)
+    copies[TOK_C], copies[MEM_C] = [tok_back], [mem_back]
+    needs[TOK_C], needs[MEM_C] = [TOK], [MEM]
+    seg_start, seg_wait = seg_of(seg, seg_v)
+    mseg_start, mseg_wait = seg_of(mseg, mseg_v)
+    sctx_out = [there(sctx.at[others, lane_of(i)], sctx_o.at[:, lane_of(i)], to_c) for i in range(4)]
+    cctx_out = [there(cctx.at[others, lane_of(i)], cctx_o.at[:, lane_of(i)], to_c) for i in range(4)]
+    q_out = there(q_send, q_all.at[mine], to_c)
+
+    landed = set()
+
+    def wait_for(op):
+        if op in landed:
+            return
+        landed.add(op)
+        if op == TOK:
+            tok_wait()
+        elif op == MEM:
+            mem_wait()
+        elif op in copies:
+            for copy in copies[op]:
+                copy.wait_recv()
+
+    def launch(op):
+        if op == TOK:
+            tok_start()
+        elif op == MEM:
+            mem_start()
+        else:
+            for need in needs[op]:
+                wait_for(need)
+            for copy in copies[op]:
+                copy.start()
+                pending.append(copy)
+
     saves = []
 
     def keep(src, dst):
-        copy = here(KEEP + len(saves), src, dst)
+        copy = here(src, dst)
         copy.start()
         saves.append(copy)
 
-    keep(tok.at[mine], o_tok)
-    seg_wait(SEG, seg, seg_v)
-    seg_wait(MSEG, mseg, mseg_v)
-    dec, men = seg_v[...], mseg_v[...]
-
-    def below(values, d):
-        return jnp.sum((values < d).astype(jnp.int32), axis=1, keepdims=True)
-
-    def pick(counts):
-        out = jnp.broadcast_to(counts[0], dec.shape)
-        for d in range(1, 4):
-            out = jnp.where(dec == d, counts[d], out)
-        return out
-
-    zero = jnp.zeros((1, 1), jnp.int32)
-    full = jnp.full((1, 1), MLEN, jnp.int32)
-    self_lo = pick([zero] + [below(dec, d) for d in range(1, 4)])
-    mem_counts = [zero] + [below(men, d) for d in range(1, 4)] + [full]
-    bounds[...] = jnp.concatenate(
-        [self_lo, lax.broadcasted_iota(jnp.int32, dec.shape, 1), pick(mem_counts[:4]), pick(mem_counts[1:]) - 1]
-        + [jnp.zeros_like(dec)] * 4,
-        axis=0,
-    )
-    keep(bounds, o_bounds)
-    for copy in own_a:
-        copy.wait()
-    tok_c.wait_recv()
-
-    def first_piece(p, _):
-        @pl.when(p == 1)
-        def _():
-            for copy in ax:
-                copy.wait_recv()
-            for copy in ad_ + rx + rd:
-                copy.start()
-            swap_start(MEM, memory, mem, partner_rows, mine)
-            for copy in cx:
-                copy.start()
-
-        @pl.when(p == 2)
-        def _():
-            for copy in ay:
-                copy.wait_recv()
-            for copy in ry + [fi.y, fi.x] + cy:
-                copy.start()
-
-        @pl.when(p == 3)
-        def _():
-            for copy in ad_:
-                copy.wait_recv()
-
+    own_a = [here(w_self.at[i, :, lanes], wself.at[0, :, lane_of(i)]) for i in range(3)]
+    own_a.append(here(prefix.at[:, :, lanes], pre.at[0]))
+    own_b = [
+        here(w_so.at[rows_c], wso_m.at[lane_of(0)]),
+        here(w_so.at[rows_o], wso_o.at[lane_of(0)]),
+        here(w_co.at[rows_c], wco_m.at[lane_of(0)]),
+        here(w_co.at[rows_o], wco_o.at[lane_of(0)]),
+        here(w_cq.at[:, lanes], wq_m.at[:, lane_of(0)]),
+        here(w_cq.at[:, other_lanes], wq_o.at[:, lane_of(0)]),
+        here(w_ckv.at[0, :, lanes], wkv.at[0, :, lane_of(0)]),
+        here(w_ckv.at[1, :, lanes], wkv.at[0, :, lane_of(1)]),
+    ]
+
+    def bounds_of():
+        seg_wait()
+        mseg_wait()
+        dec, men = seg_v[...], mseg_v[...]
+
+        def below(values, d):
+            return jnp.sum((values < d).astype(jnp.int32), axis=1, keepdims=True)
+
+        def pick(counts):
+            out = jnp.broadcast_to(counts[0], dec.shape)
+            for d in range(1, 4):
+                out = jnp.where(dec == d, counts[d], out)
+            return out
+
+        zero = jnp.zeros((1, 1), jnp.int32)
+        full = jnp.full((1, 1), MLEN, jnp.int32)
+        self_lo = pick([zero] + [below(dec, d) for d in range(1, 4)])
+        mem_counts = [zero] + [below(men, d) for d in range(1, 4)] + [full]
+        bounds[...] = jnp.concatenate(
+            [self_lo, lax.broadcasted_iota(jnp.int32, dec.shape, 1), pick(mem_counts[:4]), pick(mem_counts[1:]) - 1]
+            + [jnp.zeros_like(dec)] * 4,
+            axis=0,
+        )
+        keep(bounds, o_bounds)
+
+    def weight_needs(base, piece):
+        found = [base + piece - 1, base + 2 + piece]
+        return [op for op in found if op in copies]
+
+    def project(dst, p, source, weight):
         def rows_of(t, _):
-            rows = pl.ds(pl.multiple_of(t * TILE, TILE), TILE)
-            qkv[p, rows, :] = nn(tok[rows, :], wself[p]).astype(jnp.bfloat16)
+            rows = step(t * TILE, TILE, TILE)
+            dst[p, rows, :] = nn(source[rows, :], weight[p]).astype(jnp.bfloat16)
             return 0
 
         lax.fori_loop(0, SEQ // TILE, rows_of, 0)
+
+    def self_piece(p):
+        project(qkv, p, tok, wself)
         vt[...] = qkv[p, :, 256:384].astype(jnp.float32).T.astype(jnp.bfloat16)
         kp = prefix_block(pre[p, 0])
         vpt = prefix_block(pre[p, 1]).astype(jnp.float32).T.astype(jnp.bfloat16)
-        place = pl.ds(pl.multiple_of(p * 128, 128), 128)
+        place = step(p * 128, 128, 128)
         for qi in range(SEQ // QB):
             width = (qi + 1) * QB
-            span = slice(qi * QB, (qi + 1) * QB)
+            rows = slice(qi * QB, (qi + 1) * QB)
             pos = lax.broadcasted_iota(jnp.int32, (width, QB), 0)
-            mask = (pos >= bounds[0:1, span]) & (pos <= bounds[1:2, span])
-            out, lse = attend_tile(qkv[p, span, 0:128], qkv[p, 0:width, 128:256], vt[:, 0:width], mask, kp, vpt)
-            sctx[span, place] = out
+            mask = (pos >= bounds[0:1, rows]) & (pos <= bounds[1:2, rows])
+            out, lse = attend_tile(qkv[p, rows, 0:128], qkv[p, 0:width, 128:256], vt[:, 0:width], mask, kp, vpt)
+            sctx[rows, place] = out
             for h in range(2):
-                slse[p, h : h + 1, span] = lse[h]
-        there(SELF_CTX + p, sctx.at[others, place], sctx_o.at[:, place], to_c).start()
-        return 0
-
-    lax.fori_loop(0, 4, first_piece, 0)
-    pending.extend(ad_ + rx + rd + cx + ry + cy + [fi.x, fi.y])
-    for i in range(4):
-        copy = there(SELF_CTX + i, sctx.at[others, pl.ds(128 * i, 128)], sctx_o.at[:, pl.ds(128 * i, 128)], to_c)
-        pending.append(copy)
-    sctx_in = pending[-4:]
-    keep(qkv, o_qkv)
-    keep(wself, o_wself)
-    keep(sctx, o_sctx)
-    keep(slse, o_slse)
-    keep(pre, o_pre)
-
-    for copy in rx + ry + rd:
-        copy.wait_recv()
-    for copy in own_b:
-        copy.wait()
-    foreign = pl.ds(128, 384)
-    so_c = go(there(SO_C, wso_m.at[foreign], wso_o.at[foreign], to_c))
-    co_c = go(there(CO_C, wco_m.at[foreign], wco_o.at[foreign], to_c))
-    fi.y.wait_recv()
-    go(fi.d)
-    go(fi.zy)
-    for copy in sctx_in + [so_c]:
-        copy.wait_recv()
-    keep(wso_m, o_wso_m)
-    keep(wso_o, o_wso_o)
-
-    def out_rows(t, resid_before, ctx_m, ctx_o, w_m, w_o):
-        rows = pl.ds(pl.multiple_of(t * TILE, TILE), TILE)
-        rows_all = pl.ds(pl.multiple_of(c * half + t * TILE, TILE), TILE)
-        return rows, rows_all, resid_before + nn(ctx_m[rows_all, :], w_m[...]) + nn(ctx_o[rows, :], w_o[...])
+                slse[p, h : h + 1, rows] = lse[h]
+
+    def cross_piece(p):
+        project(kv, p, mem, wkv)
+        vt[...] = kv[p, :, 128:256].astype(jnp.float32).T.astype(jnp.bfloat16)
+        place = step(p * 128, 128, 128)
+
+        def block(qi, _):
+            rows = step(qi * QB, QB, QB)
+            pos = lax.broadcasted_iota(jnp.int32, (MLEN, QB), 0)
+            mask = (pos >= bounds[2:3, rows]) & (pos <= bounds[3:4, rows])
+            out, lse = attend_tile(q_all[rows, place], kv[p, :, 0:128], vt[...], mask, None, None)
+            cctx[rows, place] = out
+            for h in range(2):
+                clse[p, h : h + 1, rows] = lse[h]
+            return 0
+
+        lax.fori_loop(0, SEQ // QB, block, 0)
+
+    def with_out(t, resid_before, ctx_m, ctx_o, w_m, w_o):
+        rows = step(t * TILE, TILE, TILE)
+        rows_all = step(c * half + t * TILE, TILE, TILE)
+        return resid_before + nn(ctx_m[rows_all, :], w_m[...]) + nn(ctx_o[rows, :], w_o[...])
 
     def out_one(t, _):
-        rows_all = pl.ds(pl.multiple_of(c * half + t * TILE, TILE), TILE)
-        rows, _, resid = out_rows(t, tok[rows_all, :].astype(jnp.float32), sctx, sctx_o, wso_m, wso_o)
+        rows = step(t * TILE, TILE, TILE)
+        rows_all = step(c * half + t * TILE, TILE, TILE)
+        resid = with_out(t, tok[rows_all, :].astype(jnp.float32), sctx, sctx_o, wso_m, wso_o)
         resid1[rows, :] = resid
         normed = norm_forward(resid, gain[0:1, :], bias[0:1, :])
         hidden[rows, :] = normed
         low_one[rows, :] = normed.astype(jnp.bfloat16)
         return 0
 
-    lax.fori_loop(0, half // TILE, out_one, 0)
-    keep(resid1, o_resid1)
-
-    fi.x.wait_recv()
-    go(fi.zx)
-    for copy in cx:
-        copy.wait_recv()
-    for copy in cd:
-        go(copy)
-    go(fo.x)
-    go(fa.x)
-    swap_wait(MEM, memory, mem, mine)
-    mem_c = go(there(MEM_C, mem.at[mine], mem.at[mine], to_c))
-    for copy in cy:
-        copy.wait_recv()
-    go(fo.y)
-    go(fa.y)
-    for copy in cd:
-        copy.wait_recv()
-    cq_c = go(there(CQ_C, wq_m.at[:, foreign], wq_o.at[:, foreign], to_c))
-    mem_c.wait_recv()
-
-    def kv_rows(step, _):
-        p, t = lax.div(step, SEQ // TILE), lax.rem(step, SEQ // TILE)
-        rows = pl.ds(pl.multiple_of(t * TILE, TILE), TILE)
-        kv[p, rows, :] = nn(mem[rows, :], wkv[p]).astype(jnp.bfloat16)
+    def out_two(t, _):
+        rows = step(t * TILE, TILE, TILE)
+        resid2[rows, :] = with_out(t, hidden[rows, :], cctx, cctx_o, wco_m, wco_o)
         return 0
 
-    lax.fori_loop(0, 4 * (MLEN // TILE), kv_rows, 0)
-    keep(kv, o_kv)
-    keep(wkv, o_wkv)
-    fi.d.wait_recv()
-    go(fi.zd)
-    cq_c.wait_recv()
-    keep(wq_m, o_wq_m)
-    keep(wq_o, o_wq_o)
-
     def q_rows(t, _):
-        rows = pl.ds(pl.multiple_of(t * TILE, TILE), TILE)
-        rows_all = pl.ds(pl.multiple_of(c * half + t * TILE, TILE), TILE)
+        rows = step(t * TILE, TILE, TILE)
+        rows_all = step(c * half + t * TILE, TILE, TILE)
         q_send[rows, :] = nn(low_one[rows, :], wq_o[...]).astype(jnp.bfloat16)
         q_all[rows_all, :] = nn(low_one[rows, :], wq_m[...]).astype(jnp.bfloat16)
         return 0
 
+    def split_at(order, first, count):
+        places = [order.index(first + k) for k in range(count)]
+        starts = [0] + [place + 1 for place in places]
+        return [order[a:b] for a, b in zip(starts, places)], order[places[-1] + 1 :]
+
+    def pieces_loop(segments, ready, work, sends):
+        def body(p, _):
+            for k, segment in enumerate(segments):
+
+                @pl.when(p == k)
+                def _():
+                    for op in segment:
+                        launch(op)
+                    ready(k)
+
+            work(p)
+            for k, copy in enumerate(sends):
+                pl.when(p == k)(copy.start)
+            return 0
+
+        lax.fori_loop(0, len(segments), body, 0)
+        pending.extend(sends)
+
+    for copy in own_a[:3]:
+        copy.start()
+    own_a[3].start()
+    seg_start()
+    mseg_start()
+    segments, rest = split_at(list(SCHEDULE), SELF_PIECE, 4)
+    for op in segments[0]:
+        launch(op)
+    for copy in own_b:
+        copy.start()
+    bounds_of()
+    for copy in own_a:
+        copy.wait()
+    segments[0] = []
+
+    def self_ready(k):
+        if k == 0:
+            wait_for(TOK_C)
+        else:
+            for op in weight_needs(0, k):
+                wait_for(op)
+
+    pieces_loop(segments, self_ready, self_piece, sctx_out)
+    for src, dst in ((qkv, o_qkv), (wself, o_wself), (sctx, o_sctx), (slse, o_slse), (pre, o_pre)):
+        keep(src, dst)
+    for copy in own_b:
+        copy.wait()
+    before, rest = split_at(rest, OUT_ONE, 1)
+    for op in before[0]:
+        launch(op)
+    for copy in sctx_out:
+        copy.wait_recv()
+    wait_for(16 + 6)
+    lax.fori_loop(0, half // TILE, out_one, 0)
+    for src, dst in ((resid1, o_resid1), (wso_m, o_wso_m), (wso_o, o_wso_o)):
+        keep(src, dst)
+    before, rest = split_at(rest, CROSS_Q, 1)
+    for op in before[0]:
+        launch(op)
+    wait_for(32 + 6)
     lax.fori_loop(0, half // TILE, q_rows, 0)
-    q_c = go(there(Q_C, q_send, q_all.at[mine], to_c))
-    q_c.wait_recv()
-    keep(q_all, o_q)
-
-    def second_piece(p, _):
-        @pl.when(p == 2)
-        def _():
-            fo.x.wait_recv()
-            fa.x.wait_recv()
-            for copy in (fo.d, fa.d, fo.zx, fa.zx):
-                copy.start()
-
-        vt[...] = kv[p, :, 128:256].astype(jnp.float32).T.astype(jnp.bfloat16)
-        place = pl.ds(pl.multiple_of(p * 128, 128), 128)
-
-        def block(qi, _):
-            span = pl.ds(pl.multiple_of(qi * QB, QB), QB)
-            pos = lax.broadcasted_iota(jnp.int32, (MLEN, QB), 0)
-            mask = (pos >= bounds[2:3, span]) & (pos <= bounds[3:4, span])
-            out, lse = attend_tile(q_all[span, place], kv[p, :, 0:128], vt[...], mask, None, None)
-            cctx[span, place] = out
-            for h in range(2):
-                clse[p, h : h + 1, span] = lse[h]
-            return 0
-
-        lax.fori_loop(0, SEQ // QB, block, 0)
-        there(CROSS_CTX + p, cctx.at[others, place], cctx_o.at[:, place], to_c).start()
-        return 0
-
-    lax.fori_loop(0, 4, second_piece, 0)
-    pending.extend([fo.d, fa.d, fo.zx, fa.zx])
-    for i in range(4):
-        copy = there(CROSS_CTX + i, cctx.at[others, pl.ds(128 * i, 128)], cctx_o.at[:, pl.ds(128 * i, 128)], to_c)
-        pending.append(copy)
-    cctx_in = pending[-4:]
-    keep(cctx, o_cctx)
-    keep(clse, o_clse)
-    for copy in (fo.y, fa.y):
+    q_out.start()
+    pending.append(q_out)
+    for src, dst in ((wq_m, o_wq_m), (wq_o, o_wq_o)):
+        keep(src, dst)
+    segments, rest = split_at(rest, CROSS_PIECE, 4)
+
+    def cross_ready(k):
+        if k == 0:
+            wait_for(MEM_C)
+            q_out.wait_recv()
+        else:
+            for op in weight_needs(48, k):
+                wait_for(op)
+
+    pieces_loop(segments, cross_ready, cross_piece, cctx_out)
+    for src, dst in ((q_all, o_q), (kv, o_kv), (wkv, o_wkv), (cctx, o_cctx), (clse, o_clse)):
+        keep(src, dst)
+    before, rest = split_at(rest, OUT_TWO, 1)
+    for op in before[0]:
+        launch(op)
+    for copy in cctx_out:
         copy.wait_recv()
-    go(fo.zy)
-    go(fa.zy)
-    swap_start(COT, cotangent, o_cot, slice(None), slice(None))
-    for copy in (fi.zx, fi.zy, fi.zd):
-        copy.wait_recv()
-    go(fi.c)
-    for copy in cctx_in + [co_c]:
-        copy.wait_recv()
-    keep(wco_m, o_wco_m)
-    keep(wco_o, o_wco_o)
-
-    def out_two(t, _):
-        rows = pl.ds(pl.multiple_of(t * TILE, TILE), TILE)
-        rows, _, resid = out_rows(t, hidden[rows, :], cctx, cctx_o, wco_m, wco_o)
-        resid2[rows, :] = resid
-        return 0
-
+    wait_for(64 + 6)
     lax.fori_loop(0, half // TILE, out_two, 0)
-    keep(resid2, o_resid2)
-    for copy in (fo.d, fa.d):
-        copy.wait_recv()
-    go(fo.zd)
-    go(fa.zd)
-    for group in (fo, fa):
-        for copy in (group.zx, group.zy, group.zd):
-            copy.wait_recv()
-    go(fo.c)
-    go(fa.c)
-    for group in (fi, fo, fa):
-        group.c.wait_recv()
-    swap_wait(COT, cotangent, o_cot, slice(None))
+    for src, dst in ((resid2, o_resid2), (wco_m, o_wco_m), (wco_o, o_wco_o)):
+        keep(src, dst)
+    for op in rest:
+        launch(op)
+    for op in list(copies):
+        wait_for(op)
     for copy in pending:
         copy.wait_send()
     for copy in saves:
@@ -939,14 +961,12 @@
     resid1: jax.Array
     resid2: jax.Array
     bounds: jax.Array
-    tok: jax.Array
-    cot: jax.Array
     fin: jax.Array
     fout: jax.Array
     fad: jax.Array
 
 
-def forward_call(tokens, memory, cotangent, seg, mseg, prefix, w_self, w_so, w_cq, w_ckv, w_co, fc_in, fc_out, ad, gain, bias):
+def forward_call(tokens, memory, seg, mseg, prefix, w_self, w_so, w_cq, w_ckv, w_co, fc_in, fc_out, ad, gain, bias):
     bf16, f32 = jnp.bfloat16, jnp.float32
     half, deep = tokens.shape
     shape = jax.ShapeDtypeStruct
@@ -972,7 +992,6 @@
         bounds=((8, SEQ), jnp.int32),
     )
     outs = [shape(*value) for value in held.values()]
-    outs += [shape((half, deep), bf16), shape((half, deep), bf16)]
     outs += [shape((3,) + fc_in.shape, bf16), shape((3,) + fc_out.shape, bf16), shape((3,) + ad.shape, bf16)]
     scratch = [pltpu.VMEM(*value) for value in held.values()] + [
         pltpu.VMEM((SEQ, deep), bf16),
@@ -994,14 +1013,14 @@
     results = pl.pallas_call(
         forward_kernel,
         out_shape=outs,
-        in_specs=[anywhere] * 14 + [vmem] * 2,
+        in_specs=[anywhere] * 13 + [vmem] * 2,
         out_specs=[anywhere] * len(outs),
         scratch_shapes=scratch,
         compiler_params=pltpu.CompilerParams(
             collective_id=0, has_side_effects=True, vmem_limit_bytes=58 * 2**20
         ),
         name="layer_forward",
-    )(tokens, memory, cotangent, seg, mseg, prefix, w_self, w_so, w_cq, w_ckv, w_co, fc_in, fc_out, ad, gain, bias)
+    )(tokens, memory, seg, mseg, prefix, w_self, w_so, w_cq, w_ckv, w_co, fc_in, fc_out, ad, gain, bias)
     return Held(*results)
 
 
@@ -1348,7 +1367,6 @@
     held = forward_call(
         tokens,
         memory,
-        cotangent,
         dec_seg.reshape(2, 1, SEQ),
         mem_seg.reshape(2, 1, MLEN),
         jnp.pad(prefix, ((0, 0), (0, 32 - count), (0, 0))),
@@ -1382,7 +1400,7 @@
         return lax.optimization_barrier((value,) + earlier)[0]
 
     out, grad_two, unit_grads, dctx_m, dctx_s = feed_call(
-        held.resid2, held.cot, ln_gain, ln_bias, held.wco_m, held.wco_o,
+        held.resid2, move.swap(cotangent), ln_gain, ln_bias, held.wco_m, held.wco_o,
         fc_in, held.fin, fc_out, held.fout, ad, held.fad,
     )
     output = move.swap(out)

time: 420 us -> 358 us (0.85)
  Pallas kernels: 301 us -> 243 us
    pallas_call x1, Pallas kernels: 196 us -> 135 us  [forward_call(): pl.pallas_call(forward_kernel, out_shape=outs, in_specs=[anywhere] * 13 +...]
    ppermute x18, starting transfers between devices: 36 us -> 28.8 us  [perm(): return lambda value: lax.ppermute(value, AXES, table)]
    ppermute x3 -> x4, starting transfers between devices: 8.93 us -> 14.8 us  [swap(): return jnp.where(stays, value, lax.ppermute(value, AXES, crossing))]
  transfers between devices with their start and end apart: 21 -> 22, of which waited for: 5 -> 7; matrix products, arithmetic and copies ran while one was open for 6% -> 8% of each run, Pallas kernels for 15% -> 57%
where the time goes in v3:
time: 358 us; the launch traced here: 356 us
  Pallas kernels  243 us (68%)
  starting transfers between devices  43.6 us (12%)
  waiting for transfers between devices  28 us (8%)
  other arithmetic  15.8 us (4%)
  local copies, waits for them, and re-layouts  12.6 us (4%)
  matrix products  12.1 us (3%)
    pallas_call x1, Pallas kernels, forward_call(): pl.pallas_call(forward_kernel, out_shape=outs, in_specs=[anywhere] * 13 +...  135 us
    pallas_call x2, Pallas kernels, backward_call(): pl.pallas_call(functools.partial(backward_kernel, has_prefix, 0 if has_pr...  65.9 us
    pallas_call x1, Pallas kernels, feed_call(): pl.pallas_call(feed_kernel, out_shape=[shape((rows, deep), bf16), shape((...  41.7 us
    ppermute x18, starting transfers between devices, perm(): return lambda value: lax.ppermute(value, AXES, table)  28.8 us
    ppermute x18, waiting for transfers between devices, perm(): return lambda value: lax.ppermute(value, AXES, table)  20.5 us
    ppermute x4, starting transfers between devices, swap(): return jnp.where(stays, value, lax.ppermute(value, AXES, crossing))  14.8 us
    dot_general x12, matrix products, dot_right(): lax.dot_general(left, right, (((1,), (1,)), ((), ())), preferred_element_...  12.1 us
    unnamed x44, local copies, waits for them, and re-layouts  7.75 us
  transfers between devices with their start and end apart: 22, of which 7 were waited for; matrix products, arithmetic and copies ran while one was open for 8% of the time, Pallas kernels for 57%

profile of v3, /device:TPU:1, one launch (start us, length us, event | category | flops | bytes accessed | tf_op | source)
XLA Modules:
  0.0 356.2 jit_solution(513943181670557022)
XLA Ops:
  0.6 4.5 %collective-permute-start = (bf16[512,1024]{1,0:T(8,128)(2,1)}, bf16[512,1024]{1,0:T(8,128)(2,1)S(1)}, u32[]{:S(2)}, u32[]{:S(2)}) collective-permute-start(bf16[512,1024]{1,0:T(8,128)(2,1)} %param.19), channel_id=1, source_target_pairs={{1,4},{3,6},{4,1},{6,3},{9,12},{11,14},{12,9},{14,11},{17,20},{19,... | collective-permute-start | bytes 3145736 | tf_op jit(solution)/shard_map/ppermute | solution.py:1331
  7.7 1.8 pad_maximum_fusion.ad
  9.4 135.4 %layer_forward.1 = (bf16[4,1024,384]{2,1,0:T(8,128)(2,1)}, bf16[4,1024,384]{2,1,0:T(8,128)(2,1)}, bf16[1024,512]{1,0:T(8,128)(2,1)}, f32[4,8,1024]{2,1,0:T(8,128...) custom-call(bf16[512,1024]{1,0:T(8,128)(2,1)} %tokens.1, ...), custom_call_target="tpu_custom_call" | custom-call | tf_op jit(solution)/shard_map/layer_forward/pallas_call | solution.py:1013
  146.0 41.7 %feed_forward.1 = (bf16[512,1024]{1,0:T(8,128)(2,1)}, f32[512,1024]{1,0:T(8,128)}, f32[512,2048]{1,0:T(8,128)}, bf16[512,512]{1,0:T(8,128)(2,1)}, bf16[512,512]{1,0:T(8,128)(2,1)}) custom-call(f32[512,1024]{1,0:T(8,128)} %get-tuple-element.39.resid2, bf16[512,1024]{1,0:T(8,128)(2,1)} %broadcast_select_fusion.1.cot, f32[3,1024]{1,0:T(4,128)} %gain.3, ...), custom_call_target="tpu_custom_call" | custom-call | tf_op jit(solution)/shard_map/feed_forward/pallas_call | solution.py:1266
  187.6 2.9 fusion
  193.4 2.0 fusion.53
  198.3 4.3 %collective-permute-start.1 = (bf16[512,1024]{1,0:T(8,128)(2,1)}, bf16[512,1024]{1,0:T(8,128)(2,1)}, u32[]{:S(2)}, u32[]{:S(2)}) collective-permute-start(bf16[512,1024]{1,0:T(8,128)(2,1)} %get-tuple-element.45), channel_id=1, source_target_pairs={{1,4},{3,6},{4,1},{6,3},{9,12},{11,14},{12,9},{14,11},{17,20},{19,... | collective-permute-start | bytes 3145736 | tf_op jit(solution)/shard_map/ppermute | solution.py:1331
  204.2 5.5 %collective-permute-done.6 = bf16[64,2048]{1,0:T(8,128)(2,1)S(1)} collective-permute-done((bf16[64,2048]{1,0:T(8,128)(2,1)S(1)}, bf16[64,2048]{1,0:T(8,128)(2,1)S(1)}, u32[]{:S(2)}, u32[]{:S(2)}) %collective-permute-start.6) | collective-permute-done | bytes 262176 | tf_op jit(solution)/shard_map/ppermute | solution.py:1321
  209.9 31.0 %cross_backward.1 = (bf16[1024,512]{1,0:T(8,128)(2,1)S(1)}, bf16[4,1024,256]{2,1,0:T(8,128)(2,1)S(1)}) custom-call(s32[8,1024]{1,0:T(8,128)S(1)} %copy-done.8, bf16[1024,512]{1,0:T(8,128)(2,1)S(1)} %copy-done.3, bf16[4,1024,256]{2,1,0:T(8,128)(2,1)S(1)} %copy-done.1, s32[8,1024]{1,0:T(8,128)S(1)} %copy-done.8, bf16[1024,512]{1,0:T(8,128)(2,1)S(1)} %copy-done.4, ...), custom_call_target="tpu_custom_call" | custom-call | flops 5368709120 | bytes 10485760 | tf_op jit(solution)/shard_map/cross_backward/pallas_call | solution.py:1146
  242.5 1.6 collective-permute-start.7
  254.8 34.9 %self_backward.1 = (bf16[4,1024,384]{2,1,0:T(8,128)(2,1)S(1)}, f32[4,2,32,128]{3,2,1,0:T(8,128)S(1)}) custom-call(s32[8,1024]{1,0:T(8,128)S(1)} %copy-done.8, bf16[4,1024,384]{2,1,0:T(8,128)(2,1)S(1)} %copy-done, s32[8,1024]{1,0:T(8,128)S(1)} %copy-done.8, bf16[1024,512]{1,0:T(8,128)(2,1)S(1)} %copy-done.2, ...), custom_call_target="tpu_custom_call" | custom-call | flops 5368709120 | bytes 10485760 | tf_op jit(solution)/shard_map/self_backward/pallas_call | solution.py:1146
  293.5 7.8 %collective-permute-start.13 = (f32[2,32,128]{2,1,0:T(8,128)S(1)}, f32[2,32,128]{2,1,0:T(8,128)S(1)}, u32[]{:S(2)}, u32[]{:S(2)}) collective-permute-start(f32[2,32,128]{2,1,0:T(8,128)S(1)} %get-tuple-element.90), channel_id=1, source_target_pairs={{0,1},{1,0},{2,3},{3,2},{4,5},{5,4},{6,7},{7,6},{8,9},{9,8},{10,11... | collective-permute-start | bytes 98312 | tf_op jit(solution)/shard_map/ppermute | solution.py:1321
  302.6 1.5 add_add_fusion.1
  304.2 4.8 %collective-permute-start.19 = (bf16[64,2048]{1,0:T(8,128)(2,1)S(1)}, bf16[64,2048]{1,0:T(8,128)(2,1)S(1)}, u32[]{:S(2)}, u32[]{:S(2)}) collective-permute-start(bf16[64,2048]{1,0:T(8,128)(2,1)S(1)} %convert_element_type.92), channel_id=1, source_target_pairs={{0,8},{1,9},{2,10},{3,11},{4,12},{5,13},{6,14},{7,15},{8,0},{9,1},... | collective-permute-start | bytes 786440 | tf_op jit(solution)/shard_map/ppermute | solution.py:1321
  310.1 1.9 collective-permute-start.9
  312.1 3.3 collective-permute-done.16
  315.4 5.4 %collective-permute-start.17 = (f32[2,32,128]{2,1,0:T(8,128)S(1)}, f32[2,32,128]{2,1,0:T(8,128)S(1)}, u32[]{:S(2)}, u32[]{:S(2)}) collective-permute-start(f32[2,32,128]{2,1,0:T(8,128)S(1)} %add.137), channel_id=1, source_target_pairs={{0,16},{1,17},{2,18},{3,19},{4,20},{5,21},{6,22},{7,23},{8,24},{9,... | collective-permute-start | bytes 98312 | tf_op jit(solution)/shard_map/ppermute | solution.py:1321
  322.2 3.7 %collective-permute-start.12 = (bf16[512,1024]{1,0:T(8,128)(2,1)}, bf16[512,1024]{1,0:T(8,128)(2,1)S(1)}, u32[]{:S(2)}, u32[]{:S(2)}) collective-permute-start(bf16[512,1024]{1,0:T(8,128)(2,1)} %add_convert_fusion), channel_id=1, source_target_pairs={{1,4},{3,6},{4,1},{6,3},{9,12},{11,14},{12,9},{14,11},{17,20},{19,... | collective-permute-start | bytes 3145736 | tf_op jit(solution)/shard_map/ppermute | solution.py:1331
  326.1 9.4 %collective-permute-done.20 = bf16[64,2048]{1,0:T(8,128)(2,1)S(1)} collective-permute-done((bf16[64,2048]{1,0:T(8,128)(2,1)S(1)}, bf16[64,2048]{1,0:T(8,128)(2,1)S(1)}, u32[]{:S(2)}, u32[]{:S(2)}) %collective-permute-start.20) | collective-permute-done | bytes 262176 | tf_op jit(solution)/shard_map/ppermute | solution.py:1321
  337.3 2.2 collective-permute-start.10
  339.5 2.3 broadcast_select_fusion
  344.5 1.5 select_convert_fusion
  346.0 7.5 %collective-permute-done.10 = bf16[512,1024]{1,0:T(8,128)(2,1)} collective-permute-done((bf16[512,1024]{1,0:T(8,128)(2,1)S(1)}, bf16[512,1024]{1,0:T(8,128)(2,1)}, u32[]{:S(2)}, u32[]{:S(2)}) %collective-permute-start.10) | collective-permute-done | bytes 1048608 | tf_op jit(solution)/shard_map/ppermute | solution.py:1331
  353.5 2.7 select_convert_fusion.1
  (116 shorter events, 35.3 us)
Async XLA Ops:
  0.6 144.2 %collective-permute-start = (bf16[512,1024]{1,0:T(8,128)(2,1)}, bf16[512,1024]{1,0:T(8,128)(2,1)S(1)}, u32[]{:S(2)}, u32[]{:S(2)}) collective-permute-start(bf16[512,1024]{1,0:T(8,128)(2,1)} %param.19), channel_id=1, source_target_pairs={{1,4},{3,6},{4,1},{6,3},{9,12},{11,14},{12,9},{14,11},{17,20},{19,... | collective-permute-start | bytes 3145736 | tf_op jit(solution)/shard_map/ppermute | solution.py:1331
  9.4 135.4 %copy-start.15 = (bf16[512,1024]{1,0:T(8,128)(2,1)S(1)}, bf16[512,1024]{1,0:T(8,128)(2,1)}, u32[]{:S(2)}) copy-start(bf16[512,1024]{1,0:T(8,128)(2,1)} %param.19) | copy-start | bytes 3145732
  190.5 2.9 collective-permute-start.3
  191.8 10.9 %collective-permute-start.2 = (bf16[512,512]{1,0:T(8,128)(2,1)S(1)}, bf16[512,512]{1,0:T(8,128)(2,1)S(1)}, u32[]{:S(2)}, u32[]{:S(2)}) collective-permute-start(bf16[512,512]{1,0:T(8,128)(2,1)S(1)} %copy-done.19), channel_id=1, source_target_pairs={{0,4},{1,5},{2,6},{3,7},{4,0},{5,1},{6,2},{7,3},{8,12},{9,13},{10,... | collective-permute-start | bytes 1572872 | tf_op jit(solution)/shard_map/ppermute | solution.py:1321
  195.6 7.8 %collective-permute-start.4 = (bf16[64,2048]{1,0:T(8,128)(2,1)S(1)}, bf16[64,2048]{1,0:T(8,128)(2,1)S(1)}, u32[]{:S(2)}, u32[]{:S(2)}) collective-permute-start(bf16[64,2048]{1,0:T(8,128)(2,1)S(1)} %get-tuple-element.87), channel_id=1, source_target_pairs={{0,1},{1,0},{2,3},{3,2},{4,5},{5,4},{6,7},{7,6},{8,9},{9,8},{10,11... | collective-permute-start | bytes 786440 | tf_op jit(solution)/shard_map/ppermute | solution.py:1321
  197.0 7.3 %collective-permute-start.5 = (bf16[64,2048]{1,0:T(8,128)(2,1)S(1)}, bf16[64,2048]{1,0:T(8,128)(2,1)S(1)}, u32[]{:S(2)}, u32[]{:S(2)}) collective-permute-start(bf16[64,2048]{1,0:T(8,128)(2,1)S(1)} %get-tuple-element.89), channel_id=1, source_target_pairs={{0,2},{1,3},{2,0},{3,1},{4,6},{5,7},{6,4},{7,5},{8,10},{9,11},{10,... | collective-permute-start | bytes 786440 | tf_op jit(solution)/shard_map/ppermute | solution.py:1321
  198.0 11.7 %collective-permute-start.6 = (bf16[64,2048]{1,0:T(8,128)(2,1)S(1)}, bf16[64,2048]{1,0:T(8,128)(2,1)S(1)}, u32[]{:S(2)}, u32[]{:S(2)}) collective-permute-start(bf16[64,2048]{1,0:T(8,128)(2,1)S(1)} %get-tuple-element.88), channel_id=1, source_target_pairs={{0,3},{1,2},{2,1},{3,0},{4,7},{5,6},{6,5},{7,4},{8,11},{9,10},{10,... | collective-permute-start | bytes 786440 | tf_op jit(solution)/shard_map/ppermute | solution.py:1321
  198.3 141.2 %collective-permute-start.1 = (bf16[512,1024]{1,0:T(8,128)(2,1)}, bf16[512,1024]{1,0:T(8,128)(2,1)}, u32[]{:S(2)}, u32[]{:S(2)}) collective-permute-start(bf16[512,1024]{1,0:T(8,128)(2,1)} %get-tuple-element.45), channel_id=1, source_target_pairs={{1,4},{3,6},{4,1},{6,3},{9,12},{11,14},{12,9},{14,11},{17,20},{19,... | collective-permute-start | bytes 3145736 | tf_op jit(solution)/shard_map/ppermute | solution.py:1331
  242.5 3.2 collective-permute-start.7
  249.9 3.4 collective-permute-start.8
  251.5 69.3 %collective-permute-start.11 = (bf16[512,1024]{1,0:T(8,128)(2,1)S(1)}, bf16[512,1024]{1,0:T(8,128)(2,1)S(1)}, u32[]{:S(2)}, u32[]{:S(2)}) collective-permute-start(bf16[512,1024]{1,0:T(8,128)(2,1)S(1)} %dynamic-slice_convert_fusion), channel_id=1, source_target_pairs={{0,4},{1,5},{2,6},{3,7},{4,0},{5,1},{6,2},{7,3},{8,12},{9,13},{10,... | collective-permute-start | bytes 3145736 | tf_op jit(solution)/shard_map/ppermute | solution.py:1321
  254.8 34.9 %copy-start.10 = (bf16[4,1024,384]{2,1,0:T(8,128)(2,1)S(1)}, bf16[4,1024,384]{2,1,0:T(8,128)(2,1)}, u32[]{:S(2)}) copy-start(bf16[4,1024,384]{2,1,0:T(8,128)(2,1)} %get-tuple-element.67) | copy-start | bytes 9437188
  293.5 10.6 %collective-permute-start.13 = (f32[2,32,128]{2,1,0:T(8,128)S(1)}, f32[2,32,128]{2,1,0:T(8,128)S(1)}, u32[]{:S(2)}, u32[]{:S(2)}) collective-permute-start(f32[2,32,128]{2,1,0:T(8,128)S(1)} %get-tuple-element.90), channel_id=1, source_target_pairs={{0,1},{1,0},{2,3},{3,2},{4,5},{5,4},{6,7},{7,6},{8,9},{9,8},{10,11... | collective-permute-start | bytes 98312 | tf_op jit(solution)/shard_map/ppermute | solution.py:1321
  301.3 7.7 %collective-permute-start.14 = (f32[2,32,128]{2,1,0:T(8,128)S(1)}, f32[2,32,128]{2,1,0:T(8,128)S(1)}, u32[]{:S(2)}, u32[]{:S(2)}) collective-permute-start(f32[2,32,128]{2,1,0:T(8,128)S(1)} %get-tuple-element.92), channel_id=1, source_target_pairs={{0,2},{1,3},{2,0},{3,1},{4,6},{5,7},{6,4},{7,5},{8,10},{9,11},{10,... | collective-permute-start | bytes 98312 | tf_op jit(solution)/shard_map/ppermute | solution.py:1321
  301.7 7.3 %collective-permute-start.15 = (f32[2,32,128]{2,1,0:T(8,128)S(1)}, f32[2,32,128]{2,1,0:T(8,128)S(1)}, u32[]{:S(2)}, u32[]{:S(2)}) collective-permute-start(f32[2,32,128]{2,1,0:T(8,128)S(1)} %get-tuple-element.91), channel_id=1, source_target_pairs={{0,3},{1,2},{2,1},{3,0},{4,7},{5,6},{6,5},{7,4},{8,11},{9,10},{10,... | collective-permute-start | bytes 98312 | tf_op jit(solution)/shard_map/ppermute | solution.py:1321
  304.2 16.5 %collective-permute-start.19 = (bf16[64,2048]{1,0:T(8,128)(2,1)S(1)}, bf16[64,2048]{1,0:T(8,128)(2,1)S(1)}, u32[]{:S(2)}, u32[]{:S(2)}) collective-permute-start(bf16[64,2048]{1,0:T(8,128)(2,1)S(1)} %convert_element_type.92), channel_id=1, source_target_pairs={{0,8},{1,9},{2,10},{3,11},{4,12},{5,13},{6,14},{7,15},{8,0},{9,1},... | collective-permute-start | bytes 786440 | tf_op jit(solution)/shard_map/ppermute | solution.py:1321
  309.0 6.3 %collective-permute-start.16 = (f32[2,32,128]{2,1,0:T(8,128)S(1)}, f32[2,32,128]{2,1,0:T(8,128)S(1)}, u32[]{:S(2)}, u32[]{:S(2)}) collective-permute-start(f32[2,32,128]{2,1,0:T(8,128)S(1)} %fusion.49), channel_id=1, source_target_pairs={{0,8},{1,9},{2,10},{3,11},{4,12},{5,13},{6,14},{7,15},{8,0},{9,1},... | collective-permute-start | bytes 98312 | tf_op jit(solution)/shard_map/ppermute | solution.py:1321
  310.1 26.5 %collective-permute-start.9 = (bf16[512,1024]{1,0:T(8,128)(2,1)S(1)}, bf16[512,1024]{1,0:T(8,128)(2,1)S(1)}, u32[]{:S(2)}, u32[]{:S(2)}) collective-permute-start(bf16[512,1024]{1,0:T(8,128)(2,1)S(1)} %dynamic-slice_convert_fusion.1), channel_id=1, source_target_pairs={{0,4},{1,5},{2,6},{3,7},{4,0},{5,1},{6,2},{7,3},{8,12},{9,13},{10,... | collective-permute-start | bytes 3145736 | tf_op jit(solution)/shard_map/ppermute | solution.py:1321
  315.4 10.6 %collective-permute-start.17 = (f32[2,32,128]{2,1,0:T(8,128)S(1)}, f32[2,32,128]{2,1,0:T(8,128)S(1)}, u32[]{:S(2)}, u32[]{:S(2)}) collective-permute-start(f32[2,32,128]{2,1,0:T(8,128)S(1)} %add.137), channel_id=1, source_target_pairs={{0,16},{1,17},{2,18},{3,19},{4,20},{5,21},{6,22},{7,23},{8,24},{9,... | collective-permute-start | bytes 98312 | tf_op jit(solution)/shard_map/ppermute | solution.py:1321
  320.8 14.6 %collective-permute-start.20 = (bf16[64,2048]{1,0:T(8,128)(2,1)S(1)}, bf16[64,2048]{1,0:T(8,128)(2,1)S(1)}, u32[]{:S(2)}, u32[]{:S(2)}) collective-permute-start(bf16[64,2048]{1,0:T(8,128)(2,1)S(1)} %fusion.46), channel_id=1, source_target_pairs={{0,16},{1,17},{2,18},{3,19},{4,20},{5,21},{6,22},{7,23},{8,24},{9,... | collective-permute-start | bytes 786440 | tf_op jit(solution)/shard_map/ppermute | solution.py:1321
  322.2 22.3 %collective-permute-start.12 = (bf16[512,1024]{1,0:T(8,128)(2,1)}, bf16[512,1024]{1,0:T(8,128)(2,1)S(1)}, u32[]{:S(2)}, u32[]{:S(2)}) collective-permute-start(bf16[512,1024]{1,0:T(8,128)(2,1)} %add_convert_fusion), channel_id=1, source_target_pairs={{1,4},{3,6},{4,1},{6,3},{9,12},{11,14},{12,9},{14,11},{17,20},{19,... | collective-permute-start | bytes 3145736 | tf_op jit(solution)/shard_map/ppermute | solution.py:1331
  326.0 15.8 %collective-permute-start.18 = (f32[2,32,128]{2,1,0:T(8,128)S(1)}, f32[2,32,128]{2,1,0:T(8,128)S(1)}, u32[]{:S(2)}, u32[]{:S(2)}) collective-permute-start(f32[2,32,128]{2,1,0:T(8,128)S(1)} %add.138), channel_id=1, source_target_pairs={{0,4},{1,5},{2,6},{3,7},{4,0},{5,1},{6,2},{7,3},{8,12},{9,13},{10,... | collective-permute-start | bytes 98312 | tf_op jit(solution)/shard_map/ppermute | solution.py:1321
  335.5 7.0 %collective-permute-start.21 = (bf16[64,2048]{1,0:T(8,128)(2,1)S(1)}, bf16[64,2048]{1,0:T(8,128)(2,1)S(1)}, u32[]{:S(2)}, u32[]{:S(2)}) collective-permute-start(bf16[64,2048]{1,0:T(8,128)(2,1)S(1)} %get-tuple-element.80), channel_id=1, source_target_pairs={{0,4},{1,5},{2,6},{3,7},{4,0},{5,1},{6,2},{7,3},{8,12},{9,13},{10,... | collective-permute-start | bytes 786440 | tf_op jit(solution)/shard_map/ppermute | solution.py:1321
  337.3 16.2 %collective-permute-start.10 = (bf16[512,1024]{1,0:T(8,128)(2,1)S(1)}, bf16[512,1024]{1,0:T(8,128)(2,1)}, u32[]{:S(2)}, u32[]{:S(2)}) collective-permute-start(bf16[512,1024]{1,0:T(8,128)(2,1)S(1)} %add_convert_fusion.1), channel_id=1, source_target_pairs={{1,4},{3,6},{4,1},{6,3},{9,12},{11,14},{12,9},{14,11},{17,20},{19,... | collective-permute-start | bytes 3145736 | tf_op jit(solution)/shard_map/ppermute | solution.py:1331
  (19 other events, 136.3 us)

commit v4 on v3

--- a/solution.py
+++ b/solution.py
@@ -1158,11 +1158,49 @@
 HIDDEN = 512
 
 
+def swap_halves(place, src, dst_there, dst_here, send, recv, local):
+    moves = place.c != place.x
+    away = pltpu.make_async_remote_copy(
+        src_ref=src, dst_ref=dst_there, send_sem=send, recv_sem=recv, device_id=place.to_s, device_id_type=MESH
+    )
+    home = pltpu.make_async_copy(src, dst_here, local)
+
+    def start():
+        pl.when(moves)(away.start)
+        pl.when(jnp.logical_not(moves))(home.start)
+
+    def wait():
+        pl.when(moves)(away.wait)
+        pl.when(jnp.logical_not(moves))(home.wait)
+
+    return start, wait
+
+
 def feed_kernel(
-    resid2, cot, gain, bias, wco_m, wco_o, fc_in, fin, fc_out, fout, ad, fad,
-    out, grad_two, units, dctx_m, dctx_s,
+    resid2, cotangent, gain, bias, wco_m, wco_o, fc_in, fin, fc_out, fout, ad, fad,
+    out, grad_two, unit_sum, dctx,
     win, wout, down, up, slope, low, hidden, acc, gate, ada, branch_low, sem,
+    cot, out_v, units, unit_send, unit_recv, near_send, near_recv, dctx_s, send, recv, local,
 ):
+    place = Place()
+    place.greet((place.to_x, place.to_y, place.to_d, place.to_c), True)
+    c = place.c
+    cot_start, cot_wait = swap_halves(place, cotangent, cot, cot, send.at[0], recv.at[0], local.at[0])
+    out_start, out_wait = swap_halves(place, out_v, out, out, send.at[1], recv.at[1], local.at[1])
+    cot_start()
+
+    def there(slot, src, dst, device):
+        return pltpu.make_async_remote_copy(
+            src_ref=src, dst_ref=dst, send_sem=send.at[slot], recv_sem=recv.at[slot], device_id=device, device_id_type=MESH
+        )
+
+    half = resid2.shape[0]
+    mine = pl.ds(pl.multiple_of(c * half, half), half)
+    unit_core = there(2, unit_send, unit_recv, place.to_c)
+    unit_near = [
+        there(3 + i, near_send.at[i], near_recv.at[i], device) for i, device in enumerate((place.to_x, place.to_y, place.to_d))
+    ]
+    dctx_core = there(6, dctx_s, dctx.at[mine], place.to_c)
     bf16 = jnp.bfloat16
     per = fc_in.shape[1] // HIDDEN
     steps = 4 * per
@@ -1218,7 +1256,7 @@
         rows = at(t)
         resid = hidden[rows, :] + acc[rows, :]
         normed, inv = norm_parts(resid)
-        out[rows, :] = (normed * gain[2:3, :] + bias[2:3, :]).astype(bf16)
+        out_v[rows, :] = (normed * gain[2:3, :] + bias[2:3, :]).astype(bf16)
         scaled = cot[rows, :].astype(jnp.float32) * gain[2:3, :]
         grad = inv * (
             scaled
@@ -1229,11 +1267,18 @@
         branch_low[rows, :] = grad.astype(bf16)
         return 0
 
+    cot_wait()
     lax.fori_loop(0, tiles, middle, 0)
+    out_start()
     grelu = (adapter_scale * nt(branch_low[...], up[...]) * gate[...]).astype(bf16)
     features = low.shape[1]
-    units[:, 0:features] = tn(grelu, low[...])
-    units[:, features : 2 * features] = adapter_scale * tn(ada[...], branch_low[...])
+    some = group // 2
+    for first, value in ((0, tn(grelu, low[...])), (features, adapter_scale * tn(ada[...], branch_low[...]))):
+        for k in range(8):
+            units[k // 2, k % 2, :, first : first + features] = value[some * k : some * (k + 1)]
+    for i in range(4):
+        unit_send[i] = units[i, 1 - c].astype(bf16)
+    unit_core.start()
     acc[...] += nn(grelu, down[...])
 
     def behind(j, _):
@@ -1241,18 +1286,34 @@
         acc[...] += nt(grad, win[j])
         return 0
 
-    lax.fori_loop(0, steps, behind, 0)
+    lax.fori_loop(0, steps // 2, behind, 0)
+    unit_core.wait()
+    for i in range(3):
+        near_send[i] = (units[i + 1, c] + unit_recv[i + 1].astype(jnp.float32)).astype(bf16)
+    for copy in unit_near:
+        copy.start()
+    lax.fori_loop(steps // 2, steps, behind, 0)
 
     def finish(t, _):
         rows = at(t)
         grad = norm_backward(resid2[rows, :], gain[1:2, :], acc[rows, :])
         grad_two[rows, :] = grad
         small = grad.astype(bf16)
-        dctx_m[rows, :] = nt(small, wco_m[...]).astype(bf16)
+        low[rows, :] = small
         dctx_s[rows, :] = nt(small, wco_o[...]).astype(bf16)
         return 0
 
     lax.fori_loop(0, tiles, finish, 0)
+    dctx_core.start()
+    dctx[mine, :] = nt(low[...], wco_m[...]).astype(bf16)
+    for copy in unit_near:
+        copy.wait()
+    total = units[0, c] + unit_recv[0].astype(jnp.float32)
+    for i in range(3):
+        total = total + near_recv[i].astype(jnp.float32)
+    unit_sum[...] = total
+    out_wait()
+    dctx_core.wait()
 
 
 def feed_call(resid2, cot, gain, bias, wco_m, wco_o, fc_in, fin, fc_out, fout, ad, fad):
@@ -1263,17 +1324,17 @@
     vmem = pl.BlockSpec(memory_space=pltpu.VMEM)
     steps = 4 * fc_in.shape[1] // HIDDEN
     units = 4 * ad.shape[1]
+    some = ad.shape[1] // 2
     return pl.pallas_call(
         feed_kernel,
         out_shape=[
             shape((rows, deep), bf16),
             shape((rows, deep), f32),
-            shape((units, 2 * deep), f32),
-            shape((rows, 512), bf16),
-            shape((rows, 512), bf16),
+            shape((some, 2 * deep), f32),
+            shape((2 * rows, 512), bf16),
         ],
-        in_specs=[vmem] * 6 + [anywhere] * 6,
-        out_specs=[vmem] * 5,
+        in_specs=[vmem, anywhere] + [vmem] * 4 + [anywhere] * 6,
+        out_specs=[anywhere] + [vmem] * 3,
         scratch_shapes=[
             pltpu.VMEM((steps, deep, HIDDEN), bf16),
             pltpu.VMEM((steps, HIDDEN, deep), bf16),
@@ -1287,10 +1348,248 @@
             pltpu.VMEM((rows, units), bf16),
             pltpu.VMEM((rows, deep), bf16),
             pltpu.SemaphoreType.DMA((3, 8)),
+            pltpu.VMEM((rows, deep), bf16),
+            pltpu.VMEM((rows, deep), bf16),
+            pltpu.VMEM((4, 2, some, 2 * deep), f32),
+            pltpu.VMEM((4, some, 2 * deep), bf16),
+            pltpu.VMEM((4, some, 2 * deep), bf16),
+            pltpu.VMEM((3, some, 2 * deep), bf16),
+            pltpu.VMEM((3, some, 2 * deep), bf16),
+            pltpu.VMEM((rows, 512), bf16),
+            pltpu.SemaphoreType.DMA((7,)),
+            pltpu.SemaphoreType.DMA((7,)),
+            pltpu.SemaphoreType.DMA((2,)),
         ],
-        compiler_params=pltpu.CompilerParams(vmem_limit_bytes=60 * 2**20),
+        compiler_params=pltpu.CompilerParams(
+            collective_id=1, has_side_effects=True, vmem_limit_bytes=61 * 2**20
+        ),
         name="feed_forward",
     )(resid2, cot, gain, bias, wco_m, wco_o, fc_in, fin, fc_out, fout, ad, fad)
+
+
+def query_kernel(
+    dq, dkv, wkv, wq_m, wq_o, grad_two, resid1, wso_m, wso_o, gain,
+    grad_one, dctx, mem_sum,
+    dq_o, mem_s, mem_r, dctx_s, low, send, recv,
+):
+    bf16 = jnp.bfloat16
+    place = Place()
+    place.greet((place.to_c,), False)
+    c = place.c
+    half = resid1.shape[0]
+    mine = pl.ds(pl.multiple_of(c * half, half), half)
+    others = pl.ds(pl.multiple_of((1 - c) * half, half), half)
+
+    def there(slot, src, dst):
+        return pltpu.make_async_remote_copy(
+            src_ref=src, dst_ref=dst, send_sem=send.at[slot], recv_sem=recv.at[slot], device_id=place.to_c, device_id_type=MESH
+        )
+
+    dq_core = there(0, dq.at[others], dq_o)
+    mem_core = there(1, mem_s, mem_r)
+    dctx_core = there(2, dctx_s, dctx.at[mine])
+    dq_core.start()
+    tiles = half // TILE
+    at = lambda t: pl.ds(pl.multiple_of(t * TILE, TILE), TILE)
+    place_at = lambda first, t: pl.ds(pl.multiple_of(first * half + t * TILE, TILE), TILE)
+
+    def memory_rows(rows):
+        return sum(nt(dkv[p, rows, :], wkv[p]) for p in range(4))
+
+    def far(t, _):
+        mem_s[at(t), :] = memory_rows(place_at(1 - c, t)).astype(bf16)
+        return 0
+
+    lax.fori_loop(0, tiles, far, 0)
+    mem_core.start()
+    dq_core.wait()
+
+    def one(t, _):
+        rows = at(t)
+        grad_in = grad_two[rows, :] + nt(dq[place_at(c, t), :], wq_m[...]) + nt(dq_o[rows, :], wq_o[...])
+        grad = norm_backward(resid1[rows, :], gain[0:1, :], grad_in)
+        grad_one[rows, :] = grad
+        small = grad.astype(bf16)
+        low[rows, :] = small
+        dctx_s[rows, :] = nt(small, wso_o[...]).astype(bf16)
+        return 0
+
+    lax.fori_loop(0, tiles, one, 0)
+    dctx_core.start()
+    dctx[mine, :] = nt(low[...], wso_m[...]).astype(bf16)
+    mem_core.wait()
+
+    def near(t, _):
+        mem_sum[at(t), :] = (memory_rows(place_at(c, t)) + mem_r[at(t), :].astype(jnp.float32)).astype(bf16)
+        return 0
+
+    lax.fori_loop(0, tiles, near, 0)
+    dctx_core.wait()
+
+
+def query_call(dq, dkv, wkv, wq_m, wq_o, grad_two, resid1, wso_m, wso_o, gain):
+    bf16, f32 = jnp.bfloat16, jnp.float32
+    half, deep = resid1.shape
+    shape = jax.ShapeDtypeStruct
+    vmem = pl.BlockSpec(memory_space=pltpu.VMEM)
+    return pl.pallas_call(
+        query_kernel,
+        out_shape=[shape((half, deep), f32), shape((2 * half, 512), bf16), shape((half, deep), bf16)],
+        in_specs=[vmem] * 10,
+        out_specs=[vmem] * 3,
+        scratch_shapes=[
+            pltpu.VMEM((half, 512), bf16),
+            pltpu.VMEM((half, deep), bf16),
+            pltpu.VMEM((half, deep), bf16),
+            pltpu.VMEM((half, 512), bf16),
+            pltpu.VMEM((half, deep), bf16),
+            pltpu.SemaphoreType.DMA((3,)),
+            pltpu.SemaphoreType.DMA((3,)),
+        ],
+        compiler_params=pltpu.CompilerParams(collective_id=2, has_side_effects=True, vmem_limit_bytes=40 * 2**20),
+        name="query_backward",
+    )(dq, dkv, wkv, wq_m, wq_o, grad_two, resid1, wso_m, wso_o, gain)
+
+
+def last_kernel(
+    planes, dqkv, wself, grad_one, blocks, unit_sum,
+    grad_input, prefix_grad, down_grad, up_grad,
+    part_s, part_r, out_s, out_r, pre_near, pre_sum, pre_z, pre_c, unit_s, unit_z, unit_all, total, send, recv,
+):
+    bf16, f32 = jnp.bfloat16, jnp.float32
+    place = Place()
+    c, x, z = place.c, place.x, place.z
+    steps = []
+    step = 1
+    while step < planes:
+        other = z + step - 2 * step * lax.rem(lax.div(z, step), 2)
+        steps.append((2 * other + c, place.head))
+        step *= 2
+    place.greet([place.to_x, place.to_y, place.to_d, place.to_c] + steps, True)
+    moves = c != x
+    half = grad_one.shape[0]
+    slots = []
+
+    def there(src, dst, device):
+        slot = len(slots)
+        slots.append(slot)
+        return pltpu.make_async_remote_copy(
+            src_ref=src, dst_ref=dst, send_sem=send.at[slot], recv_sem=recv.at[slot], device_id=device, device_id_type=MESH
+        )
+
+    tiles = half // TILE
+    at = lambda t: pl.ds(t * TILE, TILE)
+    place_at = lambda first, t: pl.ds(pl.multiple_of(first * half + t * TILE, TILE), TILE)
+    pre_copies = [
+        there(blocks.at[i + 1], pre_near.at[i], device) for i, device in enumerate((place.to_x, place.to_y, place.to_d))
+    ]
+    pre_steps = [there(pre_sum.at[i], pre_z.at[i], device) for i, device in enumerate(steps)]
+    pre_core = there(pre_sum.at[len(steps)], pre_c, place.to_c)
+    unit_steps = [there(unit_s.at[i], unit_z.at[i], device) for i, device in enumerate(steps)]
+    unit_core = there(unit_s.at[len(steps)], unit_z.at[len(steps)], place.to_c)
+    part_copies = [there(part_s.at[at(t)], part_r.at[at(t)], place.to_c) for t in range(tiles)]
+    out_copies = [there(out_s.at[at(t)], out_r.at[at(t)], place.to_s) for t in range(tiles)]
+    for copy in pre_copies:
+        copy.start()
+    unit_s[0] = unit_sum[...].astype(bf16)
+    unit_steps[0].start()
+
+    def input_rows(rows):
+        return sum(nt(dqkv[p, rows, :], wself[p]) for p in range(4))
+
+    part_s[at(0), :] = input_rows(place_at(1 - c, 0)).astype(bf16)
+    part_copies[0].start()
+    for copy in pre_copies:
+        copy.wait()
+    pre_sum[0] = blocks[0] + pre_near[0] + pre_near[1] + pre_near[2]
+    pre_steps[0].start()
+    for t in range(1, tiles):
+        part_s[at(t), :] = input_rows(place_at(1 - c, t)).astype(bf16)
+        part_copies[t].start()
+
+    def advance(i):
+        pre_steps[i].wait()
+        pre_sum[i + 1] = pre_sum[i] + pre_z[i]
+        if i + 1 < len(steps):
+            pre_steps[i + 1].start()
+        else:
+            pre_core.start()
+        unit_steps[i].wait()
+        unit_s[i + 1] = (unit_s[i].astype(f32) + unit_z[i].astype(f32)).astype(bf16)
+        if i + 1 < len(steps):
+            unit_steps[i + 1].start()
+        else:
+            unit_core.start()
+
+    for t in range(tiles):
+        part_copies[t].wait()
+        total[at(t), :] = input_rows(place_at(c, t)) + part_r[at(t), :].astype(f32) + grad_one[at(t), :]
+        out_s[at(t), :] = total[at(t), :].astype(bf16)
+        pl.when(moves)(out_copies[t].start)
+        if t < len(steps):
+            advance(t)
+    for i in range(tiles, len(steps)):
+        advance(i)
+    pre_core.wait()
+    unit_core.wait()
+    my_lanes = pl.ds(pl.multiple_of(c * 128, 128), 128)
+    other_lanes = pl.ds(pl.multiple_of((1 - c) * 128, 128), 128)
+    prefix_grad[:, :, my_lanes] = pre_sum[len(steps)]
+    prefix_grad[:, :, other_lanes] = pre_c[...]
+    some = unit_sum.shape[0]
+    unit_all[pl.ds(pl.multiple_of(c * some, some), some), :] = unit_s[len(steps)].astype(f32)
+    unit_all[pl.ds(pl.multiple_of((1 - c) * some, some), some), :] = unit_z[len(steps)].astype(f32)
+    features = grad_one.shape[1]
+    down_grad[...] = unit_all[:, 0:features].T
+    up_grad[...] = unit_all[:, features : 2 * features]
+
+    @pl.when(moves)
+    def _():
+        for copy in out_copies:
+            copy.wait()
+        grad_input[...] = out_r[...].astype(f32)
+
+    @pl.when(jnp.logical_not(moves))
+    def _():
+        grad_input[...] = total[...]
+
+
+def last_call(planes, dqkv, wself, grad_one, blocks, unit_sum):
+    bf16, f32 = jnp.bfloat16, jnp.float32
+    half, deep = grad_one.shape
+    some = unit_sum.shape[0]
+    count = planes.bit_length() - 1
+    shape = jax.ShapeDtypeStruct
+    vmem = pl.BlockSpec(memory_space=pltpu.VMEM)
+    return pl.pallas_call(
+        functools.partial(last_kernel, planes),
+        out_shape=[
+            shape((half, deep), f32),
+            shape((2, 32, 256), f32),
+            shape((deep, 2 * some), f32),
+            shape((2 * some, deep), f32),
+        ],
+        in_specs=[vmem] * 5,
+        out_specs=[vmem] * 4,
+        scratch_shapes=[
+            pltpu.VMEM((half, deep), bf16),
+            pltpu.VMEM((half, deep), bf16),
+            pltpu.VMEM((half, deep), bf16),
+            pltpu.VMEM((half, deep), bf16),
+            pltpu.VMEM((3, 2, 32, 128), f32),
+            pltpu.VMEM((count + 1, 2, 32, 128), f32),
+            pltpu.VMEM((count, 2, 32, 128), f32),
+            pltpu.VMEM((2, 32, 128), f32),
+            pltpu.VMEM((count + 1, some, 2 * deep), bf16),
+            pltpu.VMEM((count + 1, some, 2 * deep), bf16),
+            pltpu.VMEM((2 * some, 2 * deep), f32),
+            pltpu.VMEM((half, deep), f32),
+            pltpu.SemaphoreType.DMA((3 + 2 * count + 2 + 2 * (half // TILE),)),
+            pltpu.SemaphoreType.DMA((3 + 2 * count + 2 + 2 * (half // TILE),)),
+        ],
+        compiler_params=pltpu.CompilerParams(collective_id=3, has_side_effects=True, vmem_limit_bytes=40 * 2**20),
+        name="last_sums",
+    )(dqkv, wself, grad_one, blocks, unit_sum)
 
 
 AXES = ("rows", "heads")
@@ -1314,28 +1613,13 @@
     return found
 
 
-class Moves:
-    def __init__(self, rows):
-        def perm(move):
-            table = pairs_of(rows, move)
-            return lambda value: lax.ppermute(value, AXES, table)
-
-        self.core = perm(lambda z, c, y, x: (z, 1 - c, y, x))
-        self.x = perm(lambda z, c, y, x: (z, c, y, 1 - x))
-        self.y = perm(lambda z, c, y, x: (z, c, 1 - y, x))
-        self.d = perm(lambda z, c, y, x: (z, c, 1 - y, 1 - x))
-        crossing = [pair for pair in pairs_of(rows, lambda z, c, y, x: (z, x, y, c)) if pair[0] != pair[1]]
-
-        def swap(value):
-            stays = lax.axis_index("rows") % 2 == lax.axis_index("heads") % 2
-            return jnp.where(stays, value, lax.ppermute(value, AXES, crossing))
-
-        self.swap = swap
-        self.z = []
-        step = 1
-        while step < rows // 2:
-            self.z.append(perm(lambda z, c, y, x, step=step: (z ^ step, c, y, x)))
-            step *= 2
+def swap_in(rows, value):
+    def swapped(z, c, y, x):
+        return (z, x, y, c)
+
+    crossing = [pair for pair in pairs_of(rows, swapped) if pair[0] != pair[1]]
+    stays = lax.axis_index("rows") % 2 == lax.axis_index("heads") % 2
+    return jnp.where(stays, value, lax.ppermute(value, AXES, crossing))
 
 
 def fast_body(
@@ -1358,10 +1642,6 @@
     ln_gain,
     ln_bias,
 ):
-    bf16 = jnp.bfloat16
-    f32 = jnp.float32
-    move = Moves(rows)
-    core = lax.axis_index("rows") % 2
     count = prefix.shape[1]
     ad = jnp.stack([ad_down.T, ad_up])
     held = forward_call(
@@ -1381,87 +1661,24 @@
         ln_gain,
         ln_bias,
     )
-    half = tokens.shape[0]
-
-    def own_rows(value):
-        return lax.dynamic_slice_in_dim(value, core * half, half, 0)
-
-    def other_rows(value):
-        return lax.dynamic_slice_in_dim(value, (1 - core) * half, half, 0)
-
-    def whole(mine, others):
-        return jnp.where(
-            core == 0,
-            jnp.concatenate([mine, others], axis=0),
-            jnp.concatenate([others, mine], axis=0),
-        )
-
-    def after(value, *earlier):
-        return lax.optimization_barrier((value,) + earlier)[0]
-
-    out, grad_two, unit_grads, dctx_m, dctx_s = feed_call(
-        held.resid2, move.swap(cotangent), ln_gain, ln_bias, held.wco_m, held.wco_o,
+    output, grad_two, unit_sum, cross_dctx = feed_call(
+        held.resid2, cotangent, ln_gain, ln_bias, held.wco_m, held.wco_o,
         fc_in, held.fin, fc_out, held.fout, ad, held.fad,
     )
-    output = move.swap(out)
-    units = ad.shape[1] // 2
-    unit_grads = unit_grads.reshape(4, 2, units, -1)
-    unit_mine = lax.dynamic_index_in_dim(unit_grads, core, 1, keepdims=False)
-    unit_other = lax.dynamic_index_in_dim(unit_grads, 1 - core, 1, keepdims=False)
-    unit_mine = unit_mine + move.core(unit_other.astype(bf16)).astype(f32)
-    low_pieces = unit_mine.astype(bf16)
-    unit_sum = (
-        unit_mine[0]
-        + move.x(low_pieces[1]).astype(f32)
-        + move.y(low_pieces[2]).astype(f32)
-        + move.d(low_pieces[3]).astype(f32)
-    )
-
-    cross_dctx = whole(dctx_m, move.core(dctx_s))
-    cross_dctx = after(cross_dctx, unit_sum)
     cross_dq, cross_dkv = backward_call(
         False, (held.q, held.kv), held.bounds, held.cctx, cross_dctx, held.clse
     )
-    got = move.core(other_rows(cross_dq))
-    resid_one = held.resid1
-    grad_one_in = grad_two + dot_right(own_rows(cross_dq), held.wq_m) + dot_right(got, held.wq_o)
-    memory_part = sum(dot_right(cross_dkv[i], held.wkv[i]) for i in range(4))
-    memory_sum = own_rows(memory_part) + move.core(other_rows(memory_part).astype(bf16)).astype(f32)
-    grad_memory = move.swap(memory_sum.astype(bf16)).astype(f32)
-    grad_one = norm_backward(resid_one, ln_gain[0], grad_one_in)
-
-    low_grad_one = grad_one.astype(bf16)
-    d_send = dot_right(low_grad_one, held.wso_o).astype(bf16)
-    self_dctx = whole(dot_right(low_grad_one, held.wso_m).astype(bf16), move.core(d_send))
+    grad_one, self_dctx, memory_sum = query_call(
+        cross_dq, cross_dkv, held.wkv, held.wq_m, held.wq_o, grad_two, held.resid1, held.wso_m, held.wso_o, ln_gain
+    )
+    grad_memory = swap_in(rows, memory_sum).astype(jnp.float32)
     self_dqkv, prefix_blocks = backward_call(
         True, (held.qkv,), held.bounds, held.sctx, self_dctx, held.slse, held.pre
     )
-    input_part = sum(dot_right(self_dqkv[i], held.wself[i]) for i in range(4))
-    input_sum = own_rows(input_part) + move.core(other_rows(input_part).astype(bf16)).astype(f32) + grad_one
-    grad_input = move.swap(input_sum.astype(bf16)).astype(f32)
-    unit_sum = after(unit_sum, self_dqkv)
-    for step in move.z:
-        unit_sum = unit_sum + step(unit_sum.astype(bf16)).astype(f32)
-    unit_all = whole(unit_sum, move.core(unit_sum.astype(bf16)).astype(f32))
-    features = tokens.shape[1]
-    down_grad = unit_all[:, :features].T
-    up_grad = unit_all[:, features:]
-
-    prefix_sum = (
-        prefix_blocks[0]
-        + move.x(prefix_blocks[1])
-        + move.y(prefix_blocks[2])
-        + move.d(prefix_blocks[3])
-    )
-    for step in move.z:
-        prefix_sum = prefix_sum + step(prefix_sum)
-    prefix_other = move.core(prefix_sum)
-    prefix_grad = jnp.where(
-        core == 0,
-        jnp.concatenate([prefix_sum, prefix_other], axis=2),
-        jnp.concatenate([prefix_other, prefix_sum], axis=2),
-    )[:, :count]
-    return (output, grad_input, grad_memory, prefix_grad, down_grad, up_grad)
+    grad_input, prefix_grad, down_grad, up_grad = last_call(
+        rows // 2, self_dqkv, held.wself, grad_one, prefix_blocks, unit_sum
+    )
+    return (output, grad_input, grad_memory, prefix_grad[:, :count], down_grad, up_grad)
 
 
 def solution(mesh):

time: 358 us -> 330 us (0.922)
  Pallas kernels: 243 us -> 300 us
  starting transfers between devices: 43.6 us -> 1.91 us
  waiting for transfers between devices: 28 us -> 0.01 us
  matrix products: 12.1 us -> 0 us
  other arithmetic: 15.8 us -> 4.56 us
  local copies, waits for them, and re-layouts: 12.6 us -> 20 us
    ppermute x22 -> x1, starting transfers between devices: 43.6 us -> 1.91 us  [swap_in(): return jnp.where(stays, value, lax.ppermute(value, AXES, crossing))]
    pallas_call x0 -> x2, Pallas kernels: none -> 37.3 us  [the longest x1 25.4 us: last_call(): pl.pallas_call(functools.partial(last_kernel, planes), out_shape=[shape((...]
    ppermute x22 -> x1, waiting for transfers between devices: 28 us -> 0.01 us  [swap_in(): return jnp.where(stays, value, lax.ppermute(value, AXES, crossing))]
    pallas_call x2, Pallas kernels: 65.9 us -> 78 us  [backward_call(): pl.pallas_call(functools.partial(backward_kernel, has_prefix, 0 if has_pr...]
    dot_general x12 -> x0, matrix products: 12.1 us -> none  [dot_right(): lax.dot_general(left, right, (((1,), (1,)), ((), ())), preferred_element_...]
    unnamed x44 -> x61, local copies, waits for them, and re-layouts: 7.75 us -> 19.4 us
    pallas_call x1, Pallas kernels: 41.7 us -> 49.7 us  [feed_call(): pl.pallas_call(feed_kernel, out_shape=[shape((rows, deep), bf16), shape((...]
    convert_element_type x9 -> x1, other arithmetic: 8.38 us -> 2.77 us  [fast_body(): grad_memory = swap_in(rows, memory_sum).astype(jnp.float32)]
  transfers between devices with their start and end apart: 22 -> 1, of which waited for: 7 -> 0; matrix products, arithmetic and copies ran while one was open for 8% -> 0% of each run, Pallas kernels for 57% -> 18%
where the time goes in v4:
time: 330 us; the launch traced here: 327 us
  Pallas kernels  300 us (91%)
  local copies, waits for them, and re-layouts  20 us (6%)
  other arithmetic  4.56 us (1%)
    pallas_call x1, Pallas kernels, forward_call(): pl.pallas_call(forward_kernel, out_shape=outs, in_specs=[anywhere] * 13 +...  135 us
    pallas_call x2, Pallas kernels, backward_call(): pl.pallas_call(functools.partial(backward_kernel, has_prefix, 0 if has_pr...  78 us
    pallas_call x1, Pallas kernels, feed_call(): pl.pallas_call(feed_kernel, out_shape=[shape((rows, deep), bf16), shape((...  49.7 us
    pallas_call x1, Pallas kernels, last_call(): pl.pallas_call(functools.partial(last_kernel, planes), out_shape=[shape((...  25.4 us
    unnamed x61, local copies, waits for them, and re-layouts  19.4 us
    pallas_call x1, Pallas kernels, query_call(): pl.pallas_call(query_kernel, out_shape=[shape((half, deep), f32), shape((...  11.9 us
  transfers between devices with their start and end apart: 1, of which 0 were waited for; matrix products, arithmetic and copies ran while one was open for 0% of the time, Pallas kernels for 18%

profile of v4, /device:TPU:1, one launch (start us, length us, event | category | flops | bytes accessed | tf_op | source)
XLA Modules:
  0.0 327.3 jit_solution(17687931668571139373)
XLA Ops:
  0.6 1.1 copy.24
  2.5 1.8 pad_maximum_fusion.ad
  4.9 135.0 %layer_forward.1 = (bf16[4,1024,384]{2,1,0:T(8,128)(2,1)}, bf16[4,1024,384]{2,1,0:T(8,128)(2,1)}, bf16[1024,512]{1,0:T(8,128)(2,1)}, f32[4,8,1024]{2,1,0:T(8,128...) custom-call(bf16[512,1024]{1,0:T(8,128)(2,1)} %tokens.1, ...), custom_call_target="tpu_custom_call" | custom-call | tf_op jit(solution)/shard_map/layer_forward/pallas_call | solution.py:1013
  139.9 49.7 %feed_forward.1 = (bf16[512,1024]{1,0:T(8,128)(2,1)}, f32[512,1024]{1,0:T(8,128)}, f32[64,2048]{1,0:T(8,128)}, bf16[1024,512]{1,0:T(8,128)(2,1)}) custom-call(f32[512,1024]{1,0:T(8,128)} %get-tuple-element.43.resid2, bf16[512,1024]{1,0:T(8,128)(2,1)} %cotangent.1, f32[3,1024]{1,0:T(4,128)} %gain.5, f32[3,1024]{1,0:T(4,128)} %bias.3, ...), custom_call_target="tpu_custom_call" | custom-call | tf_op jit(solution)/shard_map/feed_forward/pallas_call | solution.py:1328
  189.6 1.2 copy-done.19
  190.8 1.2 copy-done.20
  192.1 1.2 copy-done.21
  193.3 43.3 %cross_backward.1 = (bf16[1024,512]{1,0:T(8,128)(2,1)S(1)}, bf16[4,1024,256]{2,1,0:T(8,128)(2,1)S(1)}) custom-call(s32[8,1024]{1,0:T(8,128)S(1)} %copy-done.25, bf16[1024,512]{1,0:T(8,128)(2,1)S(1)} %copy-done.19, bf16[4,1024,256]{2,1,0:T(8,128)(2,1)S(1)} %copy-done.15, s32[8,1024]{1,0:T(8,128)S(1)} %copy-done.25, bf16[1024,512]{1,0:T(8,128)(2,1)S(1)} %copy-done.20, ...), custom_call_target="tpu_custom_call" | custom-call | flops 5368709120 | bytes 10485760 | tf_op jit(solution)/shard_map/cross_backward/pallas_call | solution.py:1146
  236.7 11.9 %query_backward.1 = (f32[512,1024]{1,0:T(8,128)S(1)}, bf16[1024,512]{1,0:T(8,128)(2,1)S(1)}, bf16[512,1024]{1,0:T(8,128)(2,1)S(1)}) custom-call(bf16[1024,512]{1,0:T(8,128)(2,1)S(1)} %get-tuple-element.58.dq, bf16[4,1024,256]{2,1,0:T(8,128)(2,1)S(1)} %get-tuple-element.59.dkv, bf16[4,1024,256]{2,1,0:T(8,128)(2,1)S(1)} %copy-done.3, ...), custom_call_target="tpu_custom_call" | custom-call | tf_op jit(solution)/shard_map/query_backward/pallas_call | solution.py:1435
  248.6 1.0 copy-done.17
  249.6 1.9 collective-permute-start
  251.5 1.9 copy-done.14
  253.4 1.2 copy-done.16
  254.6 1.2 copy-done.18
  255.9 34.7 %self_backward.1 = (bf16[4,1024,384]{2,1,0:T(8,128)(2,1)S(1)}, f32[4,2,32,128]{3,2,1,0:T(8,128)S(1)}) custom-call(s32[8,1024]{1,0:T(8,128)S(1)} %copy-done.25, bf16[4,1024,384]{2,1,0:T(8,128)(2,1)S(1)} %copy-done.14, s32[8,1024]{1,0:T(8,128)S(1)} %copy-done.25, bf16[1024,512]{1,0:T(8,128)(2,1)S(1)} %copy-done.16, bf16[1024,512]{1,0:T(8,128)(2,1)S(1)} %copy-done.18, ...), custom_call_target="tpu_custom_call" | custom-call | flops 5368709120 | bytes 10485760 | tf_op jit(solution)/shard_map/self_backward/pallas_call | solution.py:1146
  290.6 25.4 %last_sums.1 = (f32[512,1024]{1,0:T(8,128)S(1)}, f32[2,32,256]{2,1,0:T(8,128)S(1)}, f32[1024,128]{1,0:T(8,128)S(1)}, f32[128,1024]{1,0:T(8,128)S(1)}) custom-call(bf16[4,1024,384]{2,1,0:T(8,128)(2,1)S(1)} %get-tuple-element.70.dqkv, bf16[4,1024,384]{2,1,0:T(8,128)(2,1)S(1)} %copy-done, f32[512,1024]{1,0:T(8,128)S(1)} %get-tuple-element.72.grad_one, ...), custom_call_target="tpu_custom_call" | custom-call | tf_op jit(solution)/shard_map/last_sums/pallas_call | solution.py:1564
  316.0 1.3 copy-done.1
  317.3 0.8 copy-done.9
  319.6 2.8 select_convert_fusion
  322.3 1.0 copy.30
  323.3 1.0 copy-done.2
  324.3 1.3 copy.31
  325.7 0.8 copy.32
  326.5 0.8 copy.33
  (48 shorter events, 3.0 us)
Async XLA Ops:
  139.9 49.7 %copy-start.15 = (bf16[4,1024,256]{2,1,0:T(8,128)(2,1)S(1)}, bf16[4,1024,256]{2,1,0:T(8,128)(2,1)}, u32[]{:S(2)}) copy-start(bf16[4,1024,256]{2,1,0:T(8,128)(2,1)} %get-tuple-element.54.refs_1_) | copy-start | bytes 6291460
  139.9 49.7 %copy-start.23 = (f32[4,8,1024]{2,1,0:T(8,128)S(1)}, f32[4,8,1024]{2,1,0:T(8,128)}, u32[]{:S(2)}) copy-start(f32[4,8,1024]{2,1,0:T(8,128)} %get-tuple-element.57.refs_5_) | copy-start | bytes 393220
  139.9 49.7 %copy-start.25 = (s32[8,1024]{1,0:T(8,128)S(1)}, s32[8,1024]{1,0:T(8,128)}, u32[]{:S(2)}) copy-start(s32[8,1024]{1,0:T(8,128)} %get-tuple-element.50.bounds_s.refs_2_.refs_1_) | copy-start | bytes 98308
  189.6 1.2 copy-start.19
  192.1 1.2 copy-start.21
  193.3 43.3 %copy-start.3 = (bf16[4,1024,256]{2,1,0:T(8,128)(2,1)S(1)}, bf16[4,1024,256]{2,1,0:T(8,128)(2,1)}, u32[]{:S(2)}) copy-start(bf16[4,1024,256]{2,1,0:T(8,128)(2,1)} %get-tuple-element.60.wkv) | copy-start | bytes 6291460
  193.3 43.4 %copy-start.4 = (bf16[512,1024]{1,0:T(8,128)(2,1)S(1)}, bf16[512,1024]{1,0:T(8,128)(2,1)}, u32[]{:S(2)}) copy-start(bf16[512,1024]{1,0:T(8,128)(2,1)} %get-tuple-element.65.wso_m) | copy-start | bytes 3145732
  193.3 43.4 %copy-start.5 = (bf16[512,1024]{1,0:T(8,128)(2,1)S(1)}, bf16[512,1024]{1,0:T(8,128)(2,1)}, u32[]{:S(2)}) copy-start(bf16[512,1024]{1,0:T(8,128)(2,1)} %get-tuple-element.66.wso_o) | copy-start | bytes 3145732
  193.3 43.4 %copy-start.6 = (bf16[1024,512]{1,0:T(8,128)(2,1)S(1)}, bf16[1024,512]{1,0:T(8,128)(2,1)}, u32[]{:S(2)}) copy-start(bf16[1024,512]{1,0:T(8,128)(2,1)} %get-tuple-element.61.wq_m) | copy-start | bytes 3145732
  193.3 43.4 %copy-start.7 = (bf16[1024,512]{1,0:T(8,128)(2,1)S(1)}, bf16[1024,512]{1,0:T(8,128)(2,1)}, u32[]{:S(2)}) copy-start(bf16[1024,512]{1,0:T(8,128)(2,1)} %get-tuple-element.62.wq_o) | copy-start | bytes 3145732
  193.3 43.4 %copy-start.13 = (f32[3,1024]{1,0:T(4,128)S(1)}, f32[3,1024]{1,0:T(4,128)}, u32[]{:S(2)}) copy-start(f32[3,1024]{1,0:T(4,128)} %gain.5) | copy-start | bytes 36868
  236.7 14.8 %copy-start.22 = (f32[4,8,1024]{2,1,0:T(8,128)S(1)}, f32[4,8,1024]{2,1,0:T(8,128)}, u32[]{:S(2)}) copy-start(f32[4,8,1024]{2,1,0:T(8,128)} %get-tuple-element.68.refs_4_) | copy-start | bytes 393220
  236.7 14.8 %copy-start.24 = (bf16[4,2,32,128]{3,2,1,0:T(8,128)(2,1)S(1)}, bf16[4,2,32,128]{3,2,1,0:T(8,128)(2,1)}, u32[]{:S(2)}) copy-start(bf16[4,2,32,128]{3,2,1,0:T(8,128)(2,1)} %get-tuple-element.69.refs_5_) | copy-start | bytes 196612
  249.6 70.0 %collective-permute-start = (bf16[512,1024]{1,0:T(8,128)(2,1)S(1)}, bf16[512,1024]{1,0:T(8,128)(2,1)}, u32[]{:S(2)}, u32[]{:S(2)}) collective-permute-start(bf16[512,1024]{1,0:T(8,128)(2,1)S(1)} %get-tuple-element.76), channel_id=1, source_target_pairs={{1,4},{3,6},{4,1},{6,3},{9,12},{11,14},{12,9},{14,11},{17,20},{19,... | collective-permute-start | bytes 3145736 | tf_op jit(solution)/shard_map/ppermute | solution.py:1622
  251.5 1.9 copy-start.14
  253.4 1.2 copy-start.16
  254.6 1.2 copy-start.18
  255.9 34.7 %copy-start = (bf16[4,1024,384]{2,1,0:T(8,128)(2,1)S(1)}, bf16[4,1024,384]{2,1,0:T(8,128)(2,1)}, u32[]{:S(2)}) copy-start(bf16[4,1024,384]{2,1,0:T(8,128)(2,1)} %get-tuple-element.71.wself) | copy-start | bytes 9437188
  255.9 34.7 %copy-start.8 = (f32[64,2048]{1,0:T(8,128)S(1)}, f32[64,2048]{1,0:T(8,128)}, u32[]{:S(2)}) copy-start(f32[64,2048]{1,0:T(8,128)} %get-tuple-element.74.unit_sum) | copy-start | bytes 1572868
  316.0 1.3 copy-start.1
  319.5 2.8 copy-start.26
  322.3 2.0 copy-start.2
  324.3 1.4 copy-start.12
  324.3 2.2 copy-start.10
  (4 other events, 3.8 us)

commit v5 on v4

--- a/solution.py
+++ b/solution.py
@@ -1024,103 +1024,114 @@
     return Held(*results)
 
 
+TOGETHER = 4
+
+
 def backward_kernel(has_prefix, first_bound, bounds_s, *refs):
     if has_prefix:
-        qkv_ref, bounds, ctx_ref, dctx_ref, lse_ref, pre_ref, dqkv_ref, dpre_ref, kt_ref, dk_acc, dv_acc, dq_acc, dpre_acc = refs
-        q_at = lambda rows: qkv_ref[0, rows, 0:128]
-        k_at = lambda rows: qkv_ref[0, rows, 128:256]
-        v_at = lambda rows: qkv_ref[0, rows, 256:384]
+        qkv_ref, bounds, ctx_ref, dctx_ref, lse_ref, pre_ref, dqkv_ref, dpre_ref, dk_acc, dv_acc, dq_acc, dpre_acc = refs
+        q_at = lambda g, rows: qkv_ref[g, rows, 0:128]
+        k_at = lambda g, rows: qkv_ref[g, rows, 128:256]
+        v_at = lambda g, rows: qkv_ref[g, rows, 256:384]
     else:
-        q_ref, kv_ref, bounds, ctx_ref, dctx_ref, lse_ref, dq_ref, dkv_ref, kt_ref, dk_acc, dv_acc, dq_acc = refs
-        q_at = lambda rows: q_ref[rows, :]
-        k_at = lambda rows: kv_ref[0, rows, 0:128]
-        v_at = lambda rows: kv_ref[0, rows, 128:256]
+        q_ref, kv_ref, bounds, ctx_ref, dctx_ref, lse_ref, dq_ref, dkv_ref, dk_acc, dv_acc, dq_acc = refs
+        q_at = lambda g, rows: q_ref[rows, 128 * g : 128 * g + 128]
+        k_at = lambda g, rows: kv_ref[g, rows, 0:128]
+        v_at = lambda g, rows: kv_ref[g, rows, 128:256]
     scale = 0.125 * LOG2E
-    kt_ref[...] = k_at(slice(None)).astype(jnp.float32).T.astype(jnp.bfloat16)
     dk_acc[...] = jnp.zeros_like(dk_acc)
     dv_acc[...] = jnp.zeros_like(dv_acc)
+    kps, vps = [], []
+    for g in range(TOGETHER):
+        if has_prefix:
+            kps.append(prefix_block(pre_ref[g, 0]))
+            vps.append(prefix_block(pre_ref[g, 1]))
     if has_prefix:
         dpre_acc[...] = jnp.zeros_like(dpre_acc)
-        kp = prefix_block(pre_ref[0, 0])
-        vp = prefix_block(pre_ref[0, 1])
-        kpt = kp.astype(jnp.float32).T.astype(jnp.bfloat16)
 
     def one(qi, _):
         q0 = pl.multiple_of(qi * QB, QB)
         span = pl.ds(q0, QB)
-        q = q_at(span)
-        dctx = dctx_ref[span, :]
         lo = bounds[first_bound : first_bound + 1, span]
         hi = bounds[first_bound + 1 : first_bound + 2, span]
-        prod = (dctx.astype(jnp.float32) * ctx_ref[span, :].astype(jnp.float32)).T
-        inner = [jnp.sum(prod[h * 64 : h * 64 + 64], axis=0, keepdims=True) for h in range(2)]
-        lse = [lse_ref[0, h : h + 1, span] for h in range(2)]
-        qh = [half_lanes(q, h) for h in range(2)]
-        dh = [half_lanes(dctx, h) for h in range(2)]
-        if has_prefix:
-            sp = prefix_rows(nt(kp, q) * scale)
-            rows = lambda pair: jnp.concatenate([jnp.broadcast_to(t, (64, QB)) for t in pair], axis=0)
-            pp = jnp.exp2(sp - rows(lse))
-            dpp = nt(vp, dctx)
-            dsp = (pp * (dpp - rows(inner))).astype(jnp.bfloat16)
-            dpre_acc[0] += nn(dsp, q)
-            dpre_acc[1] += nn(pp.astype(jnp.bfloat16), dctx)
-            dq_acc[...] = nn(kpt, dsp)
-        else:
-            dq_acc[...] = jnp.zeros_like(dq_acc)
+        inner, lse, qh, dh = [], [], [], []
+        for g in range(TOGETHER):
+            q = q_at(g, span)
+            dctx = dctx_ref[span, 128 * g : 128 * g + 128]
+            ctx = ctx_ref[span, 128 * g : 128 * g + 128]
+            prod = (dctx.astype(jnp.float32) * ctx.astype(jnp.float32)).T
+            inner.append([jnp.sum(prod[h * 64 : h * 64 + 64], axis=0, keepdims=True) for h in range(2)])
+            lse.append([lse_ref[g, h : h + 1, span] for h in range(2)])
+            qh.append([half_lanes(q, h) for h in range(2)])
+            dh.append([half_lanes(dctx, h) for h in range(2)])
+            if has_prefix:
+                sp = prefix_rows(nt(kps[g], q) * scale)
+                rows = lambda pair: jnp.concatenate([jnp.broadcast_to(t, (64, QB)) for t in pair], axis=0)
+                pp = jnp.exp2(sp - rows(lse[g]))
+                dpp = nt(vps[g], dctx)
+                dsp = (pp * (dpp - rows(inner[g]))).astype(jnp.bfloat16)
+                dpre_acc[g, 0] += nn(dsp, q)
+                dpre_acc[g, 1] += nn(pp.astype(jnp.bfloat16), dctx)
+                dq_acc[g] = tn(dsp, kps[g])
+            else:
+                dq_acc[g] = jnp.zeros((QB, 128), jnp.float32)
 
         def chunk(ki, _):
             k0 = pl.multiple_of(ki * KB, KB)
             keys = pl.ds(k0, KB)
-            k = k_at(keys)
-            v = v_at(keys)
             pos = k0 + lax.broadcasted_iota(jnp.int32, (KB, QB), 0)
             mask = (pos >= lo) & (pos <= hi)
-            ps, dss = [], []
-            for h in range(2):
-                s = nt(k, qh[h]) * scale
-                p = jnp.exp2(jnp.where(mask, s, NEG) - lse[h])
-                dp = nt(v, dh[h])
-                ds = (p * (dp - inner[h])).astype(jnp.bfloat16)
-                ps.append(p.astype(jnp.bfloat16))
-                dss.append(ds)
-                dq_acc[h * 64 : h * 64 + 64, :] += nn(kt_ref[h * 64 : h * 64 + 64, keys], ds)
-            dv_acc[keys, :] += nn(ps[0], dh[0]) + nn(ps[1], dh[1])
-            dk_acc[keys, :] += nn(dss[0], qh[0]) + nn(dss[1], qh[1])
+            for g in range(TOGETHER):
+                k = k_at(g, keys)
+                v = v_at(g, keys)
+                ps, dss = [], []
+                for h in range(2):
+                    s = nt(k, qh[g][h]) * scale
+                    p = jnp.exp2(jnp.where(mask, s, NEG) - lse[g][h])
+                    dp = nt(v, dh[g][h])
+                    ds = (p * (dp - inner[g][h])).astype(jnp.bfloat16)
+                    ps.append(p.astype(jnp.bfloat16))
+                    dss.append(ds)
+                dv_acc[g, keys, :] += nn(jnp.concatenate(ps, axis=1), jnp.concatenate(dh[g], axis=0))
+                dq_acc[g] += tn(jnp.concatenate(dss, axis=0), jnp.concatenate([half_lanes(k, 0), half_lanes(k, 1)], axis=0))
+                dk_acc[g, keys, :] += nn(jnp.concatenate(dss, axis=1), jnp.concatenate(qh[g], axis=0))
             return 0
 
         lowest = lax.div(bounds_s[first_bound, q0], KB)
         highest = lax.div(bounds_s[first_bound + 1, q0 + QB - 1], KB) + 1
         lax.fori_loop(lowest, highest, chunk, 0)
-        dq = (dq_acc[...].T * 0.125).astype(jnp.bfloat16)
+        for g in range(TOGETHER):
+            dq = (dq_acc[g] * 0.125).astype(jnp.bfloat16)
+            if has_prefix:
+                dqkv_ref[g, span, 0:128] = dq
+            else:
+                dq_ref[span, 128 * g : 128 * g + 128] = dq
+        return 0
+
+    lax.fori_loop(0, SEQ // QB, one, 0)
+    for g in range(TOGETHER):
+        dk = (dk_acc[g] * 0.125).astype(jnp.bfloat16)
+        dv = dv_acc[g].astype(jnp.bfloat16)
         if has_prefix:
-            dqkv_ref[0, span, 0:128] = dq
+            dqkv_ref[g, :, 128:256] = dk
+            dqkv_ref[g, :, 256:384] = dv
+            lane = lax.broadcasted_iota(jnp.int32, (32, 128), 1)
+            for i, factor in ((0, 0.125), (1, 1.0)):
+                dpre_ref[g, i] = jnp.where(lane < 64, dpre_acc[g, i, 0:32], dpre_acc[g, i, 64:96]) * factor
         else:
-            dq_ref[span, :] = dq
-        return 0
-
-    lax.fori_loop(0, SEQ // QB, one, 0)
-    dk = (dk_acc[...] * 0.125).astype(jnp.bfloat16)
-    dv = dv_acc[...].astype(jnp.bfloat16)
-    if has_prefix:
-        dqkv_ref[0, :, 128:256] = dk
-        dqkv_ref[0, :, 256:384] = dv
-        lane = lax.broadcasted_iota(jnp.int32, (32, 128), 1)
-        for i, factor in ((0, 0.125), (1, 1.0)):
-            dpre_ref[0, i] = jnp.where(lane < 64, dpre_acc[i, 0:32], dpre_acc[i, 64:96]) * factor
-    else:
-        dkv_ref[0, :, 0:128] = dk
-        dkv_ref[0, :, 128:256] = dv
+            dkv_ref[g, :, 0:128] = dk
+            dkv_ref[g, :, 128:256] = dv
 
 
 def backward_call(has_prefix, arrays, bounds, ctx, dctx, lse, pre=None):
-    col = pl.BlockSpec((SEQ, 128), lambda j, *_: (0, j))
-    piece = lambda width: pl.BlockSpec((1, SEQ, width), lambda j, *_: (j, 0, 0))
+    col = pl.BlockSpec((SEQ, 128 * TOGETHER), lambda j, *_: (0, j))
+    piece = lambda width: pl.BlockSpec((TOGETHER, SEQ, width), lambda j, *_: (j, 0, 0))
     shape = jax.ShapeDtypeStruct
     bf16, f32 = jnp.bfloat16, jnp.float32
+    pre_spec = pl.BlockSpec((TOGETHER, 2, 32, 128), lambda j, *_: (j, 0, 0, 0))
     if has_prefix:
         in_specs = [piece(384)]
-        out_specs = [piece(384), pl.BlockSpec((1, 2, 32, 128), lambda j, *_: (j, 0, 0, 0))]
+        out_specs = [piece(384), pre_spec]
         out_shape = [shape((4, SEQ, 384), bf16), shape((4, 2, 32, 128), f32)]
     else:
         in_specs = [col, piece(256)]
@@ -1130,26 +1141,25 @@
         pl.BlockSpec((8, SEQ), lambda j, *_: (0, 0)),
         col,
         col,
-        pl.BlockSpec((1, 8, SEQ), lambda j, *_: (j, 0, 0)),
+        pl.BlockSpec((TOGETHER, 8, SEQ), lambda j, *_: (j, 0, 0)),
     ]
     args = list(arrays) + [bounds, ctx, dctx, lse]
     scratch = [
-        pltpu.VMEM((128, SEQ), bf16),
-        pltpu.VMEM((SEQ, 128), f32),
-        pltpu.VMEM((SEQ, 128), f32),
-        pltpu.VMEM((128, QB), f32),
+        pltpu.VMEM((TOGETHER, SEQ, 128), f32),
+        pltpu.VMEM((TOGETHER, SEQ, 128), f32),
+        pltpu.VMEM((TOGETHER, QB, 128), f32),
     ]
     if has_prefix:
-        in_specs.append(pl.BlockSpec((1, 2, 32, 128), lambda j, *_: (j, 0, 0, 0)))
+        in_specs.append(pre_spec)
         args.append(pre)
-        scratch.append(pltpu.VMEM((2, 128, 128), f32))
+        scratch.append(pltpu.VMEM((TOGETHER, 2, 128, 128), f32))
     return pl.pallas_call(
         functools.partial(backward_kernel, has_prefix, 0 if has_prefix else 2),
         grid_spec=pltpu.PrefetchScalarGridSpec(
-            num_scalar_prefetch=1, grid=(4,), in_specs=in_specs, out_specs=out_specs, scratch_shapes=scratch
+            num_scalar_prefetch=1, grid=(4 // TOGETHER,), in_specs=in_specs, out_specs=out_specs, scratch_shapes=scratch
         ),
         out_shape=out_shape,
-        compiler_params=pltpu.CompilerParams(vmem_limit_bytes=40 * 2**20),
+        compiler_params=pltpu.CompilerParams(vmem_limit_bytes=60 * 2**20),
         cost_estimate=pl.CostEstimate(flops=10 * 8 * SEQ * SEQ * 64, bytes_accessed=10 * 2**20, transcendentals=8 * SEQ * SEQ),
         name="self_backward" if has_prefix else "cross_backward",
     )(bounds, *args)

time: 330 us -> 317 us (0.961)
  Pallas kernels: 300 us -> 279 us
  starting transfers between devices: 1.91 us -> 7.52 us
  local copies, waits for them, and re-layouts: 20 us -> 24.1 us
    pallas_call x2, Pallas kernels: 78 us -> 48.5 us  [backward_call(): pl.pallas_call(functools.partial(backward_kernel, has_prefix, 0 if has_pr...]
    pallas_call x1, Pallas kernels: 25.4 us -> 33.3 us  [last_call(): pl.pallas_call(functools.partial(last_kernel, planes), out_shape=[shape((...]
    ppermute x1, starting transfers between devices: 1.91 us -> 7.52 us  [swap_in(): return jnp.where(stays, value, lax.ppermute(value, AXES, crossing))]
    unnamed x61 -> x51, local copies, waits for them, and re-layouts: 19.4 us -> 23.5 us
  transfers between devices with their start and end apart: 1 -> 1, of which waited for: 0 -> 0; matrix products, arithmetic and copies ran while one was open for 0% -> 0% of each run, Pallas kernels for 18% -> 19%
where the time goes in v5:
time: 317 us; the launch traced here: 316 us
  Pallas kernels  279 us (88%)
  local copies, waits for them, and re-layouts  24.1 us (8%)
  starting transfers between devices  7.52 us (2%)
  other arithmetic  4.57 us (1%)
    pallas_call x1, Pallas kernels, forward_call(): pl.pallas_call(forward_kernel, out_shape=outs, in_specs=[anywhere] * 13 +...  135 us
    pallas_call x1, Pallas kernels, feed_call(): pl.pallas_call(feed_kernel, out_shape=[shape((rows, deep), bf16), shape((...  49.6 us
    pallas_call x2, Pallas kernels, backward_call(): pl.pallas_call(functools.partial(backward_kernel, has_prefix, 0 if has_pr...  48.5 us
    pallas_call x1, Pallas kernels, last_call(): pl.pallas_call(functools.partial(last_kernel, planes), out_shape=[shape((...  33.3 us
    unnamed x51, local copies, waits for them, and re-layouts  23.5 us
    pallas_call x1, Pallas kernels, query_call(): pl.pallas_call(query_kernel, out_shape=[shape((half, deep), f32), shape((...  12.7 us
    ppermute x1, starting transfers between devices, swap_in(): return jnp.where(stays, value, lax.ppermute(value, AXES, crossing))  7.52 us
  transfers between devices with their start and end apart: 1, of which 0 were waited for; matrix products, arithmetic and copies ran while one was open for 0% of the time, Pallas kernels for 19%

profile of v5, /device:TPU:1, one launch (start us, length us, event | category | flops | bytes accessed | tf_op | source)
XLA Modules:
  0.0 316.0 jit_solution(6746355581565541679)
XLA Ops:
  0.6 1.1 copy.24
  2.5 1.8 pad_maximum_fusion.ad
  4.9 135.0 %layer_forward.1 = (bf16[4,1024,384]{2,1,0:T(8,128)(2,1)}, bf16[4,1024,384]{2,1,0:T(8,128)(2,1)}, bf16[1024,512]{1,0:T(8,128)(2,1)}, f32[4,8,1024]{2,1,0:T(8,128...) custom-call(bf16[512,1024]{1,0:T(8,128)(2,1)} %tokens.1, ...), custom_call_target="tpu_custom_call" | custom-call | tf_op jit(solution)/shard_map/layer_forward/pallas_call | solution.py:1013
  139.9 49.6 %feed_forward.1 = (bf16[512,1024]{1,0:T(8,128)(2,1)}, f32[512,1024]{1,0:T(8,128)}, f32[64,2048]{1,0:T(8,128)}, bf16[1024,512]{1,0:T(8,128)(2,1)}) custom-call(f32[512,1024]{1,0:T(8,128)} %get-tuple-element.43.resid2, bf16[512,1024]{1,0:T(8,128)(2,1)} %cotangent.1, f32[3,1024]{1,0:T(4,128)} %gain.5, f32[3,1024]{1,0:T(4,128)} %bias.3, ...), custom_call_target="tpu_custom_call" | custom-call | tf_op jit(solution)/shard_map/feed_forward/pallas_call | solution.py:1338
  189.5 21.6 %cross_backward.1 = (bf16[1024,512]{1,0:T(8,128)(2,1)}, bf16[4,1024,256]{2,1,0:T(8,128)(2,1)}) custom-call(s32[8,1024]{1,0:T(8,128)} %get-tuple-element.50.bounds_s.refs_2_.refs_1_, bf16[1024,512]{1,0:T(8,128)(2,1)} %get-tuple-element.53.refs_0_, bf16[4,1024,256]{2,1,0:T(8,128)(2,1)} %get-tuple-element.54.refs_1_, ...), custom_call_target="tpu_custom_call" | custom-call | flops 5368709120 | bytes 10485760 | tf_op jit(solution)/shard_map/cross_backward/pallas_call | solution.py:1156
  211.1 1.6 copy-done.7
  212.7 1.2 copy-done.9
  213.9 1.2 copy-done.10
  215.1 1.2 copy-done.11
  216.4 1.2 copy-done.12
  217.6 12.7 %query_backward.1 = (f32[512,1024]{1,0:T(8,128)S(1)}, bf16[1024,512]{1,0:T(8,128)(2,1)S(1)}, bf16[512,1024]{1,0:T(8,128)(2,1)}) custom-call(bf16[1024,512]{1,0:T(8,128)(2,1)S(1)} %copy-done.12, bf16[4,1024,256]{2,1,0:T(8,128)(2,1)S(1)} %copy-done.7, bf16[4,1024,256]{2,1,0:T(8,128)(2,1)S(1)} %copy-done.6, bf16[1024,512]{1,0:T(8,128)(2,1)S(1)} %copy-done.10, ...), custom_call_target="tpu_custom_call" | custom-call | tf_op jit(solution)/shard_map/query_backward/pallas_call | solution.py:1445
  230.3 1.3 copy-done.2
  231.6 1.0 copy-done.20
  232.6 7.5 %collective-permute-start = (bf16[512,1024]{1,0:T(8,128)(2,1)}, bf16[512,1024]{1,0:T(8,128)(2,1)}, u32[]{:S(2)}, u32[]{:S(2)}) collective-permute-start(bf16[512,1024]{1,0:T(8,128)(2,1)} %get-tuple-element.76), channel_id=1, source_target_pairs={{1,4},{3,6},{4,1},{6,3},{9,12},{11,14},{12,9},{14,11},{17,20},{19,... | collective-permute-start | bytes 3145736 | tf_op jit(solution)/shard_map/ppermute | solution.py:1632
  240.1 26.9 %self_backward.1 = (bf16[4,1024,384]{2,1,0:T(8,128)(2,1)}, f32[4,2,32,128]{3,2,1,0:T(8,128)}) custom-call(s32[8,1024]{1,0:T(8,128)} %get-tuple-element.50.bounds_s.refs_2_.refs_1_, bf16[4,1024,384]{2,1,0:T(8,128)(2,1)} %get-tuple-element.51.refs_0_, s32[8,1024]{1,0:T(8,128)} %get-tuple-element.50.bounds_s.refs_2_.refs_1_, ...), custom_call_target="tpu_custom_call" | custom-call | flops 5368709120 | bytes 10485760 | tf_op jit(solution)/shard_map/self_backward/pallas_call | solution.py:1156
  267.1 1.9 copy-done.1
  268.9 1.6 copy-done.3
  270.5 0.9 copy-done.19
  271.4 33.3 %last_sums.1 = (f32[512,1024]{1,0:T(8,128)S(1)}, f32[2,32,256]{2,1,0:T(8,128)S(1)}, f32[1024,128]{1,0:T(8,128)S(1)}, f32[128,1024]{1,0:T(8,128)S(1)}) custom-call(bf16[4,1024,384]{2,1,0:T(8,128)(2,1)S(1)} %copy-done.1, bf16[4,1024,384]{2,1,0:T(8,128)(2,1)S(1)} %copy-done, f32[512,1024]{1,0:T(8,128)S(1)} %copy-done.3, f32[4,2,32,128]{3,2,1,0:T(8,128)S(1)} %copy-done.19, ...), custom_call_target="tpu_custom_call" | custom-call | tf_op jit(solution)/shard_map/last_sums/pallas_call | solution.py:1574
  304.7 1.3 copy-done.4
  308.3 2.8 select_convert_fusion
  311.1 1.0 copy.30
  312.1 1.0 copy-done.5
  313.1 1.3 copy.31
  (38 shorter events, 5.3 us)
Async XLA Ops:
  189.4 21.6 %copy-start.6 = (bf16[4,1024,256]{2,1,0:T(8,128)(2,1)S(1)}, bf16[4,1024,256]{2,1,0:T(8,128)(2,1)}, u32[]{:S(2)}) copy-start(bf16[4,1024,256]{2,1,0:T(8,128)(2,1)} %get-tuple-element.60.wkv) | copy-start | bytes 6291460
  189.4 21.6 %copy-start.8 = (bf16[512,1024]{1,0:T(8,128)(2,1)S(1)}, bf16[512,1024]{1,0:T(8,128)(2,1)}, u32[]{:S(2)}) copy-start(bf16[512,1024]{1,0:T(8,128)(2,1)} %get-tuple-element.65.wso_m) | copy-start | bytes 3145732
  189.4 21.6 %copy-start.18 = (f32[3,1024]{1,0:T(4,128)S(1)}, f32[3,1024]{1,0:T(4,128)}, u32[]{:S(2)}) copy-start(f32[3,1024]{1,0:T(4,128)} %gain.5) | copy-start | bytes 36868
  211.1 1.6 copy-start.7
  212.7 1.2 copy-start.9
  213.9 1.2 copy-start.10
  215.1 1.2 copy-start.11
  216.4 1.2 copy-start.12
  230.3 1.3 copy-start.2
  231.6 1.0 copy-start.20
  232.6 75.8 %collective-permute-start = (bf16[512,1024]{1,0:T(8,128)(2,1)}, bf16[512,1024]{1,0:T(8,128)(2,1)}, u32[]{:S(2)}, u32[]{:S(2)}) collective-permute-start(bf16[512,1024]{1,0:T(8,128)(2,1)} %get-tuple-element.76), channel_id=1, source_target_pairs={{1,4},{3,6},{4,1},{6,3},{9,12},{11,14},{12,9},{14,11},{17,20},{19,... | collective-permute-start | bytes 3145736 | tf_op jit(solution)/shard_map/ppermute | solution.py:1632
  240.1 27.0 %copy-start = (bf16[4,1024,384]{2,1,0:T(8,128)(2,1)S(1)}, bf16[4,1024,384]{2,1,0:T(8,128)(2,1)}, u32[]{:S(2)}) copy-start(bf16[4,1024,384]{2,1,0:T(8,128)(2,1)} %get-tuple-element.71.wself) | copy-start | bytes 9437188
  240.1 27.0 %copy-start.13 = (f32[64,2048]{1,0:T(8,128)S(1)}, f32[64,2048]{1,0:T(8,128)}, u32[]{:S(2)}) copy-start(f32[64,2048]{1,0:T(8,128)} %get-tuple-element.74.unit_sum) | copy-start | bytes 1572868
  267.1 1.9 copy-start.1
  268.9 1.6 copy-start.3
  270.5 0.9 copy-start.19
  304.7 1.3 copy-start.4
  306.0 0.8 copy-start.14
  306.8 0.8 copy-start.16
  308.3 2.8 copy-start.21
  311.1 2.0 copy-start.5
  313.1 1.4 copy-start.17
  313.1 2.2 copy-start.15

commit v6 on v5

--- a/solution.py
+++ b/solution.py
@@ -541,11 +541,11 @@
 
 
 def forward_kernel(
-    tokens, memory, seg, mseg, prefix, w_self, w_so, w_cq, w_ckv, w_co, fc_in, fc_out, ad, gain, bias,
+    tokens, memory, seg, mseg, prefix, w_self, w_so, w_cq, w_ckv, w_co, fc_in, fc_out, ad_down, ad_up, gain, bias,
     o_wself, o_qkv, o_sctx, o_slse, o_pre, o_wso_m, o_wso_o, o_wkv, o_wq_m, o_wq_o, o_wco_m, o_wco_o,
-    o_q, o_kv, o_cctx, o_clse, o_resid1, o_resid2, o_bounds, fin, fout, fad,
+    o_q, o_kv, o_cctx, o_clse, o_resid1, o_resid2, o_bounds, o_ad, fin, fout, fad,
     wself, qkv, sctx, slse, pre, wso_m, wso_o, wkv, wq_m, wq_o, wco_m, wco_o,
-    q_all, kv, cctx, clse, resid1, resid2, bounds, tok, mem, sctx_o, cctx_o, q_send, hidden, low_one, vt, seg_v, mseg_v,
+    q_all, kv, cctx, clse, resid1, resid2, bounds, ad, tok, mem, sctx_o, cctx_o, q_send, hidden, low_one, vt, seg_v, mseg_v,
     send, recv, local,
 ):
     place_of = Place()
@@ -864,6 +864,12 @@
         lax.fori_loop(0, len(segments), body, 0)
         pending.extend(sends)
 
+    ad_copy = here(ad_up, ad.at[1])
+    ad_copy.start()
+    ad[0] = ad_down[...].astype(jnp.float32).T.astype(jnp.bfloat16)
+    ad_copy.wait()
+    keep(ad, o_ad)
+
     for copy in own_a[:3]:
         copy.start()
     own_a[3].start()
@@ -961,12 +967,13 @@
     resid1: jax.Array
     resid2: jax.Array
     bounds: jax.Array
+    ad: jax.Array
     fin: jax.Array
     fout: jax.Array
     fad: jax.Array
 
 
-def forward_call(tokens, memory, seg, mseg, prefix, w_self, w_so, w_cq, w_ckv, w_co, fc_in, fc_out, ad, gain, bias):
+def forward_call(tokens, memory, seg, mseg, prefix, w_self, w_so, w_cq, w_ckv, w_co, fc_in, fc_out, ad_down, ad_up, gain, bias):
     bf16, f32 = jnp.bfloat16, jnp.float32
     half, deep = tokens.shape
     shape = jax.ShapeDtypeStruct
@@ -990,9 +997,10 @@
         resid1=((half, deep), f32),
         resid2=((half, deep), f32),
         bounds=((8, SEQ), jnp.int32),
+        ad=((2,) + ad_up.shape, bf16),
     )
     outs = [shape(*value) for value in held.values()]
-    outs += [shape((3,) + fc_in.shape, bf16), shape((3,) + fc_out.shape, bf16), shape((3,) + ad.shape, bf16)]
+    outs += [shape((3,) + fc_in.shape, bf16), shape((3,) + fc_out.shape, bf16), shape((3, 2) + ad_up.shape, bf16)]
     scratch = [pltpu.VMEM(*value) for value in held.values()] + [
         pltpu.VMEM((SEQ, deep), bf16),
         pltpu.VMEM((MLEN, deep), bf16),
@@ -1013,14 +1021,14 @@
     results = pl.pallas_call(
         forward_kernel,
         out_shape=outs,
-        in_specs=[anywhere] * 13 + [vmem] * 2,
+        in_specs=[anywhere] * 12 + [vmem, anywhere] + [vmem] * 2,
         out_specs=[anywhere] * len(outs),
         scratch_shapes=scratch,
         compiler_params=pltpu.CompilerParams(
             collective_id=0, has_side_effects=True, vmem_limit_bytes=58 * 2**20
         ),
         name="layer_forward",
-    )(tokens, memory, seg, mseg, prefix, w_self, w_so, w_cq, w_ckv, w_co, fc_in, fc_out, ad, gain, bias)
+    )(tokens, memory, seg, mseg, prefix, w_self, w_so, w_cq, w_ckv, w_co, fc_in, fc_out, ad_down, ad_up, gain, bias)
     return Held(*results)
 
 
@@ -1187,16 +1195,21 @@
 
 
 def feed_kernel(
-    resid2, cotangent, gain, bias, wco_m, wco_o, fc_in, fin, fc_out, fout, ad, fad,
+    resid2, cotangent, gain, bias, wco_m_in, wco_o_in, fc_in, fin, fc_out, fout, ad, fad,
     out, grad_two, unit_sum, dctx,
     win, wout, down, up, slope, low, hidden, acc, gate, ada, branch_low, sem,
-    cot, out_v, units, unit_send, unit_recv, near_send, near_recv, dctx_s, send, recv, local,
+    cot, out_v, units, unit_send, unit_recv, near_send, near_recv, dctx_s, wco_m, wco_o, send, recv, local,
 ):
     place = Place()
     place.greet((place.to_x, place.to_y, place.to_d, place.to_c), True)
     c = place.c
     cot_start, cot_wait = swap_halves(place, cotangent, cot, cot, send.at[0], recv.at[0], local.at[0])
-    out_start, out_wait = swap_halves(place, out_v, out, out, send.at[1], recv.at[1], local.at[1])
+    out_copy = pltpu.make_async_copy(out_v, out, local.at[1])
+    two_copy = pltpu.make_async_copy(acc, grad_two, local.at[2])
+    co_copies = [
+        pltpu.make_async_copy(wco_m_in, wco_m, local.at[3]),
+        pltpu.make_async_copy(wco_o_in, wco_o, local.at[4]),
+    ]
     cot_start()
 
     def there(slot, src, dst, device):
@@ -1228,7 +1241,7 @@
         for i, dst in enumerate((down, up)):
             src = ad.at[i] if piece == 0 else fad.at[piece - 1, i]
             ad_loads.append(pltpu.make_async_copy(src, dst.at[pl.ds(group * piece, group)], sem.at[2, 2 * piece + i]))
-    for copy in loads + ad_loads:
+    for copy in ad_loads + loads + co_copies:
         copy.start()
 
     rows_all = resid2.shape[0]
@@ -1279,7 +1292,7 @@
 
     cot_wait()
     lax.fori_loop(0, tiles, middle, 0)
-    out_start()
+    out_copy.start()
     grelu = (adapter_scale * nt(branch_low[...], up[...]) * gate[...]).astype(bf16)
     features = low.shape[1]
     some = group // 2
@@ -1307,14 +1320,17 @@
     def finish(t, _):
         rows = at(t)
         grad = norm_backward(resid2[rows, :], gain[1:2, :], acc[rows, :])
-        grad_two[rows, :] = grad
+        acc[rows, :] = grad
         small = grad.astype(bf16)
         low[rows, :] = small
         dctx_s[rows, :] = nt(small, wco_o[...]).astype(bf16)
         return 0
 
+    for copy in co_copies:
+        copy.wait()
     lax.fori_loop(0, tiles, finish, 0)
     dctx_core.start()
+    two_copy.start()
     dctx[mine, :] = nt(low[...], wco_m[...]).astype(bf16)
     for copy in unit_near:
         copy.wait()
@@ -1322,7 +1338,8 @@
     for i in range(3):
         total = total + near_recv[i].astype(jnp.float32)
     unit_sum[...] = total
-    out_wait()
+    out_copy.wait()
+    two_copy.wait()
     dctx_core.wait()
 
 
@@ -1343,8 +1360,8 @@
             shape((some, 2 * deep), f32),
             shape((2 * rows, 512), bf16),
         ],
-        in_specs=[vmem, anywhere] + [vmem] * 4 + [anywhere] * 6,
-        out_specs=[anywhere] + [vmem] * 3,
+        in_specs=[vmem, anywhere] + [vmem] * 2 + [anywhere] * 8,
+        out_specs=[anywhere] * 2 + [vmem] * 2,
         scratch_shapes=[
             pltpu.VMEM((steps, deep, HIDDEN), bf16),
             pltpu.VMEM((steps, HIDDEN, deep), bf16),
@@ -1366,9 +1383,11 @@
             pltpu.VMEM((3, some, 2 * deep), bf16),
             pltpu.VMEM((3, some, 2 * deep), bf16),
             pltpu.VMEM((rows, 512), bf16),
+            pltpu.VMEM(wco_m.shape, bf16),
+            pltpu.VMEM(wco_o.shape, bf16),
             pltpu.SemaphoreType.DMA((7,)),
             pltpu.SemaphoreType.DMA((7,)),
-            pltpu.SemaphoreType.DMA((2,)),
+            pltpu.SemaphoreType.DMA((5,)),
         ],
         compiler_params=pltpu.CompilerParams(
             collective_id=1, has_side_effects=True, vmem_limit_bytes=61 * 2**20
@@ -1378,13 +1397,13 @@
 
 
 def query_kernel(
-    dq, dkv, wkv, wq_m, wq_o, grad_two, resid1, wso_m, wso_o, gain,
-    grad_one, dctx, mem_sum,
-    dq_o, mem_s, mem_r, dctx_s, low, send, recv,
+    dq_in, dkv_in, wkv_in, wq_m_in, wq_o_in, two_in, resid_in, wso_m_in, wso_o_in, gain,
+    one_out, dctx, mem_out,
+    dq, dkv, wkv, wq_m, wq_o, grad_two, resid1, wso_m, wso_o,
+    grad_one, mem_sum, dq_o, mem_s, mem_r, dctx_s, dctx_m, low, send, recv, local,
 ):
     bf16 = jnp.bfloat16
     place = Place()
-    place.greet((place.to_c,), False)
     c = place.c
     half = resid1.shape[0]
     mine = pl.ds(pl.multiple_of(c * half, half), half)
@@ -1395,7 +1414,19 @@
             src_ref=src, dst_ref=dst, send_sem=send.at[slot], recv_sem=recv.at[slot], device_id=place.to_c, device_id_type=MESH
         )
 
-    dq_core = there(0, dq.at[others], dq_o)
+    def here(slot, src, dst):
+        return pltpu.make_async_copy(src, dst, local.at[slot])
+
+    wkv_copy, dkv_far, dkv_near = here(0, wkv_in, wkv), here(1, dkv_in.at[:, others], dkv.at[:, others]), here(2, dkv_in.at[:, mine], dkv.at[:, mine])
+    pairs = (
+        (dq_in.at[mine], dq), (wq_m_in, wq_m), (wq_o_in, wq_o), (two_in, grad_two), (resid_in, resid1), (wso_o_in, wso_o), (wso_m_in, wso_m)
+    )
+    rest = [here(3 + i, src, dst) for i, (src, dst) in enumerate(pairs)]
+    for copy in [wkv_copy, dkv_far] + rest + [dkv_near]:
+        copy.start()
+    one_copy, mem_copy, dctx_copy = here(10, grad_one, one_out), here(11, mem_sum, mem_out), here(12, dctx_m, dctx.at[mine])
+    place.greet((place.to_c,), False)
+    dq_core = there(0, dq_in.at[others], dq_o)
     mem_core = there(1, mem_s, mem_r)
     dctx_core = there(2, dctx_s, dctx.at[mine])
     dq_core.start()
@@ -1410,13 +1441,17 @@
         mem_s[at(t), :] = memory_rows(place_at(1 - c, t)).astype(bf16)
         return 0
 
+    wkv_copy.wait()
+    dkv_far.wait()
     lax.fori_loop(0, tiles, far, 0)
     mem_core.start()
+    for copy in rest:
+        copy.wait()
     dq_core.wait()
 
     def one(t, _):
         rows = at(t)
-        grad_in = grad_two[rows, :] + nt(dq[place_at(c, t), :], wq_m[...]) + nt(dq_o[rows, :], wq_o[...])
+        grad_in = grad_two[rows, :] + nt(dq[rows, :], wq_m[...]) + nt(dq_o[rows, :], wq_o[...])
         grad = norm_backward(resid1[rows, :], gain[0:1, :], grad_in)
         grad_one[rows, :] = grad
         small = grad.astype(bf16)
@@ -1426,15 +1461,20 @@
 
     lax.fori_loop(0, tiles, one, 0)
     dctx_core.start()
-    dctx[mine, :] = nt(low[...], wso_m[...]).astype(bf16)
+    one_copy.start()
+    dctx_m[...] = nt(low[...], wso_m[...]).astype(bf16)
+    dctx_copy.start()
     mem_core.wait()
+    dkv_near.wait()
 
     def near(t, _):
         mem_sum[at(t), :] = (memory_rows(place_at(c, t)) + mem_r[at(t), :].astype(jnp.float32)).astype(bf16)
         return 0
 
     lax.fori_loop(0, tiles, near, 0)
-    dctx_core.wait()
+    mem_copy.start()
+    for copy in (dctx_core, one_copy, dctx_copy, mem_copy):
+        copy.wait()
 
 
 def query_call(dq, dkv, wkv, wq_m, wq_o, grad_two, resid1, wso_m, wso_o, gain):
@@ -1442,29 +1482,36 @@
     half, deep = resid1.shape
     shape = jax.ShapeDtypeStruct
     vmem = pl.BlockSpec(memory_space=pltpu.VMEM)
+    anywhere = pl.BlockSpec(memory_space=pl.ANY)
     return pl.pallas_call(
         query_kernel,
         out_shape=[shape((half, deep), f32), shape((2 * half, 512), bf16), shape((half, deep), bf16)],
-        in_specs=[vmem] * 10,
-        out_specs=[vmem] * 3,
-        scratch_shapes=[
+        in_specs=[anywhere] * 9 + [vmem],
+        out_specs=[anywhere] * 3,
+        scratch_shapes=[pltpu.VMEM((half, 512), bf16)]
+        + [pltpu.VMEM(value.shape, value.dtype) for value in (dkv, wkv, wq_m, wq_o, grad_two, resid1, wso_m, wso_o)]
+        + [
+            pltpu.VMEM((half, deep), f32),
+            pltpu.VMEM((half, deep), bf16),
             pltpu.VMEM((half, 512), bf16),
             pltpu.VMEM((half, deep), bf16),
             pltpu.VMEM((half, deep), bf16),
             pltpu.VMEM((half, 512), bf16),
+            pltpu.VMEM((half, 512), bf16),
             pltpu.VMEM((half, deep), bf16),
             pltpu.SemaphoreType.DMA((3,)),
             pltpu.SemaphoreType.DMA((3,)),
+            pltpu.SemaphoreType.DMA((13,)),
         ],
-        compiler_params=pltpu.CompilerParams(collective_id=2, has_side_effects=True, vmem_limit_bytes=40 * 2**20),
+        compiler_params=pltpu.CompilerParams(collective_id=2, has_side_effects=True, vmem_limit_bytes=60 * 2**20),
         name="query_backward",
     )(dq, dkv, wkv, wq_m, wq_o, grad_two, resid1, wso_m, wso_o, gain)
 
 
 def last_kernel(
-    planes, dqkv, wself, grad_one, blocks, unit_sum,
-    grad_input, prefix_grad, down_grad, up_grad,
-    part_s, part_r, out_s, out_r, pre_near, pre_sum, pre_z, pre_c, unit_s, unit_z, unit_all, total, send, recv,
+    planes, dqkv_in, wself_in, one_in, blocks_in, unit_in,
+    input_out, prefix_grad, down_grad, up_grad,
+    dqkv, wself, grad_one, blocks, unit_sum, part_s, part_r, out_s, pre_near, pre_sum, pre_z, pre_c, unit_s, unit_z, unit_all, send, recv, local,
 ):
     bf16, f32 = jnp.bfloat16, jnp.float32
     place = Place()
@@ -1475,8 +1522,8 @@
         other = z + step - 2 * step * lax.rem(lax.div(z, step), 2)
         steps.append((2 * other + c, place.head))
         step *= 2
-    place.greet([place.to_x, place.to_y, place.to_d, place.to_c] + steps, True)
     moves = c != x
+    stays = c == x
     half = grad_one.shape[0]
     slots = []
 
@@ -1490,6 +1537,19 @@
     tiles = half // TILE
     at = lambda t: pl.ds(t * TILE, TILE)
     place_at = lambda first, t: pl.ds(pl.multiple_of(first * half + t * TILE, TILE), TILE)
+
+    def here(slot, src, dst):
+        return pltpu.make_async_copy(src, dst, local.at[slot])
+
+    loads = [here(0, wself_in, wself), here(1, blocks_in, blocks), here(2, unit_in, unit_sum), here(3, one_in, grad_one)]
+    far_loads = [here(4 + t, dqkv_in.at[:, place_at(1 - c, t)], dqkv.at[:, place_at(1 - c, t)]) for t in range(tiles)]
+    near_loads = [
+        here(4 + tiles + t, dqkv_in.at[:, place_at(c, t)], dqkv.at[:, place_at(c, t)]) for t in range(tiles)
+    ]
+    for copy in [loads[1], loads[2], far_loads[0], loads[0]] + far_loads[1:] + near_loads + [loads[3]]:
+        copy.start()
+
+    place.greet([place.to_x, place.to_y, place.to_d, place.to_c] + steps, True)
     pre_copies = [
         there(blocks.at[i + 1], pre_near.at[i], device) for i, device in enumerate((place.to_x, place.to_y, place.to_d))
     ]
@@ -1498,15 +1558,20 @@
     unit_steps = [there(unit_s.at[i], unit_z.at[i], device) for i, device in enumerate(steps)]
     unit_core = there(unit_s.at[len(steps)], unit_z.at[len(steps)], place.to_c)
     part_copies = [there(part_s.at[at(t)], part_r.at[at(t)], place.to_c) for t in range(tiles)]
-    out_copies = [there(out_s.at[at(t)], out_r.at[at(t)], place.to_s) for t in range(tiles)]
+    out_copies = [there(out_s.at[at(t)], input_out.at[at(t)], place.to_s) for t in range(tiles)]
+    own_copies = [here(4 + 2 * tiles + t, out_s.at[at(t)], input_out.at[at(t)]) for t in range(tiles)]
+    loads[1].wait()
     for copy in pre_copies:
         copy.start()
+    loads[2].wait()
     unit_s[0] = unit_sum[...].astype(bf16)
     unit_steps[0].start()
 
     def input_rows(rows):
         return sum(nt(dqkv[p, rows, :], wself[p]) for p in range(4))
 
+    loads[0].wait()
+    far_loads[0].wait()
     part_s[at(0), :] = input_rows(place_at(1 - c, 0)).astype(bf16)
     part_copies[0].start()
     for copy in pre_copies:
@@ -1514,6 +1579,7 @@
     pre_sum[0] = blocks[0] + pre_near[0] + pre_near[1] + pre_near[2]
     pre_steps[0].start()
     for t in range(1, tiles):
+        far_loads[t].wait()
         part_s[at(t), :] = input_rows(place_at(1 - c, t)).astype(bf16)
         part_copies[t].start()
 
@@ -1531,11 +1597,14 @@
         else:
             unit_core.start()
 
+    loads[3].wait()
     for t in range(tiles):
+        near_loads[t].wait()
         part_copies[t].wait()
-        total[at(t), :] = input_rows(place_at(c, t)) + part_r[at(t), :].astype(f32) + grad_one[at(t), :]
-        out_s[at(t), :] = total[at(t), :].astype(bf16)
+        total = input_rows(place_at(c, t)) + part_r[at(t), :].astype(f32) + grad_one[at(t), :]
+        out_s[at(t), :] = total.astype(bf16)
         pl.when(moves)(out_copies[t].start)
+        pl.when(stays)(own_copies[t].start)
         if t < len(steps):
             advance(t)
     for i in range(tiles, len(steps)):
@@ -1553,15 +1622,9 @@
     down_grad[...] = unit_all[:, 0:features].T
     up_grad[...] = unit_all[:, features : 2 * features]
 
-    @pl.when(moves)
-    def _():
-        for copy in out_copies:
-            copy.wait()
-        grad_input[...] = out_r[...].astype(f32)
-
-    @pl.when(jnp.logical_not(moves))
-    def _():
-        grad_input[...] = total[...]
+    for t in range(tiles):
+        pl.when(moves)(out_copies[t].wait)
+        pl.when(stays)(own_copies[t].wait)
 
 
 def last_call(planes, dqkv, wself, grad_one, blocks, unit_sum):
@@ -1571,18 +1634,19 @@
     count = planes.bit_length() - 1
     shape = jax.ShapeDtypeStruct
     vmem = pl.BlockSpec(memory_space=pltpu.VMEM)
+    anywhere = pl.BlockSpec(memory_space=pl.ANY)
     return pl.pallas_call(
         functools.partial(last_kernel, planes),
         out_shape=[
-            shape((half, deep), f32),
+            shape((half, deep), bf16),
             shape((2, 32, 256), f32),
             shape((deep, 2 * some), f32),
             shape((2 * some, deep), f32),
         ],
-        in_specs=[vmem] * 5,
-        out_specs=[vmem] * 4,
-        scratch_shapes=[
-            pltpu.VMEM((half, deep), bf16),
+        in_specs=[anywhere] * 5,
+        out_specs=[anywhere] + [vmem] * 3,
+        scratch_shapes=[pltpu.VMEM(value.shape, value.dtype) for value in (dqkv, wself, grad_one, blocks, unit_sum)]
+        + [
             pltpu.VMEM((half, deep), bf16),
             pltpu.VMEM((half, deep), bf16),
             pltpu.VMEM((half, deep), bf16),
@@ -1593,11 +1657,11 @@
             pltpu.VMEM((count + 1, some, 2 * deep), bf16),
             pltpu.VMEM((count + 1, some, 2 * deep), bf16),
             pltpu.VMEM((2 * some, 2 * deep), f32),
-            pltpu.VMEM((half, deep), f32),
             pltpu.SemaphoreType.DMA((3 + 2 * count + 2 + 2 * (half // TILE),)),
             pltpu.SemaphoreType.DMA((3 + 2 * count + 2 + 2 * (half // TILE),)),
+            pltpu.SemaphoreType.DMA((4 + 3 * (half // TILE),)),
         ],
-        compiler_params=pltpu.CompilerParams(collective_id=3, has_side_effects=True, vmem_limit_bytes=40 * 2**20),
+        compiler_params=pltpu.CompilerParams(collective_id=3, has_side_effects=True, vmem_limit_bytes=60 * 2**20),
         name="last_sums",
     )(dqkv, wself, grad_one, blocks, unit_sum)
 
@@ -1623,7 +1687,7 @@
     return found
 
 
-def swap_in(rows, value):
+def swapped_rows(rows, value):
     def swapped(z, c, y, x):
         return (z, x, y, c)
 
@@ -1653,7 +1717,6 @@
     ln_bias,
 ):
     count = prefix.shape[1]
-    ad = jnp.stack([ad_down.T, ad_up])
     held = forward_call(
         tokens,
         memory,
@@ -1667,28 +1730,30 @@
         w_cross_out,
         fc_in,
         fc_out,
-        ad,
+        ad_down,
+        ad_up,
         ln_gain,
         ln_bias,
     )
-    output, grad_two, unit_sum, cross_dctx = feed_call(
+    out_own, grad_two, unit_sum, cross_dctx = feed_call(
         held.resid2, cotangent, ln_gain, ln_bias, held.wco_m, held.wco_o,
-        fc_in, held.fin, fc_out, held.fout, ad, held.fad,
-    )
+        fc_in, held.fin, fc_out, held.fout, held.ad, held.fad,
+    )
+    output = swapped_rows(rows, out_own)
     cross_dq, cross_dkv = backward_call(
         False, (held.q, held.kv), held.bounds, held.cctx, cross_dctx, held.clse
     )
     grad_one, self_dctx, memory_sum = query_call(
         cross_dq, cross_dkv, held.wkv, held.wq_m, held.wq_o, grad_two, held.resid1, held.wso_m, held.wso_o, ln_gain
     )
-    grad_memory = swap_in(rows, memory_sum).astype(jnp.float32)
+    grad_memory = swapped_rows(rows, memory_sum).astype(jnp.float32)
     self_dqkv, prefix_blocks = backward_call(
         True, (held.qkv,), held.bounds, held.sctx, self_dctx, held.slse, held.pre
     )
     grad_input, prefix_grad, down_grad, up_grad = last_call(
         rows // 2, self_dqkv, held.wself, grad_one, prefix_blocks, unit_sum
     )
-    return (output, grad_input, grad_memory, prefix_grad[:, :count], down_grad, up_grad)
+    return (output, grad_input.astype(jnp.float32), grad_memory, prefix_grad[:, :count], down_grad, up_grad)
 
 
 def solution(mesh):

time: 317 us -> 293 us (0.924); the launches traced: 316 us -> 296 us
  local copies, waits for them, and re-layouts: 24.1 us -> 3.66 us
  Pallas kernels: 279 us -> 275 us
    unnamed x51 -> x14, local copies, waits for them, and re-layouts: 23.5 us -> 3.04 us
    pallas_call x1, Pallas kernels: 49.6 us -> 42 us  [feed_call(): pl.pallas_call(feed_kernel, out_shape=[shape((rows, deep), bf16), shape((...]
    pallas_call x2, Pallas kernels: 48.5 us -> 52.3 us  [backward_call(): pl.pallas_call(functools.partial(backward_kernel, has_prefix, 0 if has_pr...]
    ppermute x1 -> x2, starting transfers between devices: 7.52 us -> 8.98 us  [swapped_rows(): return jnp.where(stays, value, lax.ppermute(value, AXES, crossing))]
  transfers between devices with their start and end apart: 1 -> 2, of which waited for: 0 -> 0; matrix products, arithmetic and copies ran while one was open for 0% -> 2% of each run, Pallas kernels for 19% -> 20%
where the time goes in v6:
time: 293 us; the launch traced here: 296 us
  Pallas kernels  275 us (94%)
  starting transfers between devices  8.98 us (3%)
  other arithmetic  6.73 us (2%)
  local copies, waits for them, and re-layouts  3.66 us (1%)
    pallas_call x1, Pallas kernels, forward_call(): pl.pallas_call(forward_kernel, out_shape=outs, in_specs=[anywhere] * 12 +...  136 us
    pallas_call x2, Pallas kernels, backward_call(): pl.pallas_call(functools.partial(backward_kernel, has_prefix, 0 if has_pr...  52.3 us
    pallas_call x1, Pallas kernels, feed_call(): pl.pallas_call(feed_kernel, out_shape=[shape((rows, deep), bf16), shape((...  42 us
    pallas_call x1, Pallas kernels, last_call(): pl.pallas_call(functools.partial(last_kernel, planes), out_shape=[shape((...  33.5 us
    pallas_call x1, Pallas kernels, query_call(): pl.pallas_call(query_kernel, out_shape=[shape((half, deep), f32), shape((...  11.4 us
    ppermute x2, starting transfers between devices, swapped_rows(): return jnp.where(stays, value, lax.ppermute(value, AXES, crossing))  8.98 us
  transfers between devices with their start and end apart: 2, of which 0 were waited for; matrix products, arithmetic and copies ran while one was open for 2% of the time, Pallas kernels for 20%

profile of v6, /device:TPU:1, one launch (start us, length us, event | category | flops | bytes accessed | tf_op | source)
XLA Modules:
  0.0 295.5 jit_solution(14783301007671497599)
XLA Ops:
  0.6 0.8 copy.23
  1.4 0.6 pad.4.prefix
  2.0 136.1 %layer_forward.1 = (bf16[4,1024,384]{2,1,0:T(8,128)(2,1)}, bf16[4,1024,384]{2,1,0:T(8,128)(2,1)}, bf16[1024,512]{1,0:T(8,128)(2,1)}, f32[4,8,1024]{2,1,0:T(8,128...) custom-call(bf16[512,1024]{1,0:T(8,128)(2,1)} %tokens.1, ...), custom_call_target="tpu_custom_call" | custom-call | tf_op jit(solution)/shard_map/layer_forward/pallas_call | solution.py:1021
  138.2 42.0 %feed_forward.1 = (bf16[512,1024]{1,0:T(8,128)(2,1)}, f32[512,1024]{1,0:T(8,128)}, f32[64,2048]{1,0:T(8,128)}, bf16[1024,512]{1,0:T(8,128)(2,1)}) custom-call(f32[512,1024]{1,0:T(8,128)} %get-tuple-element.44.resid2, bf16[512,1024]{1,0:T(8,128)(2,1)} %cotangent.1, f32[3,1024]{1,0:T(4,128)} %gain.5, f32[3,1024]{1,0:T(4,128)} %bias.3, ...), custom_call_target="tpu_custom_call" | custom-call | tf_op jit(solution)/shard_map/feed_forward/pallas_call | solution.py:1355
  180.2 25.5 %cross_backward.1 = (bf16[1024,512]{1,0:T(8,128)(2,1)}, bf16[4,1024,256]{2,1,0:T(8,128)(2,1)}) custom-call(s32[8,1024]{1,0:T(8,128)} %get-tuple-element.52.bounds_s.refs_2_.refs_1_, bf16[1024,512]{1,0:T(8,128)(2,1)} %get-tuple-element.55.refs_0_, bf16[4,1024,256]{2,1,0:T(8,128)(2,1)} %get-tuple-element.56.refs_1_, ...), custom_call_target="tpu_custom_call" | custom-call | flops 5368709120 | bytes 10485760 | tf_op jit(solution)/shard_map/cross_backward/pallas_call | solution.py:1164
  205.8 11.4 %query_backward.1 = (f32[512,1024]{1,0:T(8,128)}, bf16[1024,512]{1,0:T(8,128)(2,1)}, bf16[512,1024]{1,0:T(8,128)(2,1)}) custom-call(bf16[1024,512]{1,0:T(8,128)(2,1)} %get-tuple-element.60.dq_in, bf16[4,1024,256]{2,1,0:T(8,128)(2,1)} %get-tuple-element.61.dkv_in, bf16[4,1024,256]{2,1,0:T(8,128)(2,1)} %get-tuple-element.62.wkv_in, ...), custom_call_target="tpu_custom_call" | custom-call | tf_op jit(solution)/shard_map/query_backward/pallas_call | solution.py:1486
  217.1 7.1 %collective-permute-start.1 = (bf16[512,1024]{1,0:T(8,128)(2,1)}, bf16[512,1024]{1,0:T(8,128)(2,1)S(1)}, u32[]{:S(2)}, u32[]{:S(2)}) collective-permute-start(bf16[512,1024]{1,0:T(8,128)(2,1)} %get-tuple-element.78), channel_id=1, source_target_pairs={{1,4},{3,6},{4,1},{6,3},{9,12},{11,14},{12,9},{14,11},{17,20},{19,... | collective-permute-start | bytes 3145736 | tf_op jit(solution)/shard_map/ppermute | solution.py:1696
  224.2 0.0 copy-done.1
  224.2 1.9 collective-permute-start
  226.2 26.8 %self_backward.1 = (bf16[4,1024,384]{2,1,0:T(8,128)(2,1)}, f32[4,2,32,128]{3,2,1,0:T(8,128)}) custom-call(s32[8,1024]{1,0:T(8,128)} %get-tuple-element.52.bounds_s.refs_2_.refs_1_, bf16[4,1024,384]{2,1,0:T(8,128)(2,1)} %get-tuple-element.53.refs_0_, s32[8,1024]{1,0:T(8,128)} %get-tuple-element.52.bounds_s.refs_2_.refs_1_, ...), custom_call_target="tpu_custom_call" | custom-call | flops 5368709120 | bytes 10485760 | tf_op jit(solution)/shard_map/self_backward/pallas_call | solution.py:1164
  253.0 33.5 %last_sums.1 = (bf16[512,1024]{1,0:T(8,128)(2,1)}, f32[2,32,256]{2,1,0:T(8,128)}, f32[1024,128]{1,0:T(8,128)}, f32[128,1024]{1,0:T(8,128)}) custom-call(bf16[4,1024,384]{2,1,0:T(8,128)(2,1)} %get-tuple-element.72.dqkv_in, bf16[4,1024,384]{2,1,0:T(8,128)(2,1)} %get-tuple-element.73.wself_in, f32[512,1024]{1,0:T(8,128)} %get-tuple-element.74.one_in, ...), custom_call_target="tpu_custom_call" | custom-call | tf_op jit(solution)/shard_map/last_sums/pallas_call | solution.py:1638
  286.5 0.0 copy-start.4
  286.5 0.0 copy-start
  286.5 2.9 convert_element_type.8
  289.4 0.0 copy-done.4
  289.4 0.7 copy.24
  290.0 0.0 collective-permute-done.1
  290.1 0.0 copy-done
  290.1 1.5 select_convert_fusion
  291.5 0.0 collective-permute-done
  291.5 2.4 broadcast_select_fusion
  293.9 0.8 copy.27
  294.7 0.0 copy-done.2
  294.7 0.8 copy.28
  (4 shorter events, 0.0 us)
Async XLA Ops:
  205.7 18.5 %copy-start.1 = (bf16[512,1024]{1,0:T(8,128)(2,1)S(1)}, bf16[512,1024]{1,0:T(8,128)(2,1)}, u32[]{:S(2)}) copy-start(bf16[512,1024]{1,0:T(8,128)(2,1)} %get-tuple-element.51) | copy-start | bytes 3145732
  217.1 72.9 %collective-permute-start.1 = (bf16[512,1024]{1,0:T(8,128)(2,1)}, bf16[512,1024]{1,0:T(8,128)(2,1)S(1)}, u32[]{:S(2)}, u32[]{:S(2)}) collective-permute-start(bf16[512,1024]{1,0:T(8,128)(2,1)} %get-tuple-element.78), channel_id=1, source_target_pairs={{1,4},{3,6},{4,1},{6,3},{9,12},{11,14},{12,9},{14,11},{17,20},{19,... | collective-permute-start | bytes 3145736 | tf_op jit(solution)/shard_map/ppermute | solution.py:1696
  224.2 67.3 %collective-permute-start = (bf16[512,1024]{1,0:T(8,128)(2,1)S(1)}, bf16[512,1024]{1,0:T(8,128)(2,1)}, u32[]{:S(2)}, u32[]{:S(2)}) collective-permute-start(bf16[512,1024]{1,0:T(8,128)(2,1)S(1)} %copy-done.1), channel_id=1, source_target_pairs={{1,4},{3,6},{4,1},{6,3},{9,12},{11,14},{12,9},{14,11},{17,20},{19,... | collective-permute-start | bytes 3145736 | tf_op jit(solution)/shard_map/ppermute | solution.py:1696
  286.5 2.9 copy-start.4
  286.5 3.6 %copy-start = (bf16[512,1024]{1,0:T(8,128)(2,1)S(1)}, bf16[512,1024]{1,0:T(8,128)(2,1)}, u32[]{:S(2)}) copy-start(bf16[512,1024]{1,0:T(8,128)(2,1)} %get-tuple-element.78) | copy-start | bytes 3145732
  291.5 2.4 copy-start.3
  291.5 3.2 %copy-start.2 = (f32[128,1024]{1,0:T(8,128)S(1)}, f32[128,1024]{1,0:T(8,128)}, u32[]{:S(2)}) copy-start(f32[128,1024]{1,0:T(8,128)} %get-tuple-element.99) | copy-start | bytes 1572868
